TPU v7x, 256 devices: a whole 4x4x8 slice. The times are simulated.
256 devices in a mesh: dp: 64 (over z, y, core), mp: 4 (over x).
Axes of the slice: x: 4, y: 4, z: 8, core: 2. Of those that a mesh axis runs over, the one named last changes fastest.
Arguments:
- tokens: bfloat16 [65536, 4096], P('dp', 'mp'), may hold values from -6 to 6
- cotangent: bfloat16 [65536, 4096], P('dp', 'mp'), may hold values from -6 to 6
- w_query: bfloat16 [4096, 2048], P('dp', 'mp'), may hold values from -6 to 6
- w_key: bfloat16 [4096, 2048], P('dp', 'mp'), may hold values from -6 to 6
- w_value: bfloat16 [4096, 2048], P('dp', 'mp'), may hold values from -0.09375 to 0.09375
- w_out: bfloat16 [2048, 4096], P('mp', 'dp'), may hold values from -0.125 to 0.125
- gain: float32 [4096], replicated, may hold values from 0.25 to 1.75
- w_router: float32 [4096], replicated, may hold values from -0.09375 to 0.09375
- chosen: int32 [8192], P('dp'), may hold values from 0 to 1023, as said below
- counts: int32 [64], P('dp'), may hold values from 32 to 128, as said below
- doc_start: int32 [65536], P('dp'), may hold values from 0 to 1023, as said below
Outputs:
- block_out: bfloat16 [65536, 4096], P('dp', 'mp')
- token_grad: bfloat16 [65536, 4096], P('dp', 'mp')
- muon_step: float32 [2048, 4096], P('mp', 'dp')
Inputs may be any that keep to these rules, and one draw needn't show every extreme that they name: `chosen`: within each sequence the list's entries are distinct; the first counts entries are the live rows in increasing order. Every list contains rows 0 and 1023. `counts`: some sequence has all 128 slots live, and some other sequence has exactly 32. Along a sequence doc_start never decreases from one token to the next and never exceeds the token's own position; no document crosses a sequence boundary: the first token of each sequence starts a document, and so does the last.
All inputs are finite; a program needn't handle non-finite values.
Results may differ from a plain program's by a relative error of at most 0.008.
Values may be sent and summed in bfloat16 or wider, within the bound.
No kernel may reach another device: no remote copies, remote signals or barrier semaphores. Data moves between devices by JAX's collectives and lax.ppermute only.
A program may use at most 128 MiB of HBM per device.

v0:
```python
import math

import jax
import jax.numpy as jnp
from jax import lax
from jax.sharding import PartitionSpec as P

D = 4096
HD = 128
NS_STEPS = 2


EPS = 1e-06
COEF_A = 3.4445
COEF_B = -4.775
COEF_C = 2.0315


def attend(rows_in, gain, w_query, w_key, w_value, doc_ids, positions, live_mask):
    rows_wide = rows_in.astype(jnp.float32)
    inv_scale = lax.rsqrt(jnp.mean(rows_wide * rows_wide, axis=1, keepdims=True) + EPS)
    unit_rows = rows_wide * inv_scale
    normed = (unit_rows * gain).astype(jnp.bfloat16)
    length = rows_in.shape[0]
    heads_here = w_query.shape[1] // HD

    def project(weight):
        return (
            jnp.dot(normed, weight, preferred_element_type=jnp.float32)
            .astype(jnp.bfloat16)
            .reshape(length, heads_here, HD)
        )

    query = project(w_query)
    key_rows = project(w_key)
    values = project(w_value)
    scores = jnp.einsum(
        "qhd,khd->hqk", query, key_rows, preferred_element_type=jnp.float32
    ) * HD ** (-0.5)
    allowed = (
        (positions[None, :] <= positions[:, None])
        & (doc_ids[None, :] == doc_ids[:, None])
        & live_mask[None, :]
    )
    allowed = allowed | jnp.eye(length, dtype=bool)
    scores = jnp.where(allowed[None], scores, -1e30)
    peak = jnp.max(scores, axis=2, keepdims=True)
    expo = jnp.exp(scores - peak)
    probs = expo / jnp.sum(expo, axis=2, keepdims=True)
    probs_low = probs.astype(jnp.bfloat16)
    attn = jnp.einsum("hqk,khd->qhd", probs_low, values, preferred_element_type=jnp.float32).astype(
        jnp.bfloat16
    )
    return (
        attn.reshape(length, -1),
        (unit_rows, inv_scale, query, key_rows, values, probs, probs_low),
    )


def transposed_dot(left, right):
    return lax.dot_general(
        left, right, (((1,), (1,)), ((), ())), preferred_element_type=jnp.float32
    )


def attend_back(d_attn, saved, w_query, w_key, w_value):
    unit_rows, inv_scale, query, key_rows, values, probs, probs_low = saved
    length = d_attn.shape[0]
    d_heads = d_attn.reshape(length, -1, HD)
    d_probs = jnp.einsum("qhd,khd->hqk", d_heads, values, preferred_element_type=jnp.float32)
    d_scores = (
        probs * (d_probs - jnp.sum(d_probs * probs, axis=2, keepdims=True)) * HD ** (-0.5)
    ).astype(jnp.bfloat16)
    d_query = (
        jnp.einsum("hqk,khd->qhd", d_scores, key_rows, preferred_element_type=jnp.float32)
        .astype(jnp.bfloat16)
        .reshape(length, -1)
    )
    d_keys = (
        jnp.einsum("hqk,qhd->khd", d_scores, query, preferred_element_type=jnp.float32)
        .astype(jnp.bfloat16)
        .reshape(length, -1)
    )
    d_values = (
        jnp.einsum("hqk,qhd->khd", probs_low, d_heads, preferred_element_type=jnp.float32)
        .astype(jnp.bfloat16)
        .reshape(length, -1)
    )
    total = transposed_dot(d_query, w_query)
    total = total + transposed_dot(d_keys, w_key)
    return total + transposed_dot(d_values, w_value)


def column_dot(left, right):
    return lax.dot_general(
        left, right, (((0,), (0,)), ((), ())), preferred_element_type=jnp.float32
    )


def gram_of(ortho):
    local_gram = jnp.einsum("dhi,dhj->hij", ortho, ortho, precision=lax.Precision.HIGHEST)
    return lax.psum(local_gram, "dp")


def per_device(
    tokens, cotangent, w_query, w_key, w_value, w_out, gain, w_router, chosen, counts, doc_start
):
    slots = chosen.shape[0]
    live_mask = jnp.arange(slots) < counts[0]
    doc_ids = doc_start[chosen]
    rows_part = tokens[chosen]
    grad_part = cotangent[chosen]
    rows_in, grad_in = (
        lax.all_gather(rows_part, "mp", axis=1, tiled=True),
        lax.all_gather(grad_part, "mp", axis=1, tiled=True),
    )
    full_query, full_key, full_value, full_out = (
        lax.all_gather(w_query, "dp", axis=0, tiled=True),
        lax.all_gather(w_key, "dp", axis=0, tiled=True),
        lax.all_gather(w_value, "dp", axis=0, tiled=True),
        lax.all_gather(w_out, "dp", axis=1, tiled=True),
    )
    feat_local = rows_part.shape[1]
    feat_start = lax.axis_index("mp") * feat_local
    attn, saved = attend(
        rows_in, gain, full_query, full_key, full_value, doc_ids, chosen, live_mask
    )
    partial_mixed = jnp.dot(attn, full_out, preferred_element_type=jnp.float32)
    mixed_part = lax.psum_scatter(
        partial_mixed.astype(jnp.bfloat16), "mp", scatter_dimension=1, tiled=True
    ).astype(jnp.float32)
    rows_wide = rows_in.astype(jnp.float32)
    gate_prob = jax.nn.sigmoid(jnp.sum(rows_wide * w_router, axis=1))
    rows_part_wide = rows_part.astype(jnp.float32)
    updated = (rows_part_wide + gate_prob[:, None] * mixed_part).astype(jnp.bfloat16)
    block_out = tokens.at[chosen].set(jnp.where(live_mask[:, None], updated, rows_part))
    grad_wide = grad_in.astype(jnp.float32)
    grad_part_wide = grad_part.astype(jnp.float32)
    d_mix = (jnp.where(live_mask, gate_prob, 0.0)[:, None] * grad_wide).astype(jnp.bfloat16)
    d_gate = lax.psum(jnp.sum(grad_part_wide * mixed_part, axis=1), "mp")
    d_logit = d_gate * gate_prob * (1.0 - gate_prob)
    d_attn = transposed_dot(d_mix, full_out).astype(jnp.bfloat16)
    d_normed_part = attend_back(d_attn, saved, full_query, full_key, full_value)
    unit_rows, inv_scale = (saved[0], saved[1])
    gain_local = lax.dynamic_slice_in_dim(gain, feat_start, feat_local)
    router_local = lax.dynamic_slice_in_dim(w_router, feat_start, feat_local)
    unit_local = lax.dynamic_slice_in_dim(unit_rows, feat_start, feat_local, 1)
    d_normed_local = lax.psum_scatter(
        d_normed_part.astype(jnp.bfloat16), "mp", scatter_dimension=1, tiled=True
    ).astype(jnp.float32)
    scaled_local = d_normed_local * gain_local
    stat = lax.psum(jnp.sum(scaled_local * unit_local, axis=1), "mp")[:, None] / D
    d_rows = (
        grad_part_wide
        + inv_scale * (scaled_local - unit_local * stat)
        + d_logit[:, None] * router_local
    )
    token_grad = cotangent.at[chosen].set(
        jnp.where(live_mask[:, None], d_rows.astype(jnp.bfloat16), grad_part)
    )
    rows_dp = d_mix.shape[1] // lax.axis_size("dp")
    grad_t = lax.psum_scatter(column_dot(d_mix, attn), "dp", scatter_dimension=0, tiled=True)
    heads_here = grad_t.shape[1] // HD
    head_grad = grad_t.reshape(rows_dp, heads_here, HD)
    squares = lax.psum(jnp.sum(head_grad * head_grad, axis=(0, 2)), "dp")
    ortho = head_grad / (jnp.sqrt(squares) + 1e-07)[None, :, None]
    gram = gram_of(ortho)
    for sweep in range(NS_STEPS):
        if sweep > 0:
            gram = gram_of(ortho)
        poly = COEF_B * gram + COEF_C * jnp.einsum(
            "hij,hjk->hik", gram, gram, precision=lax.Precision.HIGHEST
        )
        ortho = COEF_A * ortho + jnp.einsum(
            "dhj,hij->dhi", ortho, poly, precision=lax.Precision.HIGHEST
        )
    muon_step = (0.2 * math.sqrt(D) * ortho).reshape(rows_dp, heads_here * HD).T
    return (block_out, token_grad, muon_step)


def solution(mesh):
    placed = (
        P("dp", "mp"),
        P("dp", "mp"),
        P("dp", "mp"),
        P("dp", "mp"),
        P("dp", "mp"),
        P("mp", "dp"),
        P(),
        P(),
        P("dp"),
        P("dp"),
        P("dp"),
    )
    return jax.shard_map(
        per_device,
        mesh=mesh,
        in_specs=placed,
        out_specs=(P("dp", "mp"), P("dp", "mp"), P("mp", "dp")),
        check_vma=False,
    )
```

profile of v0, /device:TPU:1, one launch (start us, length us, event | category | flops | bytes accessed | tf_op | source)
XLA Modules:
  0.0 1106.8 jit_solution(2116331942427348707)
XLA Ops:
  7.2 3.1 copy.88
  10.3 1.6 copy.89
  11.9 3.6 gather_fusion
  15.6 0.7 all-gather.11.cloned.1.call-update
  17.1 1.6 gather_fusion.2
  20.6 1.0 gather_fusion.1
  21.6 0.7 fusion.52
  22.3 22.8 %all-gather.17.cloned.1.call-done = bf16[128,4096]{1,0:T(8,128)(2,1)} async-done(((bf16[128,1024]{1,0:T(8,128)(2,1)}), bf16[128,4096]{1,0:T(8,128)(2,1)}) %all-gather.17.cloned.1.call-update) | async-done | bytes 1048592 | tf_op jit(solution)/shard_map/all_gather | solution.py:114
  45.1 1.7 fusion.3
  47.4 81.2 %all-gather.11.cloned.1.call-done = bf16[4096,512]{1,0:T(8,128)(2,1)} async-done(((bf16[64,512]{1,0:T(8,128)(2,1)}), bf16[4096,512]{1,0:T(8,128)(2,1)}) %all-gather.11.cloned.1.call-update) | async-done | bytes 4194320 | tf_op jit(solution)/shard_map/all_gather | solution.py:118
  128.6 3.3 convolution_convert_fusion.3
  132.0 75.7 %all-gather.13.cloned.1.call-done = bf16[4096,512]{1,0:T(8,128)(2,1)} async-done(((bf16[64,512]{1,0:T(8,128)(2,1)}), bf16[4096,512]{1,0:T(8,128)(2,1)}) %all-gather.13.cloned.1.call-update) | async-done | bytes 4194320 | tf_op jit(solution)/shard_map/all_gather | solution.py:119
  207.7 3.0 convolution_convert_fusion.2
  210.7 0.8 copy.60
  211.5 20.4 %all-gather.19.cloned.1.call-done = bf16[128,4096]{1,0:T(8,128)(2,1)} async-done(((bf16[128,1024]{1,0:T(8,128)(2,1)}), bf16[128,4096]{1,0:T(8,128)(2,1)}) %all-gather.19.cloned.1.call-update) | async-done | bytes 1048592 | tf_op jit(solution)/shard_map/all_gather | solution.py:115
  231.9 83.4 %all-gather.15.cloned.1.call-done = bf16[512,4096]{0,1:T(8,128)(2,1)} async-done(((bf16[512,64]{0,1:T(8,128)(2,1)}), bf16[512,4096]{0,1:T(8,128)(2,1)}) %all-gather.15.cloned.1.call-update) | async-done | bytes 4194320 | tf_op jit(solution)/shard_map/all_gather | solution.py:121
  315.2 3.3 convolution_convert_fusion.1
  318.5 0.8 copy.61
  319.3 1.1 fusion.11
  320.4 0.8 fusion.58
  321.2 1.8 convolution_convert_fusion.5
  323.0 71.2 %all-gather.9.cloned.1.call-done = bf16[4096,512]{1,0:T(8,128)(2,1)} async-done(((bf16[64,512]{1,0:T(8,128)(2,1)}), bf16[4096,512]{1,0:T(8,128)(2,1)}) %all-gather.9.cloned.1.call-update) | async-done | bytes 4194320 | tf_op jit(solution)/shard_map/all_gather | solution.py:120
  394.2 3.0 fusion.14
  397.9 1.3 convolution_convert_fusion.7
  399.2 1.3 convolution_convert_fusion.6
  400.6 3.9 fusion.59
  404.5 1.5 convolution_add_fusion.1
  406.7 2.6 fusion.2
  409.6 4.8 convolution_convert_fusion
  414.4 4.6 fusion.28
  419.3 0.8 dynamic_slice.9
  420.2 1.6 convert_multiply_fusion
  421.8 9.1 reduce-scatter.6.cloned.1.call-done
  431.0 1.3 multiply_reduce_fusion
  432.2 27.3 %reduce-scatter.4.cloned.1.call-done = bf16[128,1024]{1,0:T(8,128)(2,1)} async-done(((bf16[128,4096]{1,0:T(8,128)(2,1)}), bf16[128,1024]{1,0:T(8,128)(2,1)}) %reduce-scatter.4.cloned.1.call-update) | async-done | bytes 262160 | tf_op jit(solution)/shard_map/reduce_scatter | solution.py:129
  459.5 1.1 fusion.23
  460.6 6.6 all-reduce
  467.3 144.3 %reduce-scatter.8.cloned.1.call-done = f32[64,512]{1,0:T(8,128)} async-done(((f32[4096,512]{1,0:T(8,128)}), f32[64,512]{1,0:T(8,128)}) %reduce-scatter.8.cloned.1.call-update) | async-done | bytes 131088 | tf_op jit(solution)/shard_map/reduce_scatter | solution.py:162
  611.6 1.0 multiply_reduce_fusion.2
  612.7 5.2 scatter_custom_fusion
  617.9 129.0 %psum.37 = f32[4]{0:T(128)S(1)} all-reduce(f32[4]{0:T(128)S(1)} %bitcast_reduce_fusion), channel_id=1, replica_groups=mesh['dp'=64,'mp'=4] {'dp'}, use_global_device_ids=true, to_apply=%region_16.17 | all-reduce | flops 4 | bytes 32 | tf_op jit(solution)/shard_map/psum | solution.py:165
  746.9 1.4 fusion.53
  748.4 172.8 %all-reduce.4.cloned.1.call-done = f32[4,128,128]{2,1,0:T(8,128)} async-done(((f32[4,128,128]{2,1,0:T(8,128)}), f32[4,128,128]{2,1,0:T(8,128)}) %all-reduce.4.cloned.1.call-update) | async-done | bytes 262160 | tf_op jit(solution)/shard_map/psum | solution.py:102
  921.2 1.5 fusion.10
  923.4 1.3 fusion.60
  924.8 3.1 scatter_custom_fusion.1
  927.9 169.5 %all-reduce.6.cloned.1.call-done = f32[4,128,128]{2,1,0:T(8,128)} async-done(((f32[4,128,128]{2,1,0:T(8,128)}), f32[4,128,128]{2,1,0:T(8,128)}) %all-reduce.6.cloned.1.call-update) | async-done | bytes 262160 | tf_op jit(solution)/shard_map/psum | solution.py:102
  1097.4 1.5 fusion.9
  (80 shorter events, 7.0 us)
Async XLA Ops:
  7.2 13.4 %copy-start = (s32[1024]{0:T(1024)S(1)}, s32[1024]{0:T(1024)}, u32[]{:S(2)}) copy-start(s32[1024]{0:T(1024)} %param.21) | copy-start | bytes 12292
  7.2 37.9 %all-gather.17.cloned.1.call-start = ((), (), s32[]{:S(2)}) async-start(), calls=%async_computation.12 | async-start | bytes 1310720 | tf_op jit(solution)/shard_map/all_gather | solution.py:114
  10.3 1.6 copy-start.16
  11.9 6.8 copy-start.20
  15.5 29.6 %copy-start.14 = (f32[4096]{0:T(1024)S(1)}, f32[4096]{0:T(1024)}, u32[]{:S(2)}) copy-start(f32[4096]{0:T(1024)} %param.18) | copy-start | bytes 49156
  15.6 113.1 %all-gather.11.cloned.1.call-start = ((), (), s32[]{:S(2)}) async-start(), calls=%async_computation.4 | async-start | bytes 4259840 | tf_op jit(solution)/shard_map/all_gather | solution.py:118
  16.3 191.4 %all-gather.13.cloned.1.call-start = ((), (), s32[]{:S(2)}) async-start(), calls=%async_computation.5 | async-start | bytes 4259840 | tf_op jit(solution)/shard_map/all_gather | solution.py:119
  17.1 111.6 %copy-start.19 = (f32[4096]{0:T(1024)S(1)}, f32[4096]{0:T(1024)}, u32[]{:S(2)}) copy-start(f32[4096]{0:T(1024)} %param.17) | copy-start | bytes 49156
  17.1 214.8 %all-gather.19.cloned.1.call-start = ((), (), s32[]{:S(2)}) async-start(), calls=%async_computation.13 | async-start | bytes 1310720 | tf_op jit(solution)/shard_map/all_gather | solution.py:115
  18.7 296.5 %all-gather.15.cloned.1.call-start = ((), (), s32[]{:S(2)}) async-start(), calls=%async_computation.6 | async-start | bytes 4259840 | tf_op jit(solution)/shard_map/all_gather | solution.py:121
  19.3 374.9 %all-gather.9.cloned.1.call-start = ((), (), s32[]{:S(2)}) async-start(), calls=%async_computation.3 | async-start | bytes 4259840 | tf_op jit(solution)/shard_map/all_gather | solution.py:120
  19.9 411.1 %reduce-scatter.6.cloned.1.call-start = ((), (), s32[]{:S(2)}) async-start(), calls=%async_computation.8 | async-start | bytes 1310720 | tf_op jit(solution)/shard_map/reduce_scatter | solution.py:148
  46.8 161.0 %copy-start.17 = (f32[128]{0:T(128)}, f32[128]{0:T(128)S(1)}, u32[]{:S(2)}) copy-start(f32[128]{0:T(128)S(1)} %add_rsqrt_fusion) | copy-start | bytes 1540
  47.4 160.4 %copy-start.6 = (bf16[128,4096]{1,0:T(8,128)(2,1)S(1)}, bf16[128,4096]{1,0:T(8,128)(2,1)}, u32[]{:S(2)}) copy-start(bf16[128,4096]{1,0:T(8,128)(2,1)} %all-gather.17.cloned.1.call-done) | copy-start | bytes 3145732
  394.2 3.0 copy-start.9
  397.2 0.7 copy-start.12
  400.6 3.9 copy-start.5
  404.5 2.2 copy-start.4
  404.5 2.2 copy-start.10
  406.7 2.6 copy-start.13
  409.2 50.3 %reduce-scatter.4.cloned.1.call-start = ((), (), s32[]{:S(2)}) async-start(), calls=%async_computation.7 | async-start | bytes 1310720 | tf_op jit(solution)/shard_map/reduce_scatter | solution.py:129
  409.5 4.9 copy-start.2
  414.4 197.2 %reduce-scatter.8.cloned.1.call-start = ((), (), s32[]{:S(2)}) async-start(), calls=%async_computation.9 | async-start | bytes 8519680 | tf_op jit(solution)/shard_map/reduce_scatter | solution.py:162
  419.0 1.2 copy-start.7
  419.0 1.2 copy-start.18
  419.0 40.5 %copy-start.3 = (bf16[128,1024]{1,0:T(8,128)(2,1)S(1)}, bf16[128,1024]{1,0:T(8,128)(2,1)}, u32[]{:S(2)}) copy-start(bf16[128,1024]{1,0:T(8,128)(2,1)} %gather_fusion.2) | copy-start | bytes 786436
  419.0 502.2 %all-reduce.4.cloned.1.call-start = ((), (), s32[]{:S(2)}) async-start(), calls=%async_computation.10 | async-start | bytes 524288 | tf_op jit(solution)/shard_map/psum | solution.py:102
  420.2 192.5 %copy-start.15 = (f32[128]{0:T(128)S(1)}, f32[128]{0:T(128)}, u32[]{:S(2)}) copy-start(f32[128]{0:T(128)} %get-tuple-element.8) | copy-start | bytes 1540
  611.6 135.3 %copy-start.11 = (f32[64,512]{1,0:T(8,128)S(1)}, f32[64,512]{1,0:T(8,128)}, u32[]{:S(2)}) copy-start(f32[64,512]{1,0:T(8,128)} %reduce-scatter.8.cloned.1.call-done) | copy-start | bytes 393220
  617.9 306.8 %copy-start.8 = (bf16[128,1024]{1,0:T(8,128)(2,1)S(1)}, bf16[128,1024]{1,0:T(8,128)(2,1)}, u32[]{:S(2)}) copy-start(bf16[128,1024]{1,0:T(8,128)(2,1)} %reduce-scatter.6.cloned.1.call-done) | copy-start | bytes 786436
  617.9 306.8 %dynamic-slice-start = ((f32[4096]{0:T(1024)}, s32[]{:T(128)}), f32[1024]{0:T(1024)S(1)}, s32[]{:S(2)}) async-start(f32[4096]{0:T(1024)} %param.18, s32[]{:T(128)} %select_n.35), calls=%async_computation.14 | async-start | bytes 8704 | tf_op jit(solution)/shard_map/dynamic_slice | solution.py:146
  748.3 349.1 %all-reduce.6.cloned.1.call-start = ((), (), s32[]{:S(2)}) async-start(), calls=%async_computation.11 | async-start | bytes 524288 | tf_op jit(solution)/shard_map/psum | solution.py:102
  927.9 172.4 %copy-start.1 = (bf16[1024,1024]{1,0:T(8,128)(2,1)}, bf16[1024,1024]{1,0:T(8,128)(2,1)S(1)}, u32[]{:S(2)}) copy-start(bf16[1024,1024]{1,0:T(8,128)(2,1)S(1)} %scatter_custom_fusion.1) | copy-start | bytes 6291460
Sparse Core Ops, SparseCore 0:
  15.7 29.3 all-gather.16
  47.9 80.7 all-gather.10
  131.4 76.2 all-gather.12
  209.4 22.4 all-gather.18
  234.5 80.7 all-gather.14
  317.9 76.2 all-gather.8
  409.4 21.5 reduce-scatter.5
  433.7 25.8 reduce-scatter.3
  463.7 147.8 reduce-scatter.7
  748.4 172.7 all-reduce.3
  924.8 172.5 all-reduce.5
where the time goes:
time: 1110 us
  waiting for transfers between devices  880 us (79%)
  blocking collectives  136 us (12%)
  matrix products  42.9 us (4%)
  other arithmetic  17.1 us (2%)
  local copies, waits for them, and re-layouts  15.3 us (1%)
  between operations  14.8 us (1%)
    psum x2, waiting for transfers between devices, gram_of(): return lax.psum(local_gram, 'dp')  342 us
    reduce_scatter x1, waiting for transfers between devices, per_device(): lax.psum_scatter(column_dot(d_mix, attn), 'dp', scatter_dimension=0, tile...  144 us
    psum x1, blocking collectives, per_device(): squares = lax.psum(jnp.sum(head_grad * head_grad, axis=(0, 2)), 'dp')  129 us
    all_gather x1, waiting for transfers between devices, per_device(): lax.all_gather(w_out, 'dp', axis=1, tiled=True)  83.4 us
    all_gather x1, waiting for transfers between devices, per_device(): lax.all_gather(w_query, 'dp', axis=0, tiled=True)  81.2 us
    all_gather x1, waiting for transfers between devices, per_device(): lax.all_gather(w_key, 'dp', axis=0, tiled=True)  75.7 us
    all_gather x1, waiting for transfers between devices, per_device(): lax.all_gather(w_value, 'dp', axis=0, tiled=True)  71.2 us
    reduce_scatter x1, waiting for transfers between devices, per_device(): lax.psum_scatter(partial_mixed.astype(jnp.bfloat16), 'mp', scatter_dimens...  27.3 us
  transfers between devices with their start and end apart: 11, of which 11 were waited for; matrix products, arithmetic and copies ran while one was open for 3% of the time, Pallas kernels for 0%

commit v1 on v0

v1 whole, which is shorter than its diff:
```python
import math

import jax
import jax.numpy as jnp
from jax import lax
from jax.experimental import pallas as pl
from jax.experimental.pallas import tpu as pltpu
from jax.sharding import PartitionSpec as P

D = 4096
HD = 128
CAP = 128
NZ, NY, NC, NX = 8, 4, 2, 4
FEAT = D // NX
EXTRA = 128
EPS = 1e-06
COEF_A = 3.4445
COEF_B = -4.775
COEF_C = 2.0315
BF = jnp.bfloat16
F32 = jnp.float32
VMEM_LIMIT = 48 * 1024 * 1024


def dp_index(z, y, c):
    return ((z % NZ) * NY + (y % NY)) * NC + c


def dp_perm(dz, dy, dc):
    return [
        (dp_index(z, y, c), dp_index(z + dz, y + dy, (c + dc) % NC))
        for z in range(NZ)
        for y in range(NY)
        for c in range(NC)
    ]


GROUPS_ZY = [[dp_index(z, y, c) for z in range(NZ) for y in range(NY)] for c in range(NC)]
GROUPS_Z = [[dp_index(z, y, c) for z in range(NZ)] for y in range(NY) for c in range(NC)]


def move_y(v, k):
    return lax.ppermute(v, "dp", dp_perm(0, k, 0))


def swap_core(v):
    return lax.ppermute(v, "dp", dp_perm(0, 0, 1))


def move_x(v, k):
    return lax.ppermute(v, "mp", [(i, (i + k) % NX) for i in range(NX)])


def dot_nn(left, right):
    return jnp.dot(left, right, preferred_element_type=F32)


def dot_nt(left, right):
    return lax.dot_general(
        left, right, (((1,), (1,)), ((), ())), preferred_element_type=F32
    )


def dot_tn(left, right):
    return lax.dot_general(
        left, right, (((0,), (0,)), ((), ())), preferred_element_type=F32
    )


def forward_kernel(
    place, normed, d_mix, weight, mask, qkv_out, da_out, attn_out, probs_out, *rest
):
    grads, (qkv_acc, da_acc) = rest[:NY], rest[NY:]
    step = pl.program_id(0)

    @pl.when(step == 0)
    def _():
        qkv_acc[...] = jnp.zeros_like(qkv_acc)
        da_acc[...] = jnp.zeros_like(da_acc)

    qkv_acc[...] += dot_nn(normed[0], weight[:, : 6 * HD])
    x_abs = lax.rem(place[0] + step, NX)
    da_acc[...] += dot_nn(d_mix[x_abs], weight[:, 6 * HD :])

    @pl.when(step == NX - 1)
    def _():
        qkv_out[...] = qkv_acc[...].astype(BF)
        da_out[...] = da_acc[...].astype(BF)
        for s in range(2):
            rows = pl.ds(s * CAP, CAP)
            for h in range(2):
                query = qkv_out[rows, pl.ds(h * HD, HD)]
                key = qkv_out[rows, pl.ds((2 + h) * HD, HD)]
                value = qkv_out[rows, pl.ds((4 + h) * HD, HD)]
                scores = dot_nt(query, key) * HD ** (-0.5)
                scores = jnp.where(mask[rows, :] > 0.0, scores, -1e30)
                expo = jnp.exp(scores - jnp.max(scores, axis=1, keepdims=True))
                probs = expo / jnp.sum(expo, axis=1, keepdims=True)
                probs_out[s, h] = probs
                attn_out[rows, pl.ds(h * HD, HD)] = dot_nn(probs.astype(BF), value).astype(BF)
        attn = attn_out[...]
        for k in range(NY):
            y_abs = lax.rem(place[1] + k, NY)
            for i in range(NX):
                for j in range(2):
                    col = pl.ds(pl.multiple_of(j * 512 + y_abs * 128, 128), 128)
                    grads[k][2 * i + j] = dot_tn(attn, d_mix[i, :, col]).astype(BF)


def forward(place, normed, d_mix, weight, mask):
    whole = lambda *dims: pl.BlockSpec(dims, lambda i, p: (0,) * len(dims))
    return pl.pallas_call(
        forward_kernel,
        grid_spec=pltpu.PrefetchScalarGridSpec(
            num_scalar_prefetch=1,
            grid=(NX,),
            in_specs=[
                pl.BlockSpec((1, 2 * CAP, FEAT), lambda i, p: (lax.rem(p[0] + i, NX), 0, 0)),
                whole(NX, 2 * CAP, FEAT),
                pl.BlockSpec((FEAT, 8 * HD), lambda i, p: (lax.rem(p[0] + i, NX), 0)),
                whole(2 * CAP, CAP),
            ],
            out_specs=[
                whole(2 * CAP, 6 * HD),
                whole(2 * CAP, 2 * HD),
                whole(2 * CAP, 2 * HD),
                whole(2, 2, CAP, CAP),
            ]
            + [whole(NZ, 2 * HD, 128)] * NY,
            scratch_shapes=[
                pltpu.VMEM((2 * CAP, 6 * HD), F32),
                pltpu.VMEM((2 * CAP, 2 * HD), F32),
            ],
        ),
        out_shape=[
            jax.ShapeDtypeStruct((2 * CAP, 6 * HD), BF),
            jax.ShapeDtypeStruct((2 * CAP, 2 * HD), BF),
            jax.ShapeDtypeStruct((2 * CAP, 2 * HD), BF),
            jax.ShapeDtypeStruct((2, 2, CAP, CAP), F32),
        ]
        + [jax.ShapeDtypeStruct((NZ, 2 * HD, 128), BF)] * NY,
        compiler_params=pltpu.CompilerParams(vmem_limit_bytes=VMEM_LIMIT),
        cost_estimate=pl.CostEstimate(
            flops=2 * 256 * 4096 * 1280, bytes_accessed=16 << 20, transcendentals=1 << 16
        ),
        name="forward",
    )(place, normed, d_mix, weight, mask)


def backward_kernel(place, qkv, d_attn, attn, probs_in, weight, own_out, sib_out, d_qkv, sums):
    step = pl.program_id(0)

    @pl.when(step == 0)
    def _():
        lane = lax.broadcasted_iota(jnp.int32, (CAP, EXTRA), 1)
        for s in range(2):
            rows = pl.ds(s * CAP, CAP)
            gate_sum = jnp.zeros((CAP, 1), F32)
            stat_sum = jnp.zeros((CAP, 1), F32)
            for h in range(2):
                query = qkv[rows, pl.ds(h * HD, HD)]
                key = qkv[rows, pl.ds((2 + h) * HD, HD)]
                value = qkv[rows, pl.ds((4 + h) * HD, HD)]
                d_head = d_attn[rows, pl.ds(h * HD, HD)]
                probs = probs_in[s, h]
                d_probs = dot_nt(d_head, value)
                row_sum = jnp.sum(d_probs * probs, axis=1, keepdims=True)
                d_scores = (probs * (d_probs - row_sum) * HD ** (-0.5)).astype(BF)
                d_query = dot_nn(d_scores, key).astype(BF)
                d_key = dot_tn(d_scores, query).astype(BF)
                d_value = dot_tn(probs.astype(BF), d_head).astype(BF)
                d_qkv[rows, pl.ds(h * HD, HD)] = d_query
                d_qkv[rows, pl.ds((2 + h) * HD, HD)] = d_key
                d_qkv[rows, pl.ds((4 + h) * HD, HD)] = d_value
                out = attn[rows, pl.ds(h * HD, HD)]
                gate_sum += jnp.sum(out.astype(F32) * d_head.astype(F32), axis=1, keepdims=True)
                stat_sum += jnp.sum(
                    query.astype(F32) * d_query.astype(F32)
                    + key.astype(F32) * d_key.astype(F32)
                    + value.astype(F32) * d_value.astype(F32),
                    axis=1,
                    keepdims=True,
                )
            sums[s, 0] = jnp.where(lane == 0, gate_sum, 0.0).astype(BF)
            sums[s, 1] = jnp.where(lane == 0, stat_sum, 0.0).astype(BF)

    mixed = dot_nt(attn[...], weight[:, 6 * HD :]).astype(BF)
    d_normed = dot_nt(d_qkv[...], weight[:, : 6 * HD]).astype(BF)
    for s, out in ((0, own_out), (1, sib_out)):
        out[0, 0, :, :FEAT] = mixed[s * CAP : (s + 1) * CAP]
        out[0, 1, :, :FEAT] = d_normed[s * CAP : (s + 1) * CAP]
        out[0, 0, :, FEAT:] = sums[s, 0]
        out[0, 1, :, FEAT:] = sums[s, 1]


def backward(place, qkv, d_attn, attn, probs, weight):
    whole = lambda *dims: pl.BlockSpec(dims, lambda i, p: (0,) * len(dims))
    piece = pl.BlockSpec((1, 2, CAP, FEAT + EXTRA), lambda i, p: (i, 0, 0, 0))
    piece_type = jax.ShapeDtypeStruct((NX, 2, CAP, FEAT + EXTRA), BF)
    return pl.pallas_call(
        backward_kernel,
        grid_spec=pltpu.PrefetchScalarGridSpec(
            num_scalar_prefetch=1,
            grid=(NX,),
            in_specs=[
                whole(2 * CAP, 6 * HD),
                whole(2 * CAP, 2 * HD),
                whole(2 * CAP, 2 * HD),
                whole(2, 2, CAP, CAP),
                pl.BlockSpec((FEAT, 8 * HD), lambda i, p: (lax.rem(p[0] + i, NX), 0)),
            ],
            out_specs=[piece, piece],
            scratch_shapes=[
                pltpu.VMEM((2 * CAP, 6 * HD), BF),
                pltpu.VMEM((2, 2, CAP, EXTRA), BF),
            ],
        ),
        out_shape=[piece_type, piece_type],
        compiler_params=pltpu.CompilerParams(vmem_limit_bytes=VMEM_LIMIT),
        cost_estimate=pl.CostEstimate(
            flops=2 * 256 * 4096 * 1024, bytes_accessed=14 << 20, transcendentals=0
        ),
        name="backward",
    )(place, qkv, d_attn, attn, probs, weight)


def high(left, right, dims):
    return lax.dot_general(
        left,
        right,
        (dims, ((), ())),
        precision=lax.Precision.HIGHEST,
        preferred_element_type=F32,
    )


def gram_kernel(parts, total_out, gram_out):
    total = parts[0].astype(F32)
    for k in range(1, NZ):
        total = total + parts[k].astype(F32)
    total_out[...] = total
    for h in range(2):
        block = total[h * HD : (h + 1) * HD]
        gram_out[h] = high(block, block, ((1,), (1,)))


def gram_of(parts):
    return pl.pallas_call(
        gram_kernel,
        out_shape=[
            jax.ShapeDtypeStruct((2 * HD, 128), F32),
            jax.ShapeDtypeStruct((2, HD, HD), F32),
        ],
        compiler_params=pltpu.CompilerParams(vmem_limit_bytes=VMEM_LIMIT),
        name="gram",
    )(parts)


def muon_kernel(gram_in, total, out):
    row = lax.broadcasted_iota(jnp.int32, (HD, HD), 0)
    col = lax.broadcasted_iota(jnp.int32, (HD, HD), 1)
    eye = jnp.where(row == col, 1.0, 0.0).astype(F32)
    nn = ((1,), (0,))
    for h in range(2):
        gram = gram_in[h]
        diag = jnp.sum(gram * eye, axis=1, keepdims=True)
        inv = 1.0 / (jnp.sqrt(jnp.sum(diag, axis=0, keepdims=True)) + 1e-07)
        gram = gram * inv * inv
        step = COEF_A * eye + COEF_B * gram + COEF_C * high(gram, gram, nn)
        gram = high(high(step, gram, nn), step, nn)
        last = COEF_A * eye + COEF_B * gram + COEF_C * high(gram, gram, nn)
        step = high(last, step, nn) * (inv * (0.2 * math.sqrt(D)))
        block = total[h * HD : (h + 1) * HD]
        out[:, h * HD : (h + 1) * HD] = high(block, step, ((0,), (1,)))


def muon(gram, total):
    return pl.pallas_call(
        muon_kernel,
        out_shape=jax.ShapeDtypeStruct((128, 2 * HD), F32),
        compiler_params=pltpu.CompilerParams(vmem_limit_bytes=VMEM_LIMIT),
        name="muon",
    )(gram, total)


def per_device(
    tokens, cotangent, w_query, w_key, w_value, w_out, gain, w_router, chosen, counts, doc_start
):
    dp = lax.axis_index("dp")
    x = lax.axis_index("mp")
    c = lax.rem(dp, NC)
    y = lax.rem(lax.div(dp, NC), NY)
    place = jnp.stack([x, y]).astype(jnp.int32)

    stacked = jnp.concatenate(
        [w.reshape(64, 2, 2 * HD) for w in (w_query, w_key, w_value, w_out.T)], axis=2
    )
    keep = lax.dynamic_index_in_dim(stacked, c, 1, keepdims=False)
    give = lax.dynamic_index_in_dim(stacked, 1 - c, 1, keepdims=False)
    take = swap_core(give)
    shard = jnp.where(
        c == 0, jnp.concatenate([keep, take]), jnp.concatenate([take, keep])
    )
    weight = lax.all_gather(shard, "dp", axis=0, tiled=True, axis_index_groups=GROUPS_ZY)

    picks = chosen[:, None] == jnp.arange(tokens.shape[0])[None, :]
    onehot = picks.astype(BF)
    live_own = jnp.arange(CAP) < counts[0]
    docs_own = jnp.sum(jnp.where(picks, doc_start[None, :], 0), axis=1)
    rows_part = dot_nn(onehot, tokens).astype(BF)
    grad_part = dot_nn(onehot, cotangent).astype(BF)
    meta_own = jnp.stack([chosen, docs_own, live_own.astype(jnp.int32)])
    meta = jnp.stack([meta_own, swap_core(meta_own)])
    position, docs = meta[:, 0], meta[:, 1]
    live = meta[:, 2] > 0

    part = jnp.stack([rows_part, grad_part])
    around = jnp.stack([part] + [move_x(part, k) for k in (3, 2, 1)])
    both = jnp.stack([around, swap_core(around)], axis=2)
    both = jnp.roll(both, x, axis=0).reshape(NX, 2, 2 * CAP, FEAT)
    rows_wide = both[:, 0].astype(F32)
    grad_wide = both[:, 1].astype(F32)
    gain_parts = gain.reshape(NX, 1, FEAT)
    router_parts = w_router.reshape(NX, 1, FEAT)
    mean_square = jnp.sum(rows_wide * rows_wide, axis=(0, 2)) / D
    inv_scale = lax.rsqrt(mean_square + EPS)[:, None]
    gate = jax.nn.sigmoid(jnp.sum(rows_wide * router_parts, axis=(0, 2)))
    normed = (rows_wide * inv_scale * gain_parts).astype(BF)
    gate_live = jnp.where(live.reshape(-1), gate, 0.0)[:, None]
    d_mix = (gate_live * grad_wide).astype(BF)
    allowed = (
        (position[:, None, :] <= position[:, :, None])
        & (docs[:, None, :] == docs[:, :, None])
        & live[:, None, :]
    )
    allowed = allowed | jnp.eye(CAP, dtype=bool)[None]
    mask = allowed.reshape(2 * CAP, CAP).astype(F32)

    qkv, d_attn, attn, probs, grad_0, grad_1, grad_2, grad_3 = forward(
        place, normed, d_mix, weight, mask
    )
    moved = [move_y(grad_1, 1), move_y(grad_3, 3), move_y(grad_2, 2)]

    own, sibling = backward(place, qkv, d_attn, attn, probs, weight)
    got = swap_core(sibling)
    sent = [
        move_x((own[k].astype(F32) + got[k].astype(F32)).astype(BF), k) for k in (1, 3, 2)
    ]

    column = grad_0.astype(F32)
    for m in moved:
        column = column + m.astype(F32)
    column = lax.all_to_all(
        column.astype(BF), "dp", 0, 0, tiled=True, axis_index_groups=GROUPS_Z
    )
    total, gram = gram_of(column)
    pieces = gram.reshape(NZ * NY, 8, 128)
    pieces = lax.all_to_all(pieces, "dp", 0, 0, tiled=True, axis_index_groups=GROUPS_ZY)
    piece = jnp.broadcast_to(jnp.sum(pieces, axis=0)[None], (NZ * NY, 8, 128))
    gram = lax.all_to_all(piece, "dp", 0, 0, tiled=True, axis_index_groups=GROUPS_ZY)
    ortho = muon(gram.reshape(2, HD, HD), total).reshape(2, 64, 2 * HD)
    own_cols = lax.dynamic_index_in_dim(ortho, c, 0, keepdims=False)
    other_cols = swap_core(lax.dynamic_index_in_dim(ortho, 1 - c, 0, keepdims=False))
    muon_step = jnp.where(
        c == 0,
        jnp.concatenate([own_cols, other_cols], axis=1),
        jnp.concatenate([other_cols, own_cols], axis=1),
    ).T

    result = own[0].astype(F32) + got[0].astype(F32)
    for s in sent:
        result = result + s.astype(F32)
    mixed, d_normed = result[0, :, :FEAT], result[1, :, :FEAT]
    gate_sum, stat_sum = result[0, :, FEAT : FEAT + 1], result[1, :, FEAT : FEAT + 1]
    rows_own = rows_part.astype(F32)
    gate_own = gate[:CAP, None]
    inv_own = inv_scale[:CAP]
    hit = jnp.any(picks & live_own[:, None], axis=0)[:, None]
    updated = (rows_own + gate_own * mixed).astype(BF)

    def spread(values):
        return dot_tn(onehot, values).astype(BF)

    block_out = jnp.where(hit, spread(updated), tokens)
    gain_local = lax.dynamic_slice_in_dim(gain, x * FEAT, FEAT)
    router_local = lax.dynamic_slice_in_dim(w_router, x * FEAT, FEAT)
    d_logit = gate_sum * (1.0 - gate_own)
    d_rows = (
        grad_part.astype(F32)
        + inv_own * (d_normed * gain_local - rows_own * inv_own * (stat_sum / D))
        + d_logit * router_local
    )
    token_grad = jnp.where(hit, spread(d_rows.astype(BF)), cotangent)
    return (block_out, token_grad, muon_step)


def solution(mesh):
    placed = (
        P("dp", "mp"),
        P("dp", "mp"),
        P("dp", "mp"),
        P("dp", "mp"),
        P("dp", "mp"),
        P("mp", "dp"),
        P(),
        P(),
        P("dp"),
        P("dp"),
        P("dp"),
    )
    return jax.shard_map(
        per_device,
        mesh=mesh,
        in_specs=placed,
        out_specs=(P("dp", "mp"), P("dp", "mp"), P("mp", "dp")),
        check_vma=False,
    )
```

time: 1110 us -> 246 us (0.22)
  waiting for transfers between devices: 880 us -> 123 us
  blocking collectives: 136 us -> 34 us
  matrix products: 42.9 us -> 7.05 us
  starting transfers between devices: 0.62 us -> 22.3 us
  Pallas kernels: 0 us -> 20.9 us
    psum x2 -> x0, waiting for transfers between devices: 342 us -> none  [gram_of(): return lax.psum(local_gram, 'dp')]
    all_gather x6 -> x1, waiting for transfers between devices: 355 us -> 55.3 us  [per_device(): lax.all_gather(shard, 'dp', axis=0, tiled=True, axis_index_groups=GROUPS_ZY)]
    reduce_scatter x3 -> x0, waiting for transfers between devices: 181 us -> none  [the longest x1 144 us: per_device(): lax.psum_scatter(column_dot(d_mix, attn), 'dp', scatter_dimension=0, tile...]
    psum x2 -> x0, blocking collectives: 136 us -> none  [the longest x1 129 us: per_device(): squares = lax.psum(jnp.sum(head_grad * head_grad, axis=(0, 2)), 'dp')]
    ppermute x0 -> x14, waiting for transfers between devices: none -> 65.6 us  [the longest x6 38 us: move_x(): return lax.ppermute(v, 'mp', [(i, (i + k) % NX) for i in range(NX)])]
    dot_general x21 -> x4, matrix products: 42.9 us -> 7.05 us  [the longest x2 4.48 us: dot_tn(): lax.dot_general(left, right, (((0,), (0,)), ((), ())), preferred_element_...]
    all_to_all x0 -> x2, blocking collectives: none -> 34 us  [the longest x1 19.7 us: per_device(): lax.all_to_all(column.astype(BF), 'dp', 0, 0, tiled=True, axis_index_grou...]
    pallas_call x0 -> x4, Pallas kernels: none -> 20.9 us  [the longest x1 9.47 us: forward(): pl.pallas_call(forward_kernel, grid_spec=pltpu.PrefetchScalarGridSpec(num...]
  transfers between devices with their start and end apart: 11 -> 16, of which waited for: 11 -> 11; matrix products, arithmetic and copies ran while one was open for 3% -> 7% of each run, Pallas kernels for 0% -> 1%
where the time goes in v1:
time: 246 us; the launch traced here: 243 us
  waiting for transfers between devices  123 us (50%)
  blocking collectives  34 us (14%)
  starting transfers between devices  22.3 us (9%)
  Pallas kernels  20.9 us (8%)
  other arithmetic  15.9 us (6%)
  between operations  15 us (6%)
  matrix products  7.05 us (3%)
  local copies, waits for them, and re-layouts  4.92 us (2%)
    all_gather x1, waiting for transfers between devices, per_device(): lax.all_gather(shard, 'dp', axis=0, tiled=True, axis_index_groups=GROUPS_ZY)  55.3 us
    ppermute x6, waiting for transfers between devices, move_x(): return lax.ppermute(v, 'mp', [(i, (i + k) % NX) for i in range(NX)])  38 us
    ppermute x3, waiting for transfers between devices, move_y(): return lax.ppermute(v, 'dp', dp_perm(0, k, 0))  23.3 us
    all_to_all x1, blocking collectives, per_device(): lax.all_to_all(column.astype(BF), 'dp', 0, 0, tiled=True, axis_index_grou...  19.7 us
    all_to_all x1, blocking collectives, per_device(): lax.all_to_all(pieces, 'dp', 0, 0, tiled=True, axis_index_groups=GROUPS_ZY)  14.4 us
    pallas_call x1, Pallas kernels, forward(): pl.pallas_call(forward_kernel, grid_spec=pltpu.PrefetchScalarGridSpec(num...  9.47 us
    ppermute x5, starting transfers between devices, swap_core(): return lax.ppermute(v, 'dp', dp_perm(0, 0, 1))  9.37 us
    pallas_call x1, Pallas kernels, backward(): pl.pallas_call(backward_kernel, grid_spec=pltpu.PrefetchScalarGridSpec(nu...  8.65 us
  transfers between devices with their start and end apart: 16, of which 11 were waited for; matrix products, arithmetic and copies ran while one was open for 7% of the time, Pallas kernels for 1%

profile of v1, /device:TPU:1, one launch (start us, length us, event | category | flops | bytes accessed | tf_op | source)
XLA Modules:
  0.0 243.2 jit_solution(2619721083639863802)
XLA Ops:
  7.2 1.0 bitcast_dynamic-update-slice_fusion.3
  8.2 0.8 bitcast_dynamic-update-slice_fusion.2
  9.1 0.8 bitcast_dynamic-update-slice_fusion.1
  9.9 0.8 bitcast_dynamic-update-slice_fusion
  10.8 3.3 %collective-permute-start.5 = (bf16[64,1024]{1,0:T(8,128)(2,1)S(1)}, bf16[64,1024]{1,0:T(8,128)(2,1)S(1)}, u32[]{:S(2)}, u32[]{:S(2)}) collective-permute-start(bf16[64,1024]{1,0:T(8,128)(2,1)S(1)} %get-tuple-element.45), channel_id=1, source_target_pairs={{0,4},{4,0},{8,12},{12,8},{16,20},{20,16},{24,28},{28,24},{32,36},... | collective-permute-start | bytes 393224 | tf_op jit(solution)/shard_map/ppermute | solution.py:47
  14.1 1.0 collective-permute-done.5
  15.1 0.8 maximum_select_fusion
  15.9 2.1 convolution_convert_fusion.1
  18.0 0.5 convolution_convert_fusion
  18.6 0.8 collective-permute-start
  19.4 0.5 collective-permute-start.1
  19.9 0.6 collective-permute-start.2
  20.5 11.3 %collective-permute-done = bf16[2,128,1024]{2,1,0:T(8,128)(2,1)S(1)} collective-permute-done((bf16[2,128,1024]{2,1,0:T(8,128)(2,1)S(1)}, bf16[2,128,1024]{2,1,0:T(8,128)(2,1)S(1)}, u32[]{:S(2)}, u32[]{:S(2)}) %collective-permute-start) | collective-permute-done | bytes 524320 | tf_op jit(solution)/shard_map/ppermute | solution.py:51
  31.8 2.0 collective-permute-done.1
  33.8 12.2 %collective-permute-done.2 = bf16[2,128,1024]{2,1,0:T(8,128)(2,1)S(1)} collective-permute-done((bf16[2,128,1024]{2,1,0:T(8,128)(2,1)S(1)}, bf16[2,128,1024]{2,1,0:T(8,128)(2,1)S(1)}, u32[]{:S(2)}, u32[]{:S(2)}) %collective-permute-start.2) | collective-permute-done | bytes 524320 | tf_op jit(solution)/shard_map/ppermute | solution.py:51
  46.0 1.7 pad_maximum_fusion
  47.7 0.5 collective-permute-start.3
  49.0 0.3 collective-permute-start.4
  49.5 2.5 %collective-permute-done.4 = s32[3,128]{1,0:T(4,128)S(1)} collective-permute-done((s32[3,128]{1,0:T(4,128)S(1)}, s32[3,128]{1,0:T(4,128)S(1)}, u32[]{:S(2)}, u32[]{:S(2)}) %collective-permute-start.4) | collective-permute-done | bytes 1568 | tf_op jit(solution)/shard_map/ppermute | solution.py:47
  52.3 3.3 %fusion.5 = bf16[4,2,2,128,1024]{4,3,1,0,2:T(8,128)(2,1)S(1)} fusion(s32[]{:T(128)S(6)} %select_n.63, bf16[4,2,1,128,1024]{4,3,1,0,2:T(8,128)(2,1)S(1)} %get-tuple-element.41, bf16[4,2,1,128,1024]{4,3,1,0,2:T(8,128)(2,1)} %bitcast.8), kind=kLoop, calls=%fused_computation.12 | loop fusion | flops 6291456 | bytes 8388612 | tf_op jit(solution)/shard_map/jit(_roll_dynamic)/concatenate | solution.py:320
  55.6 0.6 copy.25
  56.2 0.8 fusion
  57.0 2.8 %fusion.7 = (bf16[4,256,1024]{2,1,0:T(8,128)(2,1)}, bf16[4,256,1024]{2,1,0:T(8,128)(2,1)S(1)}) fusion(bf16[4,2,256,1024]{3,2,1,0:T(8,128)(2,1)S(1)} %bitcast.124, f32[256]{0:T(256)S(1)} %get-tuple-element.31, f32[4,1024]{1,0:T(4,128)S(1)} %mul.105, f32[256]{0:T(256)S(1)} %add_rsqrt_fusion), kind=kLoop, calls=%fused_computation.15 | loop fusion | flops 7340032 | bytes 8407040 | tf_op jit(solution)/shard_map/convert_element_type | solution.py:330
  59.9 55.3 %all-gather.2.cloned.1.call-done.weight = bf16[4096,1024]{1,0:T(8,128)(2,1)} async-done(((bf16[128,1024]{1,0:T(8,128)(2,1)}), bf16[4096,1024]{1,0:T(8,128)(2,1)}) %all-gather.2.cloned.1.call-update) | async-done | bytes 8388624 | tf_op jit(solution)/shard_map/all_gather | solution.py:304
  115.1 9.5 %forward.1 = (bf16[256,768]{1,0:T(8,128)(2,1)S(1)}, bf16[256,256]{1,0:T(8,128)(2,1)S(1)}, bf16[256,256]{1,0:T(8,128)(2,1)S(1)}, f32[2,2,128,128]{3,2,1,0:T(8,128...) custom-call(s32[2]{0:T(128)S(1)} %pad_add_fusion.3.place, ...), custom_call_target="tpu_custom_call" | custom-call | flops 2684354560 | bytes 16777216 | tf_op jit(solution)/shard_map/forward/pallas_call | solution.py:112
  124.6 8.6 %backward.1 = (bf16[4,2,128,1152]{3,2,1,0:T(8,128)(2,1)S(1)}, bf16[4,2,128,1152]{3,2,1,0:T(8,128)(2,1)}) custom-call(s32[2]{0:T(128)S(1)} %pad_add_fusion.3.place, bf16[256,768]{1,0:T(8,128)(2,1)S(1)} %get-tuple-element.15.qkv, bf16[256,256]{1,0:T(8,128)(2,1)S(1)} %get-tuple-element.16.d_attn, bf16[256,256]{1,0:T(8,128)(2,1)S(1)} %get-tuple-element.17.attn, ...), custom_call_target="tpu_custom_call" | custom-call | flops 2147483648 | bytes 14680064 | tf_op jit(solution)/shard_map/backward/pallas_call | solution.py:200
  133.3 1.1 collective-permute-start.6
  134.3 2.7 %collective-permute-start.11 = (bf16[8,256,128]{2,1,0:T(8,128)(2,1)S(1)}, bf16[8,256,128]{2,1,0:T(8,128)(2,1)S(1)}, u32[]{:S(2)}, u32[]{:S(2)}) collective-permute-start(bf16[8,256,128]{2,1,0:T(8,128)(2,1)S(1)} %get-tuple-element.23), channel_id=1, source_target_pairs={{0,24},{4,28},{8,0},{12,4},{16,8},{20,12},{24,16},{28,20},{32,56},... | collective-permute-start | bytes 1572872 | tf_op jit(solution)/shard_map/ppermute | solution.py:43
  137.0 23.3 %collective-permute-done.10 = bf16[8,256,128]{2,1,0:T(8,128)(2,1)S(1)} collective-permute-done((bf16[8,256,128]{2,1,0:T(8,128)(2,1)S(1)}, bf16[8,256,128]{2,1,0:T(8,128)(2,1)S(1)}, u32[]{:S(2)}, u32[]{:S(2)}) %collective-permute-start.10) | collective-permute-done | bytes 524320 | tf_op jit(solution)/shard_map/ppermute | solution.py:43
  160.4 0.3 add_convert_fusion.3
  160.6 19.7 %all_to_all.15.parts = bf16[8,256,128]{2,1,0:T(8,128)(2,1)S(1)} all-to-all(bf16[8,256,128]{2,1,0:T(8,128)(2,1)S(1)} %add_convert_fusion.3), channel_id=1, replica_groups={{0,32,64,96,128,160,192,224},{4,36,68,100,132,164,196,228},{8,40,72,104..., dimensions={0} | all-to-all | bytes 1048576 | tf_op jit(solution)/shard_map/all_to_all | solution.py:353
  180.3 0.4 gram.1
  180.7 14.4 %all_to_all.16 = f32[32,8,128]{2,1,0:T(8,128)S(1)} all-to-all(f32[32,8,128]{2,1,0:T(8,128)S(1)} %bitcast.122), channel_id=1, replica_groups={{0,8,16,24,32,40,48,56,64,72,80,88,96,104,112,120,128,136,144,152,160,1..., dimensions={0} | all-to-all | bytes 262144 | tf_op jit(solution)/shard_map/all_to_all | solution.py:358
  195.1 0.7 broadcast_in_dim.48
  195.8 4.1 %all-to-all-start.2 = ((f32[32,8,128]{2,1,0:T(8,128)}), f32[32,8,128]{2,1,0:T(8,128)S(1)}, u32[]{:S(2)}, u32[]{:S(2)}) async-start(f32[32,8,128]{2,1,0:T(8,128)} %broadcast_in_dim.48), calls=%async_computation.2 | async-start | bytes 262144 | tf_op jit(solution)/shard_map/all_to_all | solution.py:360
  199.9 2.9 %fusion.10 = (bf16[2,128,1152]{2,1,0:T(8,128)(2,1)}, bf16[2,128,1152]{2,1,0:T(8,128)(2,1)}, bf16[2,128,1152]{2,1,0:T(8,128)(2,1)}) fusion(bf16[4,2,128,1152]{3,2,1,0:T(8,128)(2,1)} %collective-permute-done.6, bf16[4,2,128,1152]{3,2,1,0:T(8,128)(2,1)S(1)} %get-tuple-element.19), kind=kLoop, calls=%fused_computation.32 | loop fusion | flops 3538944 | bytes 5308416 | tf_op jit(solution)/shard_map/convert_element_type | solution.py:347
  202.8 1.2 collective-permute-start.7
  204.0 1.5 collective-permute-start.8
  205.4 1.5 collective-permute-start.9
  206.9 2.2 all-to-all-done.2
  209.1 2.4 muon.1
  211.5 4.2 %collective-permute-start.13 = (f32[64,256]{1,0:T(8,128)S(1)}, f32[64,256]{1,0:T(8,128)S(1)}, u32[]{:S(2)}, u32[]{:S(2)}) collective-permute-start(f32[64,256]{1,0:T(8,128)S(1)} %get-tuple-element.47), channel_id=1, source_target_pairs={{0,4},{4,0},{8,12},{12,8},{16,20},{20,16},{24,28},{28,24},{32,36},... | collective-permute-start | bytes 196616 | tf_op jit(solution)/shard_map/ppermute | solution.py:47
  215.9 0.7 collective-permute-done.13
  216.6 0.7 fusion.36
  217.3 12.5 %collective-permute-done.9 = bf16[2,128,1152]{2,1,0:T(8,128)(2,1)} collective-permute-done((bf16[2,128,1152]{2,1,0:T(8,128)(2,1)}, bf16[2,128,1152]{2,1,0:T(8,128)(2,1)}, u32[]{:S(2)}, u32[]{:S(2)}) %collective-permute-start.9) | collective-permute-done | bytes 589856 | tf_op jit(solution)/shard_map/ppermute | solution.py:51
  229.8 1.9 fusion.9
  231.9 2.2 convert_select_fusion.1
  234.1 2.3 convert_select_fusion
  (53 shorter events, 1.2 us)
Async XLA Ops:
  7.2 108.0 %all-gather.2.cloned.1.call-start = ((), (), s32[]{:S(2)}) async-start(), calls=%async_computation.3 | async-start | bytes 8650752 | tf_op jit(solution)/shard_map/all_gather | solution.py:304
  7.2 10.8 %copy-start.1 = (bf16[1024,1024]{1,0:T(8,128)(2,1)S(1)}, bf16[1024,1024]{1,0:T(8,128)(2,1)}, u32[]{:S(2)}) copy-start(bf16[1024,1024]{1,0:T(8,128)(2,1)} %param.12) | copy-start | bytes 6291460
  7.2 10.8 %copy-start.5 = (s32[128]{0:T(128)S(1)}, s32[128]{0:T(128)}, u32[]{:S(2)}) copy-start(s32[128]{0:T(128)} %param.19) | copy-start | bytes 1540
  10.8 4.3 %collective-permute-start.5 = (bf16[64,1024]{1,0:T(8,128)(2,1)S(1)}, bf16[64,1024]{1,0:T(8,128)(2,1)S(1)}, u32[]{:S(2)}, u32[]{:S(2)}) collective-permute-start(bf16[64,1024]{1,0:T(8,128)(2,1)S(1)} %get-tuple-element.45), channel_id=1, source_target_pairs={{0,4},{4,0},{8,12},{12,8},{16,20},{20,16},{24,28},{28,24},{32,36},... | collective-permute-start | bytes 393224 | tf_op jit(solution)/shard_map/ppermute | solution.py:47
  18.6 13.2 %collective-permute-start = (bf16[2,128,1024]{2,1,0:T(8,128)(2,1)S(1)}, bf16[2,128,1024]{2,1,0:T(8,128)(2,1)S(1)}, u32[]{:S(2)}, u32[]{:S(2)}) collective-permute-start(bf16[2,128,1024]{2,1,0:T(8,128)(2,1)S(1)} %get-tuple-element.43), channel_id=1, source_target_pairs={{0,3},{1,0},{2,1},{3,2},{4,7},{5,4},{6,5},{7,6},{8,11},{9,8},{10,9... | collective-permute-start | bytes 1572872 | tf_op jit(solution)/shard_map/ppermute | solution.py:51
  19.4 14.4 %collective-permute-start.1 = (bf16[2,128,1024]{2,1,0:T(8,128)(2,1)S(1)}, bf16[2,128,1024]{2,1,0:T(8,128)(2,1)S(1)}, u32[]{:S(2)}, u32[]{:S(2)}) collective-permute-start(bf16[2,128,1024]{2,1,0:T(8,128)(2,1)S(1)} %get-tuple-element.43), channel_id=1, source_target_pairs={{0,2},{1,3},{2,0},{3,1},{4,6},{5,7},{6,4},{7,5},{8,10},{9,11},{10,... | collective-permute-start | bytes 1572872 | tf_op jit(solution)/shard_map/ppermute | solution.py:51
  19.9 26.1 %collective-permute-start.2 = (bf16[2,128,1024]{2,1,0:T(8,128)(2,1)S(1)}, bf16[2,128,1024]{2,1,0:T(8,128)(2,1)S(1)}, u32[]{:S(2)}, u32[]{:S(2)}) collective-permute-start(bf16[2,128,1024]{2,1,0:T(8,128)(2,1)S(1)} %get-tuple-element.43), channel_id=1, source_target_pairs={{0,1},{1,2},{2,3},{3,0},{4,5},{5,6},{6,7},{7,4},{8,9},{9,10},{10,1... | collective-permute-start | bytes 1572872 | tf_op jit(solution)/shard_map/ppermute | solution.py:51
  46.0 2.8 %copy-start.7 = (s32[1024]{0:T(1024)S(1)}, s32[1024]{0:T(1024)}, u32[]{:S(2)}) copy-start(s32[1024]{0:T(1024)} %param.21) | copy-start | bytes 12292
  46.0 3.4 %copy-start.4 = (f32[4096]{0:T(1024)S(1)}, f32[4096]{0:T(1024)}, u32[]{:S(2)}) copy-start(f32[4096]{0:T(1024)} %param.18) | copy-start | bytes 49156
  46.0 3.5 %copy-start.3 = (f32[4096]{0:T(1024)S(1)}, f32[4096]{0:T(1024)}, u32[]{:S(2)}) copy-start(f32[4096]{0:T(1024)} %param.17) | copy-start | bytes 49156
  47.7 4.6 %collective-permute-start.3 = (bf16[4,2,128,1024]{3,2,1,0:T(8,128)(2,1)}, bf16[4,2,128,1024]{3,2,1,0:T(8,128)(2,1)}, u32[]{:S(2)}, u32[]{:S(2)}) collective-permute-start(bf16[4,2,128,1024]{3,2,1,0:T(8,128)(2,1)} %get-tuple-element.40), channel_id=1, source_target_pairs={{0,4},{4,0},{8,12},{12,8},{16,20},{20,16},{24,28},{28,24},{32,36},... | collective-permute-start | bytes 6291464 | tf_op jit(solution)/shard_map/ppermute | solution.py:47
  49.0 2.9 %collective-permute-start.4 = (s32[3,128]{1,0:T(4,128)S(1)}, s32[3,128]{1,0:T(4,128)S(1)}, u32[]{:S(2)}, u32[]{:S(2)}) collective-permute-start(s32[3,128]{1,0:T(4,128)S(1)} %get-tuple-element.51), channel_id=1, source_target_pairs={{0,4},{4,0},{8,12},{12,8},{16,20},{20,16},{24,28},{28,24},{32,36},... | collective-permute-start | bytes 4616 | tf_op jit(solution)/shard_map/ppermute | solution.py:47
  57.0 158.9 %copy-start.6 = (f32[256]{0:T(256)}, f32[256]{0:T(256)S(1)}, u32[]{:S(2)}) copy-start(f32[256]{0:T(256)S(1)} %add_rsqrt_fusion) | copy-start | bytes 3076
  133.3 66.6 %collective-permute-start.6 = (bf16[4,2,128,1152]{3,2,1,0:T(8,128)(2,1)}, bf16[4,2,128,1152]{3,2,1,0:T(8,128)(2,1)}, u32[]{:S(2)}, u32[]{:S(2)}) collective-permute-start(bf16[4,2,128,1152]{3,2,1,0:T(8,128)(2,1)} %get-tuple-element.20), channel_id=1, source_target_pairs={{0,4},{4,0},{8,12},{12,8},{16,20},{20,16},{24,28},{28,24},{32,36},... | collective-permute-start | bytes 7077896 | tf_op jit(solution)/shard_map/ppermute | solution.py:47
  134.3 26.0 %collective-permute-start.10 = (bf16[8,256,128]{2,1,0:T(8,128)(2,1)S(1)}, bf16[8,256,128]{2,1,0:T(8,128)(2,1)S(1)}, u32[]{:S(2)}, u32[]{:S(2)}) collective-permute-start(bf16[8,256,128]{2,1,0:T(8,128)(2,1)S(1)} %get-tuple-element.22), channel_id=1, source_target_pairs={{0,8},{4,12},{8,16},{12,20},{16,24},{20,28},{24,0},{28,4},{32,40},... | collective-permute-start | bytes 1572872 | tf_op jit(solution)/shard_map/ppermute | solution.py:43
  134.3 26.0 %collective-permute-start.11 = (bf16[8,256,128]{2,1,0:T(8,128)(2,1)S(1)}, bf16[8,256,128]{2,1,0:T(8,128)(2,1)S(1)}, u32[]{:S(2)}, u32[]{:S(2)}) collective-permute-start(bf16[8,256,128]{2,1,0:T(8,128)(2,1)S(1)} %get-tuple-element.23), channel_id=1, source_target_pairs={{0,24},{4,28},{8,0},{12,4},{16,8},{20,12},{24,16},{28,20},{32,56},... | collective-permute-start | bytes 1572872 | tf_op jit(solution)/shard_map/ppermute | solution.py:43
  137.0 23.3 %collective-permute-start.12 = (bf16[8,256,128]{2,1,0:T(8,128)(2,1)S(1)}, bf16[8,256,128]{2,1,0:T(8,128)(2,1)S(1)}, u32[]{:S(2)}, u32[]{:S(2)}) collective-permute-start(bf16[8,256,128]{2,1,0:T(8,128)(2,1)S(1)} %get-tuple-element.24), channel_id=1, source_target_pairs={{0,16},{4,20},{8,24},{12,28},{16,0},{20,4},{24,8},{28,12},{32,48},... | collective-permute-start | bytes 1572872 | tf_op jit(solution)/shard_map/ppermute | solution.py:43
  195.8 13.3 %all-to-all-start.2 = ((f32[32,8,128]{2,1,0:T(8,128)}), f32[32,8,128]{2,1,0:T(8,128)S(1)}, u32[]{:S(2)}, u32[]{:S(2)}) async-start(f32[32,8,128]{2,1,0:T(8,128)} %broadcast_in_dim.48), calls=%async_computation.2 | async-start | bytes 262144 | tf_op jit(solution)/shard_map/all_to_all | solution.py:360
  202.8 14.5 %collective-permute-start.7 = (bf16[2,128,1152]{2,1,0:T(8,128)(2,1)}, bf16[2,128,1152]{2,1,0:T(8,128)(2,1)}, u32[]{:S(2)}, u32[]{:S(2)}) collective-permute-start(bf16[2,128,1152]{2,1,0:T(8,128)(2,1)} %get-tuple-element.35), channel_id=1, source_target_pairs={{0,1},{1,2},{2,3},{3,0},{4,5},{5,6},{6,7},{7,4},{8,9},{9,10},{10,1... | collective-permute-start | bytes 1769480 | tf_op jit(solution)/shard_map/ppermute | solution.py:51
  204.0 13.3 %collective-permute-start.8 = (bf16[2,128,1152]{2,1,0:T(8,128)(2,1)}, bf16[2,128,1152]{2,1,0:T(8,128)(2,1)}, u32[]{:S(2)}, u32[]{:S(2)}) collective-permute-start(bf16[2,128,1152]{2,1,0:T(8,128)(2,1)} %get-tuple-element.37), channel_id=1, source_target_pairs={{0,3},{1,0},{2,1},{3,2},{4,7},{5,4},{6,5},{7,6},{8,11},{9,8},{10,9... | collective-permute-start | bytes 1769480 | tf_op jit(solution)/shard_map/ppermute | solution.py:51
  205.4 24.3 %collective-permute-start.9 = (bf16[2,128,1152]{2,1,0:T(8,128)(2,1)}, bf16[2,128,1152]{2,1,0:T(8,128)(2,1)}, u32[]{:S(2)}, u32[]{:S(2)}) collective-permute-start(bf16[2,128,1152]{2,1,0:T(8,128)(2,1)} %get-tuple-element.36), channel_id=1, source_target_pairs={{0,2},{1,3},{2,0},{3,1},{4,6},{5,7},{6,4},{7,5},{8,10},{9,11},{10,... | collective-permute-start | bytes 1769480 | tf_op jit(solution)/shard_map/ppermute | solution.py:51
  211.5 5.1 %collective-permute-start.13 = (f32[64,256]{1,0:T(8,128)S(1)}, f32[64,256]{1,0:T(8,128)S(1)}, u32[]{:S(2)}, u32[]{:S(2)}) collective-permute-start(f32[64,256]{1,0:T(8,128)S(1)} %get-tuple-element.47), channel_id=1, source_target_pairs={{0,4},{4,0},{8,12},{12,8},{16,20},{20,16},{24,28},{28,24},{32,36},... | collective-permute-start | bytes 196616 | tf_op jit(solution)/shard_map/ppermute | solution.py:47
  217.3 14.6 %copy-start = (bf16[1024,1024]{1,0:T(8,128)(2,1)S(1)}, bf16[1024,1024]{1,0:T(8,128)(2,1)}, u32[]{:S(2)}) copy-start(bf16[1024,1024]{1,0:T(8,128)(2,1)} %param.11) | copy-start | bytes 6291460
  231.8 2.2 copy-start.2
  231.9 2.2 dynamic-slice-start
  231.9 2.2 dynamic-slice-start.1
  231.9 2.2 slice-start
Sparse Core Ops, SparseCore 0:
  16.0 99.0 all-gather.1

commit v2 on v1

--- a/solution.py
+++ b/solution.py
@@ -19,7 +19,8 @@
 COEF_C = 2.0315
 BF = jnp.bfloat16
 F32 = jnp.float32
-VMEM_LIMIT = 48 * 1024 * 1024
+VMEM_LIMIT = 60 * 1024 * 1024
+SMALL_LIMIT = 16 * 1024 * 1024
 
 
 def dp_index(z, y, c):
@@ -39,6 +40,10 @@
 GROUPS_Z = [[dp_index(z, y, c) for z in range(NZ)] for y in range(NY) for c in range(NC)]
 
 
+def after(value, *others):
+    return lax.optimization_barrier((value,) + others)[0]
+
+
 def move_y(v, k):
     return lax.ppermute(v, "dp", dp_perm(0, k, 0))
 
@@ -67,10 +72,14 @@
     )
 
 
+def chunk_of(step, place):
+    return lax.rem(place[0] + step, NX)
+
+
 def forward_kernel(
     place, normed, d_mix, weight, mask, qkv_out, da_out, attn_out, probs_out, *rest
 ):
-    grads, (qkv_acc, da_acc) = rest[:NY], rest[NY:]
+    grads, (qkv_acc, da_acc, kept) = rest[:NY], rest[NY:]
     step = pl.program_id(0)
 
     @pl.when(step == 0)
@@ -79,8 +88,8 @@
         da_acc[...] = jnp.zeros_like(da_acc)
 
     qkv_acc[...] += dot_nn(normed[0], weight[:, : 6 * HD])
-    x_abs = lax.rem(place[0] + step, NX)
-    da_acc[...] += dot_nn(d_mix[x_abs], weight[:, 6 * HD :])
+    da_acc[...] += dot_nn(d_mix[0], weight[:, 6 * HD :])
+    kept[chunk_of(step, place)] = d_mix[0]
 
     @pl.when(step == NX - 1)
     def _():
@@ -98,26 +107,34 @@
                 probs = expo / jnp.sum(expo, axis=1, keepdims=True)
                 probs_out[s, h] = probs
                 attn_out[rows, pl.ds(h * HD, HD)] = dot_nn(probs.astype(BF), value).astype(BF)
-        attn = attn_out[...]
+        row = lax.broadcasted_iota(jnp.int32, (2 * CAP, 2 * CAP), 0)
+        col = lax.broadcasted_iota(jnp.int32, (2 * CAP, 2 * CAP), 1)
+        eye = jnp.where(row == col, 1.0, 0.0).astype(BF)
+        attn_t = dot_tn(attn_out[...], eye).astype(BF)
         for k in range(NY):
             y_abs = lax.rem(place[1] + k, NY)
             for i in range(NX):
-                for j in range(2):
-                    col = pl.ds(pl.multiple_of(j * 512 + y_abs * 128, 128), 128)
-                    grads[k][2 * i + j] = dot_tn(attn, d_mix[i, :, col]).astype(BF)
+                low = kept[i, :, pl.ds(pl.multiple_of(y_abs * 128, 128), 128)]
+                high = kept[i, :, pl.ds(pl.multiple_of(512 + y_abs * 128, 128), 128)]
+                res = dot_nn(attn_t, jnp.concatenate([low, high], axis=1)).astype(BF)
+                grads[k][2 * i] = res[:, :128]
+                grads[k][2 * i + 1] = res[:, 128:]
 
 
 def forward(place, normed, d_mix, weight, mask):
     whole = lambda *dims: pl.BlockSpec(dims, lambda i, p: (0,) * len(dims))
+    rows = pl.BlockSpec(
+        (1, 2 * CAP, FEAT), lambda i, p: (chunk_of(i, p), 0, 0)
+    )
     return pl.pallas_call(
         forward_kernel,
         grid_spec=pltpu.PrefetchScalarGridSpec(
             num_scalar_prefetch=1,
             grid=(NX,),
             in_specs=[
-                pl.BlockSpec((1, 2 * CAP, FEAT), lambda i, p: (lax.rem(p[0] + i, NX), 0, 0)),
-                whole(NX, 2 * CAP, FEAT),
-                pl.BlockSpec((FEAT, 8 * HD), lambda i, p: (lax.rem(p[0] + i, NX), 0)),
+                rows,
+                rows,
+                pl.BlockSpec((FEAT, 8 * HD), lambda i, p: (chunk_of(i, p), 0)),
                 whole(2 * CAP, CAP),
             ],
             out_specs=[
@@ -130,6 +147,7 @@
             scratch_shapes=[
                 pltpu.VMEM((2 * CAP, 6 * HD), F32),
                 pltpu.VMEM((2 * CAP, 2 * HD), F32),
+                pltpu.VMEM((NX, 2 * CAP, FEAT), BF),
             ],
         ),
         out_shape=[
@@ -138,7 +156,7 @@
             jax.ShapeDtypeStruct((2 * CAP, 2 * HD), BF),
             jax.ShapeDtypeStruct((2, 2, CAP, CAP), F32),
         ]
-        + [jax.ShapeDtypeStruct((NZ, 2 * HD, 128), BF)] * NY,
+        + [pltpu.HBM((NZ, 2 * HD, 128), BF)] * NY,
         compiler_params=pltpu.CompilerParams(vmem_limit_bytes=VMEM_LIMIT),
         cost_estimate=pl.CostEstimate(
             flops=2 * 256 * 4096 * 1280, bytes_accessed=16 << 20, transcendentals=1 << 16
@@ -196,7 +214,7 @@
 def backward(place, qkv, d_attn, attn, probs, weight):
     whole = lambda *dims: pl.BlockSpec(dims, lambda i, p: (0,) * len(dims))
     piece = pl.BlockSpec((1, 2, CAP, FEAT + EXTRA), lambda i, p: (i, 0, 0, 0))
-    piece_type = jax.ShapeDtypeStruct((NX, 2, CAP, FEAT + EXTRA), BF)
+    piece_type = pltpu.HBM((NX, 2, CAP, FEAT + EXTRA), BF)
     return pl.pallas_call(
         backward_kernel,
         grid_spec=pltpu.PrefetchScalarGridSpec(
@@ -224,6 +242,152 @@
     )(place, qkv, d_attn, attn, probs, weight)
 
 
+def stack_kernel(*refs):
+    out = refs[-1]
+    for j, block in enumerate(refs[:-1]):
+        out[j] = block[...]
+
+
+def stack(*blocks):
+    whole = pl.BlockSpec(memory_space=pltpu.VMEM)
+    return pl.pallas_call(
+        stack_kernel,
+        in_specs=[whole] * len(blocks),
+        out_specs=whole,
+        out_shape=jax.ShapeDtypeStruct((len(blocks),) + blocks[0].shape, BF),
+        name="stack",
+    )(*blocks)
+
+
+def prep_kernel(place, mine, other, gain, router, live, normed, d_mix, stats):
+    lane = lax.broadcasted_iota(jnp.int32, (CAP, 128), 1)
+    for s, source in ((0, mine), (1, other)):
+        rows = pl.ds(s * CAP, CAP)
+        square = jnp.zeros((CAP, 1), F32)
+        logit = jnp.zeros((CAP, 1), F32)
+        for k in range(NX):
+            x_abs = lax.rem(place[0] + k, NX)
+            wide = source[k, 0].astype(F32)
+            square += jnp.sum(wide * wide, axis=1, keepdims=True)
+            logit += jnp.sum(wide * router[x_abs], axis=1, keepdims=True)
+        inv = lax.rsqrt(square / D + EPS)
+        gate = jax.nn.sigmoid(logit)
+        stats[rows, :] = jnp.where(lane == 0, gate, inv)
+        gate_live = jnp.where(live[rows, :] > 0.0, gate, 0.0)
+        for k in range(NX):
+            x_abs = lax.rem(place[0] + k, NX)
+            wide = source[k, 0].astype(F32)
+            normed[x_abs, rows, :] = (wide * inv * gain[x_abs]).astype(BF)
+            d_mix[x_abs, rows, :] = (gate_live * source[k, 1].astype(F32)).astype(BF)
+
+
+def prep(place, mine, other, gain, router, live):
+    whole = pl.BlockSpec(memory_space=pltpu.VMEM)
+    return pl.pallas_call(
+        prep_kernel,
+        in_specs=[pl.BlockSpec(memory_space=pltpu.SMEM)] + [whole] * 5,
+        out_specs=[whole] * 3,
+        out_shape=[
+            jax.ShapeDtypeStruct((NX, 2 * CAP, FEAT), BF),
+            jax.ShapeDtypeStruct((NX, 2 * CAP, FEAT), BF),
+            jax.ShapeDtypeStruct((2 * CAP, 128), F32),
+        ],
+        compiler_params=pltpu.CompilerParams(vmem_limit_bytes=24 * 1024 * 1024),
+        name="prep",
+    )(place, mine, other, gain, router, live)
+
+
+def pack_kernel(place, w_query, w_key, w_value, w_out, keep, give):
+    for i, w in enumerate((w_query, w_key, w_value, w_out)):
+        col = pl.ds(i * 2 * HD, 2 * HD)
+        low, high = w[:, : 2 * HD], w[:, 2 * HD :]
+
+        @pl.when(place[2] == 0)
+        def _():
+            keep[:, col] = low
+            give[:, col] = high
+
+        @pl.when(place[2] != 0)
+        def _():
+            keep[:, col] = high
+            give[:, col] = low
+
+
+def pack(place, *weights):
+    whole = pl.BlockSpec(memory_space=pltpu.VMEM)
+    return pl.pallas_call(
+        pack_kernel,
+        in_specs=[pl.BlockSpec(memory_space=pltpu.SMEM)] + [whole] * 4,
+        out_specs=[whole] * 2,
+        out_shape=[jax.ShapeDtypeStruct((64, 8 * HD), BF)] * 2,
+        name="pack",
+    )(place, *weights)
+
+
+def finish_kernel(
+    place, own, got, sent_1, sent_2, sent_3, part, stats, gain, router, slots, tokens,
+    cotangent, block_out, token_grad, updated, d_rows,
+):
+    step = pl.program_id(0)
+
+    @pl.when(step == 0)
+    def _():
+        def summed(kind, cols):
+            total = own[0, kind, :, cols].astype(F32) + got[0, kind, :, cols].astype(F32)
+            for block in (sent_1, sent_2, sent_3):
+                total += block[kind, :, cols].astype(F32)
+            return total
+
+        extra = pl.ds(FEAT, EXTRA)
+        gate, inv = stats[:, :1], stats[:, 1:2]
+        d_logit = summed(0, extra)[:, :1] * (1.0 - gate)
+        stat = summed(1, extra)[:, :1] / D
+        for j in range(0, FEAT, 256):
+            cols = pl.ds(j, 256)
+            rows = part[0, :, cols].astype(F32)
+            updated[:, cols] = (rows + gate * summed(0, cols)).astype(BF)
+            value = summed(1, cols) * gain[0, :, cols] - rows * inv * stat
+            value = part[1, :, cols].astype(F32) + inv * value + d_logit * router[0, :, cols]
+            d_rows[:, cols] = value.astype(BF)
+
+    height = tokens.shape[0]
+    row = lax.broadcasted_iota(jnp.int32, (height, CAP), 0) + step * height
+    hits = jnp.where(row == slots[...], 1.0, 0.0)
+    hit = jnp.sum(hits, axis=1, keepdims=True) > 0.0
+    hits = hits.astype(BF)
+    block_out[...] = jnp.where(hit, dot_nn(hits, updated[...]).astype(BF), tokens[...])
+    token_grad[...] = jnp.where(hit, dot_nn(hits, d_rows[...]).astype(BF), cotangent[...])
+
+
+def finish(place, own, got, sent, part, stats, gain, router, slots, tokens, cotangent):
+    whole = lambda *dims: pl.BlockSpec(dims, lambda i, p: (0,) * len(dims))
+    local = pl.BlockSpec((1, 1, FEAT), lambda i, p: (p[0], 0, 0))
+    rows = tokens.shape[0]
+    tile = pl.BlockSpec((rows // 4, FEAT), lambda i, p: (i, 0))
+    piece = whole(1, 2, CAP, FEAT + EXTRA)
+    return pl.pallas_call(
+        finish_kernel,
+        grid_spec=pltpu.PrefetchScalarGridSpec(
+            num_scalar_prefetch=1,
+            grid=(4,),
+            in_specs=[piece, piece]
+            + [whole(2, CAP, FEAT + EXTRA)] * 3
+            + [whole(2, CAP, FEAT), whole(CAP, 128), local, local, whole(1, CAP), tile, tile],
+            out_specs=[tile, tile],
+            scratch_shapes=[pltpu.VMEM((CAP, FEAT), BF)] * 2,
+        ),
+        out_shape=[
+            pltpu.HBM((rows, FEAT), BF),
+            pltpu.HBM((rows, FEAT), BF),
+        ],
+        compiler_params=pltpu.CompilerParams(vmem_limit_bytes=VMEM_LIMIT),
+        cost_estimate=pl.CostEstimate(
+            flops=4 * rows * FEAT * CAP, bytes_accessed=11 << 20, transcendentals=0
+        ),
+        name="finish",
+    )(place, own, got, *sent, part, stats, gain, router, slots, tokens, cotangent)
+
+
 def high(left, right, dims):
     return lax.dot_general(
         left,
@@ -232,6 +396,27 @@
         precision=lax.Precision.HIGHEST,
         preferred_element_type=F32,
     )
+
+
+def add_kernel(*refs):
+    out = refs[-1]
+    for j in range(out.shape[0]):
+        total = refs[0][j].astype(F32)
+        for block in refs[1:-1]:
+            total = total + block[j].astype(F32)
+        out[j] = total.astype(BF)
+
+
+def add_up(*blocks):
+    whole = pl.BlockSpec(memory_space=pltpu.VMEM)
+    return pl.pallas_call(
+        add_kernel,
+        in_specs=[whole] * len(blocks),
+        out_specs=whole,
+        out_shape=jax.ShapeDtypeStruct(blocks[0].shape, BF),
+        compiler_params=pltpu.CompilerParams(vmem_limit_bytes=SMALL_LIMIT),
+        name="add",
+    )(*blocks)
 
 
 def gram_kernel(parts, total_out, gram_out):
@@ -251,9 +436,25 @@
             jax.ShapeDtypeStruct((2 * HD, 128), F32),
             jax.ShapeDtypeStruct((2, HD, HD), F32),
         ],
-        compiler_params=pltpu.CompilerParams(vmem_limit_bytes=VMEM_LIMIT),
+        compiler_params=pltpu.CompilerParams(vmem_limit_bytes=SMALL_LIMIT),
         name="gram",
     )(parts)
+
+
+def total_kernel(pieces, out):
+    total = pieces[0]
+    for k in range(1, NZ * NY):
+        total = total + pieces[k]
+    for k in range(NZ * NY):
+        out[k] = total
+
+
+def total_of(pieces):
+    return pl.pallas_call(
+        total_kernel,
+        out_shape=jax.ShapeDtypeStruct(pieces.shape, F32),
+        name="total",
+    )(pieces)
 
 
 def muon_kernel(gram_in, total, out):
@@ -278,7 +479,7 @@
     return pl.pallas_call(
         muon_kernel,
         out_shape=jax.ShapeDtypeStruct((128, 2 * HD), F32),
-        compiler_params=pltpu.CompilerParams(vmem_limit_bytes=VMEM_LIMIT),
+        compiler_params=pltpu.CompilerParams(vmem_limit_bytes=SMALL_LIMIT),
         name="muon",
     )(gram, total)
 
@@ -290,13 +491,9 @@
     x = lax.axis_index("mp")
     c = lax.rem(dp, NC)
     y = lax.rem(lax.div(dp, NC), NY)
-    place = jnp.stack([x, y]).astype(jnp.int32)
-
-    stacked = jnp.concatenate(
-        [w.reshape(64, 2, 2 * HD) for w in (w_query, w_key, w_value, w_out.T)], axis=2
-    )
-    keep = lax.dynamic_index_in_dim(stacked, c, 1, keepdims=False)
-    give = lax.dynamic_index_in_dim(stacked, 1 - c, 1, keepdims=False)
+    place = jnp.stack([x, y, c]).astype(jnp.int32)
+
+    keep, give = pack(place, w_query, w_key, w_value, w_out.T)
     take = swap_core(give)
     shard = jnp.where(
         c == 0, jnp.concatenate([keep, take]), jnp.concatenate([take, keep])
@@ -315,19 +512,15 @@
     live = meta[:, 2] > 0
 
     part = jnp.stack([rows_part, grad_part])
-    around = jnp.stack([part] + [move_x(part, k) for k in (3, 2, 1)])
-    both = jnp.stack([around, swap_core(around)], axis=2)
-    both = jnp.roll(both, x, axis=0).reshape(NX, 2, 2 * CAP, FEAT)
-    rows_wide = both[:, 0].astype(F32)
-    grad_wide = both[:, 1].astype(F32)
-    gain_parts = gain.reshape(NX, 1, FEAT)
-    router_parts = w_router.reshape(NX, 1, FEAT)
-    mean_square = jnp.sum(rows_wide * rows_wide, axis=(0, 2)) / D
-    inv_scale = lax.rsqrt(mean_square + EPS)[:, None]
-    gate = jax.nn.sigmoid(jnp.sum(rows_wide * router_parts, axis=(0, 2)))
-    normed = (rows_wide * inv_scale * gain_parts).astype(BF)
-    gate_live = jnp.where(live.reshape(-1), gate, 0.0)[:, None]
-    d_mix = (gate_live * grad_wide).astype(BF)
+    around = stack(part, *[move_x(part, k) for k in (3, 2, 1)])
+    normed, d_mix, stats = prep(
+        place,
+        around,
+        swap_core(around),
+        gain.reshape(NX, 1, FEAT),
+        w_router.reshape(NX, 1, FEAT),
+        live.reshape(2 * CAP, 1).astype(F32),
+    )
     allowed = (
         (position[:, None, :] <= position[:, :, None])
         & (docs[:, None, :] == docs[:, :, None])
@@ -342,22 +535,33 @@
     moved = [move_y(grad_1, 1), move_y(grad_3, 3), move_y(grad_2, 2)]
 
     own, sibling = backward(place, qkv, d_attn, attn, probs, weight)
+    sibling = after(sibling, *moved)
     got = swap_core(sibling)
-    sent = [
-        move_x((own[k].astype(F32) + got[k].astype(F32)).astype(BF), k) for k in (1, 3, 2)
-    ]
-
-    column = grad_0.astype(F32)
-    for m in moved:
-        column = column + m.astype(F32)
-    column = lax.all_to_all(
-        column.astype(BF), "dp", 0, 0, tiled=True, axis_index_groups=GROUPS_Z
-    )
+    sums = [(own[k].astype(F32) + got[k].astype(F32)).astype(BF) for k in (1, 3, 2)]
+
+    column = add_up(grad_0, *moved)
+    sent = [move_x(v, k) for v, k in zip(sums, (1, 3, 2))]
+    column = lax.all_to_all(column, "dp", 0, 0, tiled=True, axis_index_groups=GROUPS_Z)
     total, gram = gram_of(column)
     pieces = gram.reshape(NZ * NY, 8, 128)
     pieces = lax.all_to_all(pieces, "dp", 0, 0, tiled=True, axis_index_groups=GROUPS_ZY)
-    piece = jnp.broadcast_to(jnp.sum(pieces, axis=0)[None], (NZ * NY, 8, 128))
-    gram = lax.all_to_all(piece, "dp", 0, 0, tiled=True, axis_index_groups=GROUPS_ZY)
+    pieces = total_of(pieces)
+    pieces, *sent = lax.optimization_barrier((pieces, *sent))
+    gram = lax.all_to_all(pieces, "dp", 0, 0, tiled=True, axis_index_groups=GROUPS_ZY)
+    block_out, token_grad = finish(
+        place,
+        own,
+        got,
+        sent,
+        part,
+        stats,
+        gain.reshape(NX, 1, FEAT),
+        w_router.reshape(NX, 1, FEAT),
+        jnp.where(live_own, chosen, -1)[None],
+        tokens,
+        cotangent,
+    )
+    gram, block_out, token_grad = lax.optimization_barrier((gram, block_out, token_grad))
     ortho = muon(gram.reshape(2, HD, HD), total).reshape(2, 64, 2 * HD)
     own_cols = lax.dynamic_index_in_dim(ortho, c, 0, keepdims=False)
     other_cols = swap_core(lax.dynamic_index_in_dim(ortho, 1 - c, 0, keepdims=False))
@@ -367,30 +571,6 @@
         jnp.concatenate([other_cols, own_cols], axis=1),
     ).T
 
-    result = own[0].astype(F32) + got[0].astype(F32)
-    for s in sent:
-        result = result + s.astype(F32)
-    mixed, d_normed = result[0, :, :FEAT], result[1, :, :FEAT]
-    gate_sum, stat_sum = result[0, :, FEAT : FEAT + 1], result[1, :, FEAT : FEAT + 1]
-    rows_own = rows_part.astype(F32)
-    gate_own = gate[:CAP, None]
-    inv_own = inv_scale[:CAP]
-    hit = jnp.any(picks & live_own[:, None], axis=0)[:, None]
-    updated = (rows_own + gate_own * mixed).astype(BF)
-
-    def spread(values):
-        return dot_tn(onehot, values).astype(BF)
-
-    block_out = jnp.where(hit, spread(updated), tokens)
-    gain_local = lax.dynamic_slice_in_dim(gain, x * FEAT, FEAT)
-    router_local = lax.dynamic_slice_in_dim(w_router, x * FEAT, FEAT)
-    d_logit = gate_sum * (1.0 - gate_own)
-    d_rows = (
-        grad_part.astype(F32)
-        + inv_own * (d_normed * gain_local - rows_own * inv_own * (stat_sum / D))
-        + d_logit * router_local
-    )
-    token_grad = jnp.where(hit, spread(d_rows.astype(BF)), cotangent)
     return (block_out, token_grad, muon_step)
 
 

time: 246 us -> 224 us (0.911)
  blocking collectives: 34 us -> 0 us
  Pallas kernels: 20.9 us -> 41.5 us
  starting transfers between devices: 22.3 us -> 34 us
  other arithmetic: 15.9 us -> 7.99 us
  waiting for transfers between devices: 123 us -> 116 us
  matrix products: 7.05 us -> 2.59 us
    all_to_all x2 -> x0, blocking collectives: 34 us -> none  [the longest x1 19.7 us: per_device(): lax.all_to_all(column.astype(BF), 'dp', 0, 0, tiled=True, axis_index_grou...]
    all_to_all x1 -> x3, waiting for transfers between devices: 2.15 us -> 21.1 us  [the longest x2 10.6 us: per_device(): lax.all_to_all(pieces, 'dp', 0, 0, tiled=True, axis_index_groups=GROUPS_ZY)]
    pallas_call x0 -> x6, Pallas kernels: none -> 17.3 us  [the longest x1 7.58 us: finish(): pl.pallas_call(finish_kernel, grid_spec=pltpu.PrefetchScalarGridSpec(num_...]
    ppermute x6, waiting for transfers between devices: 38 us -> 25.5 us  [move_x(): return lax.ppermute(v, 'mp', [(i, (i + k) % NX) for i in range(NX)])]
    ppermute x3, waiting for transfers between devices: 23.3 us -> 11.7 us  [move_y(): return lax.ppermute(v, 'dp', dp_perm(0, k, 0))]
    all_to_all x1 -> x3, starting transfers between devices: 4.08 us -> 15.4 us  [the longest x2 11.4 us: per_device(): lax.all_to_all(pieces, 'dp', 0, 0, tiled=True, axis_index_groups=GROUPS_ZY)]
    dot_general x2 -> x0, matrix products: 4.48 us -> none  [dot_tn(): lax.dot_general(left, right, (((0,), (0,)), ((), ())), preferred_element_...]
    unnamed x20 -> x39, local copies, waits for them, and re-layouts: 2.73 us -> 6.39 us
  transfers between devices with their start and end apart: 16 -> 18, of which waited for: 11 -> 12; matrix products, arithmetic and copies ran while one was open for 7% -> 3% of each run, Pallas kernels for 1% -> 12%
where the time goes in v2:
time: 224 us
  waiting for transfers between devices  116 us (52%)
  Pallas kernels  41.5 us (19%)
  starting transfers between devices  34 us (15%)
  between operations  15 us (7%)
  other arithmetic  7.99 us (4%)
  local copies, waits for them, and re-layouts  6.54 us (3%)
  matrix products  2.59 us (1%)
    all_gather x1, waiting for transfers between devices, per_device(): lax.all_gather(shard, 'dp', axis=0, tiled=True, axis_index_groups=GROUPS_ZY)  52.7 us
    ppermute x6, waiting for transfers between devices, move_x(): return lax.ppermute(v, 'mp', [(i, (i + k) % NX) for i in range(NX)])  25.5 us
    ppermute x3, waiting for transfers between devices, move_y(): return lax.ppermute(v, 'dp', dp_perm(0, k, 0))  11.7 us
    all_to_all x2, starting transfers between devices, per_device(): lax.all_to_all(pieces, 'dp', 0, 0, tiled=True, axis_index_groups=GROUPS_ZY)  11.4 us
    pallas_call x1, Pallas kernels, forward(): pl.pallas_call(forward_kernel, grid_spec=pltpu.PrefetchScalarGridSpec(num...  11.1 us
    all_to_all x2, waiting for transfers between devices, per_device(): lax.all_to_all(pieces, 'dp', 0, 0, tiled=True, axis_index_groups=GROUPS_ZY)  10.6 us
    all_to_all x1, waiting for transfers between devices, per_device(): lax.all_to_all(column, 'dp', 0, 0, tiled=True, axis_index_groups=GROUPS_Z)  10.5 us
    ppermute x5, starting transfers between devices, swap_core(): return lax.ppermute(v, 'dp', dp_perm(0, 0, 1))  9.72 us
  transfers between devices with their start and end apart: 18, of which 12 were waited for; matrix products, arithmetic and copies ran while one was open for 3% of the time, Pallas kernels for 12%

profile of v2, /device:TPU:1, one launch (start us, length us, event | category | flops | bytes accessed | tf_op | source)
XLA Modules:
  0.0 223.5 jit_solution(12046921609209286276)
XLA Ops:
  7.2 0.6 pad_add_fusion.3.place
  7.9 1.7 pack.1
  9.6 3.2 %collective-permute-start.5 = (bf16[64,1024]{1,0:T(8,128)(2,1)}, bf16[64,1024]{1,0:T(8,128)(2,1)S(1)}, u32[]{:S(2)}, u32[]{:S(2)}) collective-permute-start(bf16[64,1024]{1,0:T(8,128)(2,1)} %get-tuple-element.33), channel_id=1, source_target_pairs={{0,4},{4,0},{8,12},{12,8},{16,20},{20,16},{24,28},{28,24},{32,36},... | collective-permute-start | bytes 393224 | tf_op jit(solution)/shard_map/ppermute | solution.py:52
  12.8 1.2 collective-permute-done.5
  14.0 1.7 maximum_select_fusion
  15.8 2.1 fusion.1
  18.5 0.8 collective-permute-start
  19.3 0.5 collective-permute-start.1
  19.8 0.6 collective-permute-start.2
  20.4 11.3 %collective-permute-done.refs_1_ = bf16[2,128,1024]{2,1,0:T(8,128)(2,1)S(1)} collective-permute-done((bf16[2,128,1024]{2,1,0:T(8,128)(2,1)S(1)}, bf16[2,128,1024]{2,1,0:T(8,128)(2,1)S(1)}, u32[]{:S(2)}, u32[]{:S(2)}) %collective-permute-start) | collective-permute-done | bytes 524320 | tf_op jit(solution)/shard_map/ppermute | solution.py:56
  31.7 2.0 collective-permute-done.1.refs_2_
  33.7 12.2 %collective-permute-done.2.refs_3_ = bf16[2,128,1024]{2,1,0:T(8,128)(2,1)S(1)} collective-permute-done((bf16[2,128,1024]{2,1,0:T(8,128)(2,1)S(1)}, bf16[2,128,1024]{2,1,0:T(8,128)(2,1)S(1)}, u32[]{:S(2)}, u32[]{:S(2)}) %collective-permute-start.2) | collective-permute-done | bytes 524320 | tf_op jit(solution)/shard_map/ppermute | solution.py:56
  45.9 0.8 copy-done.16
  46.7 3.0 %stack.54.mine = bf16[4,2,128,1024]{3,2,1,0:T(8,128)(2,1)} custom-call(bf16[2,128,1024]{2,1,0:T(8,128)(2,1)} %copy-done.9, bf16[2,128,1024]{2,1,0:T(8,128)(2,1)} %copy-done.14, bf16[2,128,1024]{2,1,0:T(8,128)(2,1)} %copy-done.15, bf16[2,128,1024]{2,1,0:T(8,128)(2,1)} %copy-done.16), custom_call_target="tpu_custom_call" | custom-call | tf_op jit(solution)/shard_map/stack/pallas_call | solution.py:253
  51.2 2.8 %collective-permute-done.4 = s32[3,128]{1,0:T(4,128)S(1)} collective-permute-done((s32[3,128]{1,0:T(4,128)S(1)}, s32[3,128]{1,0:T(4,128)S(1)}, u32[]{:S(2)}, u32[]{:S(2)}) %collective-permute-start.4) | collective-permute-done | bytes 1568 | tf_op jit(solution)/shard_map/ppermute | solution.py:52
  54.2 0.8 fusion.11.mask
  55.0 1.6 copy-done
  56.6 2.4 %prep.1 = (bf16[4,256,1024]{2,1,0:T(8,128)(2,1)S(1)}, bf16[4,256,1024]{2,1,0:T(8,128)(2,1)S(1)}, f32[256,128]{1,0:T(8,128)S(1)}) custom-call(s32[3]{0:T(128)S(1)} %copy-done.7, bf16[4,2,128,1024]{3,2,1,0:T(8,128)(2,1)S(1)} %copy-done, bf16[4,2,128,1024]{3,2,1,0:T(8,128)(2,1)S(1)} %collective-permute-done.3.other, f32[4,1,1024]{2,1,0:T(1,128)S(1)} %bitcast.67, ...), custom_call_target="tpu_custom_call" | custom-call | tf_op jit(solution)/shard_map/prep/pallas_call | solution.py:286
  59.0 1.3 copy-done.1
  60.3 1.3 copy-done.2
  61.6 0.6 copy-done.4
  62.2 52.7 %all-gather.2.cloned.1.call-done.weight = bf16[4096,1024]{1,0:T(8,128)(2,1)} async-done(((bf16[128,1024]{1,0:T(8,128)(2,1)}), bf16[4096,1024]{1,0:T(8,128)(2,1)}) %all-gather.2.cloned.1.call-update) | async-done | bytes 8388624 | tf_op jit(solution)/shard_map/all_gather | solution.py:501
  115.0 11.1 %forward.1 = (bf16[256,768]{1,0:T(8,128)(2,1)}, bf16[256,256]{1,0:T(8,128)(2,1)}, bf16[256,256]{1,0:T(8,128)(2,1)}, f32[2,2,128,128]{3,2,1,0:T(8,128)}, bf16[8,2...) custom-call(s32[3]{0:T(128)} %pad_add_fusion.3.place, ...), custom_call_target="tpu_custom_call" | custom-call | flops 2684354560 | bytes 16777216 | tf_op jit(solution)/shard_map/forward/pallas_call | solution.py:129
  126.1 2.7 %collective-permute-start.7 = (bf16[8,256,128]{2,1,0:T(8,128)(2,1)}, bf16[8,256,128]{2,1,0:T(8,128)(2,1)S(1)}, u32[]{:S(2)}, u32[]{:S(2)}) collective-permute-start(bf16[8,256,128]{2,1,0:T(8,128)(2,1)} %get-tuple-element.36), channel_id=1, source_target_pairs={{0,24},{4,28},{8,0},{12,4},{16,8},{20,12},{24,16},{28,20},{32,56},... | collective-permute-start | bytes 1572872 | tf_op jit(solution)/shard_map/ppermute | solution.py:48
  128.8 9.7 %backward.1 = (bf16[4,2,128,1152]{3,2,1,0:T(8,128)(2,1)}, bf16[4,2,128,1152]{3,2,1,0:T(8,128)(2,1)}) custom-call(s32[3]{0:T(128)} %pad_add_fusion.3.place, bf16[256,768]{1,0:T(8,128)(2,1)} %get-tuple-element.39.qkv, bf16[256,256]{1,0:T(8,128)(2,1)} %get-tuple-element.40.d_attn, bf16[256,256]{1,0:T(8,128)(2,1)} %get-tuple-element.41.attn, ...), custom_call_target="tpu_custom_call" | custom-call | flops 2147483648 | bytes 14680064 | tf_op jit(solution)/shard_map/backward/pallas_call | solution.py:218
  138.5 2.3 %collective-permute-done.6.refs_1_ = bf16[8,256,128]{2,1,0:T(8,128)(2,1)S(1)} collective-permute-done((bf16[8,256,128]{2,1,0:T(8,128)(2,1)}, bf16[8,256,128]{2,1,0:T(8,128)(2,1)S(1)}, u32[]{:S(2)}, u32[]{:S(2)}) %collective-permute-start.6) | collective-permute-done | bytes 524320 | tf_op jit(solution)/shard_map/ppermute | solution.py:48
  140.8 9.4 %collective-permute-done.8.refs_3_ = bf16[8,256,128]{2,1,0:T(8,128)(2,1)S(1)} collective-permute-done((bf16[8,256,128]{2,1,0:T(8,128)(2,1)}, bf16[8,256,128]{2,1,0:T(8,128)(2,1)S(1)}, u32[]{:S(2)}, u32[]{:S(2)}) %collective-permute-start.8) | collective-permute-done | bytes 524320 | tf_op jit(solution)/shard_map/ppermute | solution.py:48
  150.2 2.9 %collective-permute-start.9 = (bf16[4,2,128,1152]{3,2,1,0:T(8,128)(2,1)}, bf16[4,2,128,1152]{3,2,1,0:T(8,128)(2,1)}, u32[]{:S(2)}, u32[]{:S(2)}) collective-permute-start(bf16[4,2,128,1152]{3,2,1,0:T(8,128)(2,1)} %get-tuple-element.45), channel_id=1, source_target_pairs={{0,4},{4,0},{8,12},{12,8},{16,20},{20,16},{24,28},{28,24},{32,36},... | collective-permute-start | bytes 7077896 | tf_op jit(solution)/shard_map/ppermute | solution.py:52
  153.1 1.1 add.54
  154.2 4.1 %all-to-all-start = ((bf16[8,256,128]{2,1,0:T(8,128)(2,1)}), bf16[8,256,128]{2,1,0:T(8,128)(2,1)S(1)}, u32[]{:S(2)}, u32[]{:S(2)}) async-start(bf16[8,256,128]{2,1,0:T(8,128)(2,1)} %add.54), calls=%async_computation | async-start | bytes 1048576 | tf_op jit(solution)/shard_map/all_to_all | solution.py:544
  158.2 3.4 %fusion.4 = (bf16[2,128,1152]{2,1,0:T(8,128)(2,1)S(1)}, bf16[2,128,1152]{2,1,0:T(8,128)(2,1)}, bf16[2,128,1152]{2,1,0:T(8,128)(2,1)}) fusion(bf16[4,2,128,1152]{3,2,1,0:T(8,128)(2,1)} %collective-permute-done.9.got, bf16[4,2,128,1152]{3,2,1,0:T(8,128)(2,1)} %get-tuple-element.43.own), kind=kLoop, calls=%fused_computation.9 | loop fusion | flops 3538944 | bytes 5308416 | tf_op jit(solution)/shard_map/convert_element_type | solution.py:540
  161.6 1.2 collective-permute-start.10
  162.8 1.5 collective-permute-start.11
  164.3 1.5 collective-permute-start.12
  165.8 10.5 %all-to-all-done.parts = bf16[8,256,128]{2,1,0:T(8,128)(2,1)S(1)} async-done(((bf16[8,256,128]{2,1,0:T(8,128)(2,1)}), bf16[8,256,128]{2,1,0:T(8,128)(2,1)S(1)}, u32[]{:S(2)}, u32[]{:S(2)}) %all-to-all-start) | async-done | bytes 524320 | tf_op jit(solution)/shard_map/all_to_all | solution.py:544
  176.3 1.1 gram.1
  177.3 4.3 %all-to-all-start.1 = ((f32[32,8,128]{2,1,0:T(8,128)}), f32[32,8,128]{2,1,0:T(8,128)S(1)}, u32[]{:S(2)}, u32[]{:S(2)}) async-start(f32[32,8,128]{2,1,0:T(8,128)} %bitcast.22), calls=%async_computation.1 | async-start | bytes 262144 | tf_op jit(solution)/shard_map/all_to_all | solution.py:547
  181.7 9.3 %all-to-all-done.1.pieces = f32[32,8,128]{2,1,0:T(8,128)S(1)} async-done(((f32[32,8,128]{2,1,0:T(8,128)}), f32[32,8,128]{2,1,0:T(8,128)S(1)}, u32[]{:S(2)}, u32[]{:S(2)}) %all-to-all-start.1) | async-done | bytes 131104 | tf_op jit(solution)/shard_map/all_to_all | solution.py:547
  191.0 0.7 copy-done.13
  191.7 1.6 total.1
  193.3 7.0 %all-to-all-start.2 = ((f32[32,8,128]{2,1,0:T(8,128)}), f32[32,8,128]{2,1,0:T(8,128)S(1)}, u32[]{:S(2)}, u32[]{:S(2)}) async-start(f32[32,8,128]{2,1,0:T(8,128)} %total.1), calls=%async_computation.2 | async-start | bytes 262144 | tf_op jit(solution)/shard_map/all_to_all | solution.py:550
  200.3 0.5 fusion.12.slots
  200.9 7.6 %finish.1 = (bf16[1024,1024]{1,0:T(8,128)(2,1)}, bf16[1024,1024]{1,0:T(8,128)(2,1)}) custom-call(s32[3]{0:T(128)} %pad_add_fusion.3.place, bf16[4,2,128,1152]{3,2,1,0:T(8,128)(2,1)} %get-tuple-element.43.own, bf16[4,2,128,1152]{3,2,1,0:T(8,128)(2,1)} %collective-permute-done.9.got, bf16[2,128,1152]{2,1,0:T(8,128)(2,1)} %copy-done.10, ...), custom_call_target="tpu_custom_call" | custom-call | flops 536870912 | bytes 11534336 | tf_op jit(solution)/shard_map/finish/pallas_call | solution.py:368
  208.4 1.2 all-to-all-done.2
  209.7 2.4 %muon.1 = f32[128,256]{1,0:T(8,128)S(1)} custom-call(f32[2,128,128]{2,1,0:T(8,128)S(1)} %bitcast.64, f32[256,128]{1,0:T(8,128)S(1)} %get-tuple-element.56.total), custom_call_target="tpu_custom_call" | custom-call | tf_op jit(solution)/shard_map/muon/pallas_call | solution.py:479
  212.1 3.0 %collective-permute-start.13 = (f32[64,256]{1,0:T(8,128)S(1)}, f32[64,256]{1,0:T(8,128)S(1)}, u32[]{:S(2)}, u32[]{:S(2)}) collective-permute-start(f32[64,256]{1,0:T(8,128)S(1)} %get-tuple-element.63), channel_id=1, source_target_pairs={{0,4},{4,0},{8,12},{12,8},{16,20},{20,16},{24,28},{28,24},{32,36},... | collective-permute-start | bytes 196616 | tf_op jit(solution)/shard_map/ppermute | solution.py:52
  215.1 0.9 collective-permute-done.13
  216.0 0.7 fusion.7
  (55 shorter events, 1.7 us)
Async XLA Ops:
  7.2 10.7 %copy-start.17 = (s32[128]{0:T(128)S(1)}, s32[128]{0:T(128)}, u32[]{:S(2)}) copy-start(s32[128]{0:T(128)} %param.19) | copy-start | bytes 1540
  7.2 10.7 %copy-start.8 = (bf16[1024,1024]{1,0:T(8,128)(2,1)S(1)}, bf16[1024,1024]{1,0:T(8,128)(2,1)}, u32[]{:S(2)}) copy-start(bf16[1024,1024]{1,0:T(8,128)(2,1)} %tokens.1) | copy-start | bytes 6291460
  7.2 107.8 %all-gather.2.cloned.1.call-start = ((), (), s32[]{:S(2)}) async-start(), calls=%async_computation.3 | async-start | bytes 8650752 | tf_op jit(solution)/shard_map/all_gather | solution.py:501
  9.6 4.4 %collective-permute-start.5 = (bf16[64,1024]{1,0:T(8,128)(2,1)}, bf16[64,1024]{1,0:T(8,128)(2,1)S(1)}, u32[]{:S(2)}, u32[]{:S(2)}) collective-permute-start(bf16[64,1024]{1,0:T(8,128)(2,1)} %get-tuple-element.33), channel_id=1, source_target_pairs={{0,4},{4,0},{8,12},{12,8},{16,20},{20,16},{24,28},{28,24},{32,36},... | collective-permute-start | bytes 393224 | tf_op jit(solution)/shard_map/ppermute | solution.py:52
  18.4 27.5 %copy-start.9 = (bf16[2,128,1024]{2,1,0:T(8,128)(2,1)}, bf16[2,128,1024]{2,1,0:T(8,128)(2,1)S(1)}, u32[]{:S(2)}) copy-start(bf16[2,128,1024]{2,1,0:T(8,128)(2,1)S(1)} %pad_maximum_fusion.refs_0_.part) | copy-start | bytes 1572868
  18.5 32.4 %copy-start.18 = (s32[1024]{0:T(1024)S(1)}, s32[1024]{0:T(1024)}, u32[]{:S(2)}) copy-start(s32[1024]{0:T(1024)} %param.21) | copy-start | bytes 12292
  18.5 36.5 %copy-start.5 = (f32[4096]{0:T(1024)S(1)}, f32[4096]{0:T(1024)}, u32[]{:S(2)}) copy-start(f32[4096]{0:T(1024)} %param.17) | copy-start | bytes 49156
  18.5 36.5 %copy-start.6 = (f32[4096]{0:T(1024)S(1)}, f32[4096]{0:T(1024)}, u32[]{:S(2)}) copy-start(f32[4096]{0:T(1024)} %param.18) | copy-start | bytes 49156
  18.5 36.5 %copy-start.7 = (s32[3]{0:T(128)S(1)}, s32[3]{0:T(128)}, u32[]{:S(2)}) copy-start(s32[3]{0:T(128)} %pad_add_fusion.3.place) | copy-start | bytes 40
  18.5 13.2 %collective-permute-start = (bf16[2,128,1024]{2,1,0:T(8,128)(2,1)S(1)}, bf16[2,128,1024]{2,1,0:T(8,128)(2,1)S(1)}, u32[]{:S(2)}, u32[]{:S(2)}) collective-permute-start(bf16[2,128,1024]{2,1,0:T(8,128)(2,1)S(1)} %pad_maximum_fusion.refs_0_.part), channel_id=1, source_target_pairs={{0,3},{1,0},{2,1},{3,2},{4,7},{5,4},{6,5},{7,6},{8,11},{9,8},{10,9... | collective-permute-start | bytes 1572872 | tf_op jit(solution)/shard_map/ppermute | solution.py:56
  19.3 14.4 %collective-permute-start.1 = (bf16[2,128,1024]{2,1,0:T(8,128)(2,1)S(1)}, bf16[2,128,1024]{2,1,0:T(8,128)(2,1)S(1)}, u32[]{:S(2)}, u32[]{:S(2)}) collective-permute-start(bf16[2,128,1024]{2,1,0:T(8,128)(2,1)S(1)} %pad_maximum_fusion.refs_0_.part), channel_id=1, source_target_pairs={{0,2},{1,3},{2,0},{3,1},{4,6},{5,7},{6,4},{7,5},{8,10},{9,11},{10,... | collective-permute-start | bytes 1572872 | tf_op jit(solution)/shard_map/ppermute | solution.py:56
  19.8 26.1 %collective-permute-start.2 = (bf16[2,128,1024]{2,1,0:T(8,128)(2,1)S(1)}, bf16[2,128,1024]{2,1,0:T(8,128)(2,1)S(1)}, u32[]{:S(2)}, u32[]{:S(2)}) collective-permute-start(bf16[2,128,1024]{2,1,0:T(8,128)(2,1)S(1)} %pad_maximum_fusion.refs_0_.part), channel_id=1, source_target_pairs={{0,1},{1,2},{2,3},{3,0},{4,5},{5,6},{6,7},{7,4},{8,9},{9,10},{10,1... | collective-permute-start | bytes 1572872 | tf_op jit(solution)/shard_map/ppermute | solution.py:56
  31.7 14.2 %copy-start.14 = (bf16[2,128,1024]{2,1,0:T(8,128)(2,1)}, bf16[2,128,1024]{2,1,0:T(8,128)(2,1)S(1)}, u32[]{:S(2)}) copy-start(bf16[2,128,1024]{2,1,0:T(8,128)(2,1)S(1)} %collective-permute-done.refs_1_) | copy-start | bytes 1572868
  33.7 12.2 %copy-start.15 = (bf16[2,128,1024]{2,1,0:T(8,128)(2,1)}, bf16[2,128,1024]{2,1,0:T(8,128)(2,1)S(1)}, u32[]{:S(2)}) copy-start(bf16[2,128,1024]{2,1,0:T(8,128)(2,1)S(1)} %collective-permute-done.1.refs_2_) | copy-start | bytes 1572868
  45.9 0.8 copy-start.16
  49.7 5.3 %collective-permute-start.3 = (bf16[4,2,128,1024]{3,2,1,0:T(8,128)(2,1)}, bf16[4,2,128,1024]{3,2,1,0:T(8,128)(2,1)S(1)}, u32[]{:S(2)}, u32[]{:S(2)}) collective-permute-start(bf16[4,2,128,1024]{3,2,1,0:T(8,128)(2,1)} %stack.54.mine), channel_id=1, source_target_pairs={{0,4},{4,0},{8,12},{12,8},{16,20},{20,16},{24,28},{28,24},{32,36},... | collective-permute-start | bytes 6291464 | tf_op jit(solution)/shard_map/ppermute | solution.py:52
  51.1 2.9 %collective-permute-start.4 = (s32[3,128]{1,0:T(4,128)S(1)}, s32[3,128]{1,0:T(4,128)S(1)}, u32[]{:S(2)}, u32[]{:S(2)}) collective-permute-start(s32[3,128]{1,0:T(4,128)S(1)} %get-tuple-element.67), channel_id=1, source_target_pairs={{0,4},{4,0},{8,12},{12,8},{16,20},{20,16},{24,28},{28,24},{32,36},... | collective-permute-start | bytes 4616 | tf_op jit(solution)/shard_map/ppermute | solution.py:52
  55.0 1.6 copy-start
  59.0 1.3 copy-start.1
  60.3 1.3 copy-start.2
  61.6 0.6 copy-start.4
  126.1 14.7 %collective-permute-start.6 = (bf16[8,256,128]{2,1,0:T(8,128)(2,1)}, bf16[8,256,128]{2,1,0:T(8,128)(2,1)S(1)}, u32[]{:S(2)}, u32[]{:S(2)}) collective-permute-start(bf16[8,256,128]{2,1,0:T(8,128)(2,1)} %get-tuple-element.35), channel_id=1, source_target_pairs={{0,8},{4,12},{8,16},{12,20},{16,24},{20,28},{24,0},{28,4},{32,40},... | collective-permute-start | bytes 1572872 | tf_op jit(solution)/shard_map/ppermute | solution.py:48
  126.1 14.7 %collective-permute-start.7 = (bf16[8,256,128]{2,1,0:T(8,128)(2,1)}, bf16[8,256,128]{2,1,0:T(8,128)(2,1)S(1)}, u32[]{:S(2)}, u32[]{:S(2)}) collective-permute-start(bf16[8,256,128]{2,1,0:T(8,128)(2,1)} %get-tuple-element.36), channel_id=1, source_target_pairs={{0,24},{4,28},{8,0},{12,4},{16,8},{20,12},{24,16},{28,20},{32,56},... | collective-permute-start | bytes 1572872 | tf_op jit(solution)/shard_map/ppermute | solution.py:48
  128.8 21.4 %collective-permute-start.8 = (bf16[8,256,128]{2,1,0:T(8,128)(2,1)}, bf16[8,256,128]{2,1,0:T(8,128)(2,1)S(1)}, u32[]{:S(2)}, u32[]{:S(2)}) collective-permute-start(bf16[8,256,128]{2,1,0:T(8,128)(2,1)} %get-tuple-element.37), channel_id=1, source_target_pairs={{0,16},{4,20},{8,24},{12,28},{16,0},{20,4},{24,8},{28,12},{32,48},... | collective-permute-start | bytes 1572872 | tf_op jit(solution)/shard_map/ppermute | solution.py:48
  128.8 24.3 %copy-start.3 = (bf16[8,256,128]{2,1,0:T(8,128)(2,1)S(1)}, bf16[8,256,128]{2,1,0:T(8,128)(2,1)}, u32[]{:S(2)}) copy-start(bf16[8,256,128]{2,1,0:T(8,128)(2,1)} %get-tuple-element.34.refs_0_) | copy-start | bytes 1572868
  150.2 8.0 %collective-permute-start.9 = (bf16[4,2,128,1152]{3,2,1,0:T(8,128)(2,1)}, bf16[4,2,128,1152]{3,2,1,0:T(8,128)(2,1)}, u32[]{:S(2)}, u32[]{:S(2)}) collective-permute-start(bf16[4,2,128,1152]{3,2,1,0:T(8,128)(2,1)} %get-tuple-element.45), channel_id=1, source_target_pairs={{0,4},{4,0},{8,12},{12,8},{16,20},{20,16},{24,28},{28,24},{32,36},... | collective-permute-start | bytes 7077896 | tf_op jit(solution)/shard_map/ppermute | solution.py:52
  154.2 22.1 %all-to-all-start = ((bf16[8,256,128]{2,1,0:T(8,128)(2,1)}), bf16[8,256,128]{2,1,0:T(8,128)(2,1)S(1)}, u32[]{:S(2)}, u32[]{:S(2)}) async-start(bf16[8,256,128]{2,1,0:T(8,128)(2,1)} %add.54), calls=%async_computation | async-start | bytes 1048576 | tf_op jit(solution)/shard_map/all_to_all | solution.py:544
  161.6 31.7 %collective-permute-start.10 = (bf16[2,128,1152]{2,1,0:T(8,128)(2,1)}, bf16[2,128,1152]{2,1,0:T(8,128)(2,1)S(1)}, u32[]{:S(2)}, u32[]{:S(2)}) collective-permute-start(bf16[2,128,1152]{2,1,0:T(8,128)(2,1)} %get-tuple-element.61), channel_id=1, source_target_pairs={{0,1},{1,2},{2,3},{3,0},{4,5},{5,6},{6,7},{7,4},{8,9},{9,10},{10,1... | collective-permute-start | bytes 1769480 | tf_op jit(solution)/shard_map/ppermute | solution.py:56
  162.8 30.5 %collective-permute-start.11 = (bf16[2,128,1152]{2,1,0:T(8,128)(2,1)}, bf16[2,128,1152]{2,1,0:T(8,128)(2,1)S(1)}, u32[]{:S(2)}, u32[]{:S(2)}) collective-permute-start(bf16[2,128,1152]{2,1,0:T(8,128)(2,1)} %get-tuple-element.60), channel_id=1, source_target_pairs={{0,3},{1,0},{2,1},{3,2},{4,7},{5,4},{6,5},{7,6},{8,11},{9,8},{10,9... | collective-permute-start | bytes 1769480 | tf_op jit(solution)/shard_map/ppermute | solution.py:56
  164.3 29.0 %collective-permute-start.12 = (bf16[2,128,1152]{2,1,0:T(8,128)(2,1)S(1)}, bf16[2,128,1152]{2,1,0:T(8,128)(2,1)S(1)}, u32[]{:S(2)}, u32[]{:S(2)}) collective-permute-start(bf16[2,128,1152]{2,1,0:T(8,128)(2,1)S(1)} %get-tuple-element.59), channel_id=1, source_target_pairs={{0,2},{1,3},{2,0},{3,1},{4,6},{5,7},{6,4},{7,5},{8,10},{9,11},{10,... | collective-permute-start | bytes 1769480 | tf_op jit(solution)/shard_map/ppermute | solution.py:56
  177.3 13.7 %all-to-all-start.1 = ((f32[32,8,128]{2,1,0:T(8,128)}), f32[32,8,128]{2,1,0:T(8,128)S(1)}, u32[]{:S(2)}, u32[]{:S(2)}) async-start(f32[32,8,128]{2,1,0:T(8,128)} %bitcast.22), calls=%async_computation.1 | async-start | bytes 262144 | tf_op jit(solution)/shard_map/all_to_all | solution.py:547
  191.0 0.7 copy-start.13
  193.3 7.6 %copy-start.10 = (bf16[2,128,1152]{2,1,0:T(8,128)(2,1)}, bf16[2,128,1152]{2,1,0:T(8,128)(2,1)S(1)}, u32[]{:S(2)}) copy-start(bf16[2,128,1152]{2,1,0:T(8,128)(2,1)S(1)} %collective-permute-done.10.sent_1) | copy-start | bytes 1769476
  193.3 7.6 %copy-start.11 = (bf16[2,128,1152]{2,1,0:T(8,128)(2,1)}, bf16[2,128,1152]{2,1,0:T(8,128)(2,1)S(1)}, u32[]{:S(2)}) copy-start(bf16[2,128,1152]{2,1,0:T(8,128)(2,1)S(1)} %collective-permute-done.11.sent_2) | copy-start | bytes 1769476
  193.3 7.5 %copy-start.12 = (bf16[2,128,1152]{2,1,0:T(8,128)(2,1)}, bf16[2,128,1152]{2,1,0:T(8,128)(2,1)S(1)}, u32[]{:S(2)}) copy-start(bf16[2,128,1152]{2,1,0:T(8,128)(2,1)S(1)} %collective-permute-done.12.sent_3) | copy-start | bytes 1769476
  193.3 16.4 %all-to-all-start.2 = ((f32[32,8,128]{2,1,0:T(8,128)}), f32[32,8,128]{2,1,0:T(8,128)S(1)}, u32[]{:S(2)}, u32[]{:S(2)}) async-start(f32[32,8,128]{2,1,0:T(8,128)} %total.1), calls=%async_computation.2 | async-start | bytes 262144 | tf_op jit(solution)/shard_map/all_to_all | solution.py:550
  212.1 3.9 %collective-permute-start.13 = (f32[64,256]{1,0:T(8,128)S(1)}, f32[64,256]{1,0:T(8,128)S(1)}, u32[]{:S(2)}, u32[]{:S(2)}) collective-permute-start(f32[64,256]{1,0:T(8,128)S(1)} %get-tuple-element.63), channel_id=1, source_target_pairs={{0,4},{4,0},{8,12},{12,8},{16,20},{20,16},{24,28},{28,24},{32,36},... | collective-permute-start | bytes 196616 | tf_op jit(solution)/shard_map/ppermute | solution.py:52
Sparse Core Ops, SparseCore 0:
  15.9 99.0 all-gather.1

commit v3 on v2

--- a/solution.py
+++ b/solution.py
@@ -77,99 +77,112 @@
 
 
 def forward_kernel(
-    place, normed, d_mix, weight, mask, qkv_out, da_out, attn_out, probs_out, *rest
+    place, normed, d_mix, weight, mask, qkv_out, attn_out, probs_out, *rest
 ):
-    grads, (qkv_acc, da_acc, kept) = rest[:NY], rest[NY:]
-    step = pl.program_id(0)
-
-    @pl.when(step == 0)
-    def _():
-        qkv_acc[...] = jnp.zeros_like(qkv_acc)
-        da_acc[...] = jnp.zeros_like(da_acc)
-
-    qkv_acc[...] += dot_nn(normed[0], weight[:, : 6 * HD])
-    da_acc[...] += dot_nn(d_mix[0], weight[:, 6 * HD :])
-    kept[chunk_of(step, place)] = d_mix[0]
-
-    @pl.when(step == NX - 1)
-    def _():
-        qkv_out[...] = qkv_acc[...].astype(BF)
-        da_out[...] = da_acc[...].astype(BF)
-        for s in range(2):
-            rows = pl.ds(s * CAP, CAP)
-            for h in range(2):
-                query = qkv_out[rows, pl.ds(h * HD, HD)]
-                key = qkv_out[rows, pl.ds((2 + h) * HD, HD)]
-                value = qkv_out[rows, pl.ds((4 + h) * HD, HD)]
-                scores = dot_nt(query, key) * HD ** (-0.5)
-                scores = jnp.where(mask[rows, :] > 0.0, scores, -1e30)
-                expo = jnp.exp(scores - jnp.max(scores, axis=1, keepdims=True))
-                probs = expo / jnp.sum(expo, axis=1, keepdims=True)
-                probs_out[s, h] = probs
-                attn_out[rows, pl.ds(h * HD, HD)] = dot_nn(probs.astype(BF), value).astype(BF)
-        row = lax.broadcasted_iota(jnp.int32, (2 * CAP, 2 * CAP), 0)
-        col = lax.broadcasted_iota(jnp.int32, (2 * CAP, 2 * CAP), 1)
-        eye = jnp.where(row == col, 1.0, 0.0).astype(BF)
-        attn_t = dot_tn(attn_out[...], eye).astype(BF)
-        for k in range(NY):
-            y_abs = lax.rem(place[1] + k, NY)
-            for i in range(NX):
-                low = kept[i, :, pl.ds(pl.multiple_of(y_abs * 128, 128), 128)]
-                high = kept[i, :, pl.ds(pl.multiple_of(512 + y_abs * 128, 128), 128)]
-                res = dot_nn(attn_t, jnp.concatenate([low, high], axis=1)).astype(BF)
-                grads[k][2 * i] = res[:, :128]
-                grads[k][2 * i + 1] = res[:, 128:]
+    grads, (rows_v, mix_v, weight_v, qkv_acc, held, in_sems, out_sems) = rest[:NY], rest[NY:]
+    x, y = place[0], place[1]
+    cols = pl.ds(pl.multiple_of(place[2] * 6 * HD, 6 * HD), 6 * HD)
+
+    def copies(k):
+        chunk = chunk_of(k, place)
+        rows = pl.ds(pl.multiple_of(chunk * FEAT, FEAT), FEAT)
+        return (
+            pltpu.make_async_copy(weight.at[rows, cols], weight_v.at[k], in_sems.at[0, k]),
+            pltpu.make_async_copy(normed.at[chunk], rows_v.at[k], in_sems.at[1, k]),
+            pltpu.make_async_copy(d_mix.at[chunk], mix_v.at[k], in_sems.at[2, k]),
+        )
+
+    fetch = [copies(k) for k in range(NX)]
+    for k in range(NX):
+        fetch[k][0].start()
+        fetch[k][1].start()
+    for k in range(NX):
+        fetch[k][2].start()
+    for k in range(NX):
+        fetch[k][0].wait()
+        fetch[k][1].wait()
+        part = dot_nn(rows_v[k], weight_v[k])
+        if k == 0:
+            qkv_acc[...] = part
+        else:
+            qkv_acc[...] += part
+
+    qkv_out[...] = qkv_acc[...].astype(BF)
+    for s in range(2):
+        rows = pl.ds(s * CAP, CAP)
+        for h in range(2):
+            query = qkv_out[rows, pl.ds(h * HD, HD)]
+            key = qkv_out[rows, pl.ds((2 + h) * HD, HD)]
+            value = qkv_out[rows, pl.ds((4 + h) * HD, HD)]
+            scores = dot_nt(query, key) * HD ** (-0.5)
+            scores = jnp.where(mask[rows, :] > 0.0, scores, -1e30)
+            expo = jnp.exp(scores - jnp.max(scores, axis=1, keepdims=True))
+            probs = expo / jnp.sum(expo, axis=1, keepdims=True)
+            probs_out[s, h] = probs
+            attn_out[rows, pl.ds(h * HD, HD)] = dot_nn(probs.astype(BF), value).astype(BF)
+    row = lax.broadcasted_iota(jnp.int32, (2 * CAP, 2 * CAP), 0)
+    col = lax.broadcasted_iota(jnp.int32, (2 * CAP, 2 * CAP), 1)
+    eye = jnp.where(row == col, 1.0, 0.0).astype(BF)
+    attn_t = dot_tn(attn_out[...], eye).astype(BF)
+    for k in range(NX):
+        fetch[k][2].wait()
+    sends = [pltpu.make_async_copy(held.at[k], grads[k], out_sems.at[k]) for k in range(NY)]
+    for k in (2, 1, 3, 0):
+        y_abs = lax.rem(y + k, NY)
+        for i in range(NX):
+            low = mix_v[i, :, pl.ds(pl.multiple_of(y_abs * 128, 128), 128)]
+            high = mix_v[i, :, pl.ds(pl.multiple_of(512 + y_abs * 128, 128), 128)]
+            res = dot_nn(attn_t, jnp.concatenate([low, high], axis=1)).astype(BF)
+            x_abs = lax.rem(x + i, NX)
+            held[k, 2 * x_abs] = res[:, :128]
+            held[k, 2 * x_abs + 1] = res[:, 128:]
+        sends[k].start()
+    for k in range(NY):
+        sends[k].wait()
 
 
 def forward(place, normed, d_mix, weight, mask):
-    whole = lambda *dims: pl.BlockSpec(dims, lambda i, p: (0,) * len(dims))
-    rows = pl.BlockSpec(
-        (1, 2 * CAP, FEAT), lambda i, p: (chunk_of(i, p), 0, 0)
-    )
+    whole = pl.BlockSpec(memory_space=pltpu.VMEM)
+    outside = pl.BlockSpec(memory_space=pl.ANY)
     return pl.pallas_call(
         forward_kernel,
-        grid_spec=pltpu.PrefetchScalarGridSpec(
-            num_scalar_prefetch=1,
-            grid=(NX,),
-            in_specs=[
-                rows,
-                rows,
-                pl.BlockSpec((FEAT, 8 * HD), lambda i, p: (chunk_of(i, p), 0)),
-                whole(2 * CAP, CAP),
-            ],
-            out_specs=[
-                whole(2 * CAP, 6 * HD),
-                whole(2 * CAP, 2 * HD),
-                whole(2 * CAP, 2 * HD),
-                whole(2, 2, CAP, CAP),
-            ]
-            + [whole(NZ, 2 * HD, 128)] * NY,
-            scratch_shapes=[
-                pltpu.VMEM((2 * CAP, 6 * HD), F32),
-                pltpu.VMEM((2 * CAP, 2 * HD), F32),
-                pltpu.VMEM((NX, 2 * CAP, FEAT), BF),
-            ],
-        ),
+        in_specs=[pl.BlockSpec(memory_space=pltpu.SMEM)] + [outside] * 3 + [whole],
+        out_specs=[whole] * 3 + [outside] * NY,
+        scratch_shapes=[
+            pltpu.VMEM((NX, 2 * CAP, FEAT), BF),
+            pltpu.VMEM((NX, 2 * CAP, FEAT), BF),
+            pltpu.VMEM((NX, FEAT, 6 * HD), BF),
+            pltpu.VMEM((2 * CAP, 6 * HD), F32),
+            pltpu.VMEM((NY, NZ, 2 * HD, 128), BF),
+            pltpu.SemaphoreType.DMA((3, NX)),
+            pltpu.SemaphoreType.DMA((NY,)),
+        ],
         out_shape=[
             jax.ShapeDtypeStruct((2 * CAP, 6 * HD), BF),
-            jax.ShapeDtypeStruct((2 * CAP, 2 * HD), BF),
             jax.ShapeDtypeStruct((2 * CAP, 2 * HD), BF),
             jax.ShapeDtypeStruct((2, 2, CAP, CAP), F32),
         ]
         + [pltpu.HBM((NZ, 2 * HD, 128), BF)] * NY,
         compiler_params=pltpu.CompilerParams(vmem_limit_bytes=VMEM_LIMIT),
         cost_estimate=pl.CostEstimate(
-            flops=2 * 256 * 4096 * 1280, bytes_accessed=16 << 20, transcendentals=1 << 16
+            flops=2 * 256 * 4096 * 1024, bytes_accessed=13 << 20, transcendentals=1 << 16
         ),
         name="forward",
     )(place, normed, d_mix, weight, mask)
 
 
-def backward_kernel(place, qkv, d_attn, attn, probs_in, weight, own_out, sib_out, d_qkv, sums):
+def backward_kernel(
+    place, qkv, d_mix, out_all, attn, probs_in, weight, out_weight,
+    own_out, sib_out, d_qkv, sums, d_attn,
+):
     step = pl.program_id(0)
 
     @pl.when(step == 0)
     def _():
+        total = dot_nn(d_mix[0], out_all[:FEAT])
+        for i in range(1, NX):
+            total += dot_nn(d_mix[i], out_all[i * FEAT : (i + 1) * FEAT])
+        d_attn[...] = total.astype(BF)
         lane = lax.broadcasted_iota(jnp.int32, (CAP, EXTRA), 1)
         for s in range(2):
             rows = pl.ds(s * CAP, CAP)
@@ -202,8 +215,8 @@
             sums[s, 0] = jnp.where(lane == 0, gate_sum, 0.0).astype(BF)
             sums[s, 1] = jnp.where(lane == 0, stat_sum, 0.0).astype(BF)
 
-    mixed = dot_nt(attn[...], weight[:, 6 * HD :]).astype(BF)
-    d_normed = dot_nt(d_qkv[...], weight[:, : 6 * HD]).astype(BF)
+    mixed = dot_nt(attn[...], out_weight[...]).astype(BF)
+    d_normed = dot_nt(d_qkv[...], weight[...]).astype(BF)
     for s, out in ((0, own_out), (1, sib_out)):
         out[0, 0, :, :FEAT] = mixed[s * CAP : (s + 1) * CAP]
         out[0, 1, :, :FEAT] = d_normed[s * CAP : (s + 1) * CAP]
@@ -211,7 +224,7 @@
         out[0, 1, :, FEAT:] = sums[s, 1]
 
 
-def backward(place, qkv, d_attn, attn, probs, weight):
+def backward(place, qkv, d_mix, attn, probs, weight):
     whole = lambda *dims: pl.BlockSpec(dims, lambda i, p: (0,) * len(dims))
     piece = pl.BlockSpec((1, 2, CAP, FEAT + EXTRA), lambda i, p: (i, 0, 0, 0))
     piece_type = pltpu.HBM((NX, 2, CAP, FEAT + EXTRA), BF)
@@ -222,15 +235,18 @@
             grid=(NX,),
             in_specs=[
                 whole(2 * CAP, 6 * HD),
-                whole(2 * CAP, 2 * HD),
+                whole(NX, 2 * CAP, FEAT),
+                pl.BlockSpec((D, 2 * HD), lambda i, p: (0, 6 + p[2])),
                 whole(2 * CAP, 2 * HD),
                 whole(2, 2, CAP, CAP),
-                pl.BlockSpec((FEAT, 8 * HD), lambda i, p: (lax.rem(p[0] + i, NX), 0)),
+                pl.BlockSpec((FEAT, 6 * HD), lambda i, p: (chunk_of(i, p), p[2])),
+                pl.BlockSpec((FEAT, 2 * HD), lambda i, p: (chunk_of(i, p), 6 + p[2])),
             ],
             out_specs=[piece, piece],
             scratch_shapes=[
                 pltpu.VMEM((2 * CAP, 6 * HD), BF),
                 pltpu.VMEM((2, 2, CAP, EXTRA), BF),
+                pltpu.VMEM((2 * CAP, 2 * HD), BF),
             ],
         ),
         out_shape=[piece_type, piece_type],
@@ -239,7 +255,7 @@
             flops=2 * 256 * 4096 * 1024, bytes_accessed=14 << 20, transcendentals=0
         ),
         name="backward",
-    )(place, qkv, d_attn, attn, probs, weight)
+    )(place, qkv, d_mix, weight, attn, probs, weight, weight)
 
 
 def stack_kernel(*refs):
@@ -297,31 +313,23 @@
     )(place, mine, other, gain, router, live)
 
 
-def pack_kernel(place, w_query, w_key, w_value, w_out, keep, give):
-    for i, w in enumerate((w_query, w_key, w_value, w_out)):
-        col = pl.ds(i * 2 * HD, 2 * HD)
-        low, high = w[:, : 2 * HD], w[:, 2 * HD :]
-
-        @pl.when(place[2] == 0)
-        def _():
-            keep[:, col] = low
-            give[:, col] = high
-
-        @pl.when(place[2] != 0)
-        def _():
-            keep[:, col] = high
-            give[:, col] = low
-
-
-def pack(place, *weights):
+def pack_kernel(w_query, w_key, w_value, w_out, out):
+    for core in range(NC):
+        cols = pl.ds(core * 2 * HD, 2 * HD)
+        for i, w in enumerate((w_query, w_key, w_value)):
+            out[:, pl.ds((3 * core + i) * 2 * HD, 2 * HD)] = w[:, cols]
+        out[:, pl.ds((6 + core) * 2 * HD, 2 * HD)] = w_out[:, cols]
+
+
+def pack(*weights):
     whole = pl.BlockSpec(memory_space=pltpu.VMEM)
     return pl.pallas_call(
         pack_kernel,
-        in_specs=[pl.BlockSpec(memory_space=pltpu.SMEM)] + [whole] * 4,
-        out_specs=[whole] * 2,
-        out_shape=[jax.ShapeDtypeStruct((64, 8 * HD), BF)] * 2,
+        in_specs=[whole] * 4,
+        out_specs=whole,
+        out_shape=pltpu.HBM((64, 16 * HD), BF),
         name="pack",
-    )(place, *weights)
+    )(*weights)
 
 
 def finish_kernel(
@@ -493,12 +501,8 @@
     y = lax.rem(lax.div(dp, NC), NY)
     place = jnp.stack([x, y, c]).astype(jnp.int32)
 
-    keep, give = pack(place, w_query, w_key, w_value, w_out.T)
-    take = swap_core(give)
-    shard = jnp.where(
-        c == 0, jnp.concatenate([keep, take]), jnp.concatenate([take, keep])
-    )
-    weight = lax.all_gather(shard, "dp", axis=0, tiled=True, axis_index_groups=GROUPS_ZY)
+    packed = pack(w_query, w_key, w_value, w_out.T)
+    weight = lax.all_gather(packed, "dp", axis=0, tiled=True)
 
     picks = chosen[:, None] == jnp.arange(tokens.shape[0])[None, :]
     onehot = picks.astype(BF)
@@ -529,12 +533,12 @@
     allowed = allowed | jnp.eye(CAP, dtype=bool)[None]
     mask = allowed.reshape(2 * CAP, CAP).astype(F32)
 
-    qkv, d_attn, attn, probs, grad_0, grad_1, grad_2, grad_3 = forward(
+    qkv, attn, probs, grad_0, grad_1, grad_2, grad_3 = forward(
         place, normed, d_mix, weight, mask
     )
     moved = [move_y(grad_1, 1), move_y(grad_3, 3), move_y(grad_2, 2)]
 
-    own, sibling = backward(place, qkv, d_attn, attn, probs, weight)
+    own, sibling = backward(place, qkv, d_mix, attn, probs, weight)
     sibling = after(sibling, *moved)
     got = swap_core(sibling)
     sums = [(own[k].astype(F32) + got[k].astype(F32)).astype(BF) for k in (1, 3, 2)]

time: 224 us -> 222 us (level)
  starting transfers between devices: 34 us -> 31.5 us
  other arithmetic: 7.99 us -> 5.73 us
    ppermute x5 -> x4, starting transfers between devices: 9.72 us -> 4.65 us  [swap_core(): return lax.ppermute(v, 'dp', dp_perm(0, 0, 1))]
    all_gather x1, waiting for transfers between devices: 52.7 us -> 56.9 us  [per_device(): weight = lax.all_gather(packed, 'dp', axis=0, tiled=True)]
    ppermute x6, starting transfers between devices: 6.11 us -> 8.67 us  [move_x(): return lax.ppermute(v, 'mp', [(i, (i + k) % NX) for i in range(NX)])]
    ppermute x5 -> x4, waiting for transfers between devices: 4.88 us -> 3.49 us  [swap_core(): return lax.ppermute(v, 'dp', dp_perm(0, 0, 1))]
  transfers between devices with their start and end apart: 18 -> 17, of which waited for: 12 -> 10; matrix products, arithmetic and copies ran while one was open for 3% -> 4% of each run, Pallas kernels for 12% -> 13%
where the time goes in v3:
time: 222 us
  waiting for transfers between devices  118 us (53%)
  Pallas kernels  42.1 us (19%)
  starting transfers between devices  31.5 us (14%)
  between operations  15 us (7%)
  local copies, waits for them, and re-layouts  6.56 us (3%)
  other arithmetic  5.73 us (3%)
  matrix products  2.59 us (1%)
    all_gather x1, waiting for transfers between devices, per_device(): weight = lax.all_gather(packed, 'dp', axis=0, tiled=True)  56.9 us
    ppermute x6, waiting for transfers between devices, move_x(): return lax.ppermute(v, 'mp', [(i, (i + k) % NX) for i in range(NX)])  25.6 us
    pallas_call x1, Pallas kernels, backward(): pl.pallas_call(backward_kernel, grid_spec=pltpu.PrefetchScalarGridSpec(nu...  11.9 us
    ppermute x3, waiting for transfers between devices, move_y(): return lax.ppermute(v, 'dp', dp_perm(0, k, 0))  11.4 us
    all_to_all x2, starting transfers between devices, per_device(): lax.all_to_all(pieces, 'dp', 0, 0, tiled=True, axis_index_groups=GROUPS_ZY)  11.3 us
    all_to_all x2, waiting for transfers between devices, per_device(): lax.all_to_all(pieces, 'dp', 0, 0, tiled=True, axis_index_groups=GROUPS_ZY)  10.6 us
    all_to_all x1, waiting for transfers between devices, per_device(): lax.all_to_all(column, 'dp', 0, 0, tiled=True, axis_index_groups=GROUPS_Z)  10.5 us
    pallas_call x1, Pallas kernels, forward(): pl.pallas_call(forward_kernel, in_specs=[pl.BlockSpec(memory_space=pltpu....  9.36 us
  transfers between devices with their start and end apart: 17, of which 10 were waited for; matrix products, arithmetic and copies ran while one was open for 4% of the time, Pallas kernels for 13%

profile of v3, /device:TPU:1, one launch (start us, length us, event | category | flops | bytes accessed | tf_op | source)
XLA Modules:
  0.0 221.8 jit_solution(2315300838670351209)
XLA Ops:
  7.2 1.8 pack.1
  9.1 2.1 fusion.1
  11.2 0.5 fusion
  11.8 3.4 %collective-permute-start = (bf16[2,128,1024]{2,1,0:T(8,128)(2,1)S(1)}, bf16[2,128,1024]{2,1,0:T(8,128)(2,1)S(1)}, u32[]{:S(2)}, u32[]{:S(2)}) collective-permute-start(bf16[2,128,1024]{2,1,0:T(8,128)(2,1)S(1)} %pad_maximum_fusion.refs_0_.part), channel_id=1, source_target_pairs={{0,3},{1,0},{2,1},{3,2},{4,7},{5,4},{6,5},{7,6},{8,11},{9,8},{10,9... | collective-permute-start | bytes 1572872 | tf_op jit(solution)/shard_map/ppermute | solution.py:56
  15.2 0.5 collective-permute-start.1
  15.7 0.6 collective-permute-start.2
  16.3 12.5 %collective-permute-done.refs_1_ = bf16[2,128,1024]{2,1,0:T(8,128)(2,1)S(1)} collective-permute-done((bf16[2,128,1024]{2,1,0:T(8,128)(2,1)S(1)}, bf16[2,128,1024]{2,1,0:T(8,128)(2,1)S(1)}, u32[]{:S(2)}, u32[]{:S(2)}) %collective-permute-start) | collective-permute-done | bytes 524320 | tf_op jit(solution)/shard_map/ppermute | solution.py:56
  28.8 0.4 collective-permute-done.1.refs_2_
  29.2 12.7 %collective-permute-done.2.refs_3_ = bf16[2,128,1024]{2,1,0:T(8,128)(2,1)S(1)} collective-permute-done((bf16[2,128,1024]{2,1,0:T(8,128)(2,1)S(1)}, bf16[2,128,1024]{2,1,0:T(8,128)(2,1)S(1)}, u32[]{:S(2)}, u32[]{:S(2)}) %collective-permute-start.2) | collective-permute-done | bytes 524320 | tf_op jit(solution)/shard_map/ppermute | solution.py:56
  41.9 0.8 copy-done.16
  42.7 3.0 %stack.54.mine = bf16[4,2,128,1024]{3,2,1,0:T(8,128)(2,1)} custom-call(bf16[2,128,1024]{2,1,0:T(8,128)(2,1)} %copy-done.9, bf16[2,128,1024]{2,1,0:T(8,128)(2,1)} %copy-done.14, bf16[2,128,1024]{2,1,0:T(8,128)(2,1)} %copy-done.15, bf16[2,128,1024]{2,1,0:T(8,128)(2,1)} %copy-done.16), custom_call_target="tpu_custom_call" | custom-call | tf_op jit(solution)/shard_map/stack/pallas_call | solution.py:269
  45.7 0.4 collective-permute-start.3
  46.7 0.2 select_reduce_fusion
  47.0 0.2 collective-permute-start.4
  47.3 2.6 %collective-permute-done.4 = s32[3,128]{1,0:T(4,128)S(1)} collective-permute-done((s32[3,128]{1,0:T(4,128)S(1)}, s32[3,128]{1,0:T(4,128)S(1)}, u32[]{:S(2)}, u32[]{:S(2)}) %collective-permute-start.4) | collective-permute-done | bytes 1568 | tf_op jit(solution)/shard_map/ppermute | solution.py:52
  49.9 0.1 copy.15.live
  50.0 0.8 fusion.11.mask
  50.9 1.6 copy-done
  52.4 2.4 %prep.1 = (bf16[4,256,1024]{2,1,0:T(8,128)(2,1)S(1)}, bf16[4,256,1024]{2,1,0:T(8,128)(2,1)S(1)}, f32[256,128]{1,0:T(8,128)S(1)}) custom-call(s32[3]{0:T(128)S(1)} %pad_add_fusion.3.place, bf16[4,2,128,1024]{3,2,1,0:T(8,128)(2,1)S(1)} %copy-done, bf16[4,2,128,1024]{3,2,1,0:T(8,128)(2,1)S(1)} %collective-permute-done.3.other, f32[4,1,1024]{2,1,0:T(1,128)S(1)} %bitcast.67, ...), custom_call_target="tpu_custom_call" | custom-call | tf_op jit(solution)/shard_map/prep/pallas_call | solution.py:302
  54.8 1.3 copy-done.1
  56.1 1.3 copy-done.2
  57.5 0.6 copy-done.4
  58.1 56.9 %all-gather.2.cloned.1.call-done.weight.out_all.out_weight = bf16[4096,2048]{1,0:T(8,128)(2,1)} async-done(((bf16[64,2048]{1,0:T(8,128)(2,1)}), bf16[4096,2048]{1,0:T(8,128)(2,1)}) %all-gather.2.cloned.1.call-update) | async-done | bytes 16777232 | tf_op jit(solution)/shard_map/all_gather | solution.py:505
  115.0 9.4 %forward.1 = (bf16[256,768]{1,0:T(8,128)(2,1)}, bf16[256,256]{1,0:T(8,128)(2,1)}, f32[2,2,128,128]{3,2,1,0:T(8,128)}, bf16[8,256,128]{2,1,0:T(8,128)(2,1)}, bf16...) custom-call(s32[3]{0:T(128)} %copy-done.7, bf16[4,256,1024]{2,1,0:T(8,128)(2,1)} %copy-done.2, ...), custom_call_target="tpu_custom_call" | custom-call | flops 2147483648 | bytes 13631488 | tf_op jit(solution)/shard_map/forward/pallas_call | solution.py:147
  124.4 2.7 %collective-permute-start.6 = (bf16[8,256,128]{2,1,0:T(8,128)(2,1)}, bf16[8,256,128]{2,1,0:T(8,128)(2,1)S(1)}, u32[]{:S(2)}, u32[]{:S(2)}) collective-permute-start(bf16[8,256,128]{2,1,0:T(8,128)(2,1)} %get-tuple-element.31), channel_id=1, source_target_pairs={{0,24},{4,28},{8,0},{12,4},{16,8},{20,12},{24,16},{28,20},{32,56},... | collective-permute-start | bytes 1572872 | tf_op jit(solution)/shard_map/ppermute | solution.py:48
  127.1 11.9 %backward.1 = (bf16[4,2,128,1152]{3,2,1,0:T(8,128)(2,1)}, bf16[4,2,128,1152]{3,2,1,0:T(8,128)(2,1)}) custom-call(s32[3]{0:T(128)} %copy-done.7, bf16[256,768]{1,0:T(8,128)(2,1)} %get-tuple-element.34.qkv, bf16[4,256,1024]{2,1,0:T(8,128)(2,1)} %copy-done.1, bf16[4096,2048]{1,0:T(8,128)(2,1)} %all-gather.2.cloned.1.call-done.weight.out_all.out_weight, ...), custom_call_target="tpu_custom_call" | custom-call | flops 2147483648 | bytes 14680064 | tf_op jit(solution)/shard_map/backward/pallas_call | solution.py:231
  139.0 11.4 %collective-permute-done.5.refs_1_ = bf16[8,256,128]{2,1,0:T(8,128)(2,1)S(1)} collective-permute-done((bf16[8,256,128]{2,1,0:T(8,128)(2,1)}, bf16[8,256,128]{2,1,0:T(8,128)(2,1)S(1)}, u32[]{:S(2)}, u32[]{:S(2)}) %collective-permute-start.5) | collective-permute-done | bytes 524320 | tf_op jit(solution)/shard_map/ppermute | solution.py:48
  150.4 1.1 collective-permute-start.8
  151.4 1.0 add.54
  152.5 4.0 %all-to-all-start = ((bf16[8,256,128]{2,1,0:T(8,128)(2,1)}), bf16[8,256,128]{2,1,0:T(8,128)(2,1)S(1)}, u32[]{:S(2)}, u32[]{:S(2)}) async-start(bf16[8,256,128]{2,1,0:T(8,128)(2,1)} %add.54), calls=%async_computation | async-start | bytes 1048576 | tf_op jit(solution)/shard_map/all_to_all | solution.py:548
  156.5 3.4 %fusion.4 = (bf16[2,128,1152]{2,1,0:T(8,128)(2,1)S(1)}, bf16[2,128,1152]{2,1,0:T(8,128)(2,1)}, bf16[2,128,1152]{2,1,0:T(8,128)(2,1)}) fusion(bf16[4,2,128,1152]{3,2,1,0:T(8,128)(2,1)} %collective-permute-done.8.got, bf16[4,2,128,1152]{3,2,1,0:T(8,128)(2,1)} %get-tuple-element.37.own), kind=kLoop, calls=%fused_computation.9 | loop fusion | flops 3538944 | bytes 5308416 | tf_op jit(solution)/shard_map/convert_element_type | solution.py:544
  159.9 1.2 collective-permute-start.9
  161.1 1.5 collective-permute-start.10
  162.5 1.5 collective-permute-start.11
  164.0 10.5 %all-to-all-done.parts = bf16[8,256,128]{2,1,0:T(8,128)(2,1)S(1)} async-done(((bf16[8,256,128]{2,1,0:T(8,128)(2,1)}), bf16[8,256,128]{2,1,0:T(8,128)(2,1)S(1)}, u32[]{:S(2)}, u32[]{:S(2)}) %all-to-all-start) | async-done | bytes 524320 | tf_op jit(solution)/shard_map/all_to_all | solution.py:548
  174.5 1.1 gram.1
  175.6 4.3 %all-to-all-start.1 = ((f32[32,8,128]{2,1,0:T(8,128)}), f32[32,8,128]{2,1,0:T(8,128)S(1)}, u32[]{:S(2)}, u32[]{:S(2)}) async-start(f32[32,8,128]{2,1,0:T(8,128)} %bitcast.22), calls=%async_computation.1 | async-start | bytes 262144 | tf_op jit(solution)/shard_map/all_to_all | solution.py:551
  180.0 9.3 %all-to-all-done.1.pieces = f32[32,8,128]{2,1,0:T(8,128)S(1)} async-done(((f32[32,8,128]{2,1,0:T(8,128)}), f32[32,8,128]{2,1,0:T(8,128)S(1)}, u32[]{:S(2)}, u32[]{:S(2)}) %all-to-all-start.1) | async-done | bytes 131104 | tf_op jit(solution)/shard_map/all_to_all | solution.py:551
  189.3 0.7 copy-done.13
  189.9 1.6 total.1
  191.6 7.0 %all-to-all-start.2 = ((f32[32,8,128]{2,1,0:T(8,128)}), f32[32,8,128]{2,1,0:T(8,128)S(1)}, u32[]{:S(2)}, u32[]{:S(2)}) async-start(f32[32,8,128]{2,1,0:T(8,128)} %total.1), calls=%async_computation.2 | async-start | bytes 262144 | tf_op jit(solution)/shard_map/all_to_all | solution.py:554
  198.6 0.5 fusion.12.slots
  199.1 7.6 %finish.1 = (bf16[1024,1024]{1,0:T(8,128)(2,1)}, bf16[1024,1024]{1,0:T(8,128)(2,1)}) custom-call(s32[3]{0:T(128)} %copy-done.7, bf16[4,2,128,1152]{3,2,1,0:T(8,128)(2,1)} %get-tuple-element.37.own, bf16[4,2,128,1152]{3,2,1,0:T(8,128)(2,1)} %collective-permute-done.8.got, bf16[2,128,1152]{2,1,0:T(8,128)(2,1)} %copy-done.10, bf16[2,128,1152]{2,1,0:T(8,128)(2,1)} %copy-done.11, ...), custom_call_target="tpu_custom_call" | custom-call | flops 536870912 | bytes 11534336 | tf_op jit(solution)/shard_map/finish/pallas_call | solution.py:376
  206.7 1.2 all-to-all-done.2
  207.9 2.4 %muon.1 = f32[128,256]{1,0:T(8,128)S(1)} custom-call(f32[2,128,128]{2,1,0:T(8,128)S(1)} %bitcast.64, f32[256,128]{1,0:T(8,128)S(1)} %get-tuple-element.50.total), custom_call_target="tpu_custom_call" | custom-call | tf_op jit(solution)/shard_map/muon/pallas_call | solution.py:487
  210.4 3.0 %collective-permute-start.12 = (f32[64,256]{1,0:T(8,128)S(1)}, f32[64,256]{1,0:T(8,128)S(1)}, u32[]{:S(2)}, u32[]{:S(2)}) collective-permute-start(f32[64,256]{1,0:T(8,128)S(1)} %get-tuple-element.57), channel_id=1, source_target_pairs={{0,4},{4,0},{8,12},{12,8},{16,20},{20,16},{24,28},{28,24},{32,36},... | collective-permute-start | bytes 196616 | tf_op jit(solution)/shard_map/ppermute | solution.py:52
  213.4 0.9 collective-permute-done.12
  214.3 0.7 fusion.7
  (52 shorter events, 0.4 us)
Async XLA Ops:
  7.2 4.0 %copy-start.17 = (s32[128]{0:T(128)S(1)}, s32[128]{0:T(128)}, u32[]{:S(2)}) copy-start(s32[128]{0:T(128)} %param.19) | copy-start | bytes 1540
  7.2 4.0 %copy-start.8 = (bf16[1024,1024]{1,0:T(8,128)(2,1)S(1)}, bf16[1024,1024]{1,0:T(8,128)(2,1)}, u32[]{:S(2)}) copy-start(bf16[1024,1024]{1,0:T(8,128)(2,1)} %tokens.1) | copy-start | bytes 6291460
  7.2 107.8 %all-gather.2.cloned.1.call-start = ((), (), s32[]{:S(2)}) async-start(), calls=%async_computation.3 | async-start | bytes 17039360 | tf_op jit(solution)/shard_map/all_gather | solution.py:505
  11.7 30.1 %copy-start.9 = (bf16[2,128,1024]{2,1,0:T(8,128)(2,1)}, bf16[2,128,1024]{2,1,0:T(8,128)(2,1)S(1)}, u32[]{:S(2)}) copy-start(bf16[2,128,1024]{2,1,0:T(8,128)(2,1)S(1)} %pad_maximum_fusion.refs_0_.part) | copy-start | bytes 1572868
  11.8 35.0 %copy-start.18 = (s32[1024]{0:T(1024)S(1)}, s32[1024]{0:T(1024)}, u32[]{:S(2)}) copy-start(s32[1024]{0:T(1024)} %param.21) | copy-start | bytes 12292
  11.8 39.1 %copy-start.5 = (f32[4096]{0:T(1024)S(1)}, f32[4096]{0:T(1024)}, u32[]{:S(2)}) copy-start(f32[4096]{0:T(1024)} %param.17) | copy-start | bytes 49156
  11.8 39.1 %copy-start.6 = (f32[4096]{0:T(1024)S(1)}, f32[4096]{0:T(1024)}, u32[]{:S(2)}) copy-start(f32[4096]{0:T(1024)} %param.18) | copy-start | bytes 49156
  11.8 17.0 %collective-permute-start = (bf16[2,128,1024]{2,1,0:T(8,128)(2,1)S(1)}, bf16[2,128,1024]{2,1,0:T(8,128)(2,1)S(1)}, u32[]{:S(2)}, u32[]{:S(2)}) collective-permute-start(bf16[2,128,1024]{2,1,0:T(8,128)(2,1)S(1)} %pad_maximum_fusion.refs_0_.part), channel_id=1, source_target_pairs={{0,3},{1,0},{2,1},{3,2},{4,7},{5,4},{6,5},{7,6},{8,11},{9,8},{10,9... | collective-permute-start | bytes 1572872 | tf_op jit(solution)/shard_map/ppermute | solution.py:56
  15.2 14.0 %collective-permute-start.1 = (bf16[2,128,1024]{2,1,0:T(8,128)(2,1)S(1)}, bf16[2,128,1024]{2,1,0:T(8,128)(2,1)S(1)}, u32[]{:S(2)}, u32[]{:S(2)}) collective-permute-start(bf16[2,128,1024]{2,1,0:T(8,128)(2,1)S(1)} %pad_maximum_fusion.refs_0_.part), channel_id=1, source_target_pairs={{0,2},{1,3},{2,0},{3,1},{4,6},{5,7},{6,4},{7,5},{8,10},{9,11},{10,... | collective-permute-start | bytes 1572872 | tf_op jit(solution)/shard_map/ppermute | solution.py:56
  15.7 26.2 %collective-permute-start.2 = (bf16[2,128,1024]{2,1,0:T(8,128)(2,1)S(1)}, bf16[2,128,1024]{2,1,0:T(8,128)(2,1)S(1)}, u32[]{:S(2)}, u32[]{:S(2)}) collective-permute-start(bf16[2,128,1024]{2,1,0:T(8,128)(2,1)S(1)} %pad_maximum_fusion.refs_0_.part), channel_id=1, source_target_pairs={{0,1},{1,2},{2,3},{3,0},{4,5},{5,6},{6,7},{7,4},{8,9},{9,10},{10,1... | collective-permute-start | bytes 1572872 | tf_op jit(solution)/shard_map/ppermute | solution.py:56
  28.8 13.1 %copy-start.14 = (bf16[2,128,1024]{2,1,0:T(8,128)(2,1)}, bf16[2,128,1024]{2,1,0:T(8,128)(2,1)S(1)}, u32[]{:S(2)}) copy-start(bf16[2,128,1024]{2,1,0:T(8,128)(2,1)S(1)} %collective-permute-done.refs_1_) | copy-start | bytes 1572868
  29.2 12.7 %copy-start.15 = (bf16[2,128,1024]{2,1,0:T(8,128)(2,1)}, bf16[2,128,1024]{2,1,0:T(8,128)(2,1)S(1)}, u32[]{:S(2)}) copy-start(bf16[2,128,1024]{2,1,0:T(8,128)(2,1)S(1)} %collective-permute-done.1.refs_2_) | copy-start | bytes 1572868
  41.9 0.8 copy-start.16
  45.7 5.1 %collective-permute-start.3 = (bf16[4,2,128,1024]{3,2,1,0:T(8,128)(2,1)}, bf16[4,2,128,1024]{3,2,1,0:T(8,128)(2,1)S(1)}, u32[]{:S(2)}, u32[]{:S(2)}) collective-permute-start(bf16[4,2,128,1024]{3,2,1,0:T(8,128)(2,1)} %stack.54.mine), channel_id=1, source_target_pairs={{0,4},{4,0},{8,12},{12,8},{16,20},{20,16},{24,28},{28,24},{32,36},... | collective-permute-start | bytes 6291464 | tf_op jit(solution)/shard_map/ppermute | solution.py:52
  47.0 2.9 %collective-permute-start.4 = (s32[3,128]{1,0:T(4,128)S(1)}, s32[3,128]{1,0:T(4,128)S(1)}, u32[]{:S(2)}, u32[]{:S(2)}) collective-permute-start(s32[3,128]{1,0:T(4,128)S(1)} %get-tuple-element.61), channel_id=1, source_target_pairs={{0,4},{4,0},{8,12},{12,8},{16,20},{20,16},{24,28},{28,24},{32,36},... | collective-permute-start | bytes 4616 | tf_op jit(solution)/shard_map/ppermute | solution.py:52
  47.3 7.5 %copy-start.7 = (s32[3]{0:T(128)}, s32[3]{0:T(128)S(1)}, u32[]{:S(2)}) copy-start(s32[3]{0:T(128)S(1)} %pad_add_fusion.3.place) | copy-start | bytes 40
  50.8 1.6 copy-start
  54.8 1.3 copy-start.1
  56.1 1.3 copy-start.2
  57.5 0.6 copy-start.4
  124.3 26.0 %collective-permute-start.5 = (bf16[8,256,128]{2,1,0:T(8,128)(2,1)}, bf16[8,256,128]{2,1,0:T(8,128)(2,1)S(1)}, u32[]{:S(2)}, u32[]{:S(2)}) collective-permute-start(bf16[8,256,128]{2,1,0:T(8,128)(2,1)} %get-tuple-element.30), channel_id=1, source_target_pairs={{0,8},{4,12},{8,16},{12,20},{16,24},{20,28},{24,0},{28,4},{32,40},... | collective-permute-start | bytes 1572872 | tf_op jit(solution)/shard_map/ppermute | solution.py:48
  124.4 25.9 %collective-permute-start.6 = (bf16[8,256,128]{2,1,0:T(8,128)(2,1)}, bf16[8,256,128]{2,1,0:T(8,128)(2,1)S(1)}, u32[]{:S(2)}, u32[]{:S(2)}) collective-permute-start(bf16[8,256,128]{2,1,0:T(8,128)(2,1)} %get-tuple-element.31), channel_id=1, source_target_pairs={{0,24},{4,28},{8,0},{12,4},{16,8},{20,12},{24,16},{28,20},{32,56},... | collective-permute-start | bytes 1572872 | tf_op jit(solution)/shard_map/ppermute | solution.py:48
  127.1 23.3 %collective-permute-start.7 = (bf16[8,256,128]{2,1,0:T(8,128)(2,1)}, bf16[8,256,128]{2,1,0:T(8,128)(2,1)S(1)}, u32[]{:S(2)}, u32[]{:S(2)}) collective-permute-start(bf16[8,256,128]{2,1,0:T(8,128)(2,1)} %get-tuple-element.32), channel_id=1, source_target_pairs={{0,16},{4,20},{8,24},{12,28},{16,0},{20,4},{24,8},{28,12},{32,48},... | collective-permute-start | bytes 1572872 | tf_op jit(solution)/shard_map/ppermute | solution.py:48
  127.1 24.3 %copy-start.3 = (bf16[8,256,128]{2,1,0:T(8,128)(2,1)S(1)}, bf16[8,256,128]{2,1,0:T(8,128)(2,1)}, u32[]{:S(2)}) copy-start(bf16[8,256,128]{2,1,0:T(8,128)(2,1)} %get-tuple-element.29.refs_0_) | copy-start | bytes 1572868
  150.4 6.1 %collective-permute-start.8 = (bf16[4,2,128,1152]{3,2,1,0:T(8,128)(2,1)}, bf16[4,2,128,1152]{3,2,1,0:T(8,128)(2,1)}, u32[]{:S(2)}, u32[]{:S(2)}) collective-permute-start(bf16[4,2,128,1152]{3,2,1,0:T(8,128)(2,1)} %get-tuple-element.39), channel_id=1, source_target_pairs={{0,4},{4,0},{8,12},{12,8},{16,20},{20,16},{24,28},{28,24},{32,36},... | collective-permute-start | bytes 7077896 | tf_op jit(solution)/shard_map/ppermute | solution.py:52
  152.5 22.0 %all-to-all-start = ((bf16[8,256,128]{2,1,0:T(8,128)(2,1)}), bf16[8,256,128]{2,1,0:T(8,128)(2,1)S(1)}, u32[]{:S(2)}, u32[]{:S(2)}) async-start(bf16[8,256,128]{2,1,0:T(8,128)(2,1)} %add.54), calls=%async_computation | async-start | bytes 1048576 | tf_op jit(solution)/shard_map/all_to_all | solution.py:548
  159.9 31.7 %collective-permute-start.9 = (bf16[2,128,1152]{2,1,0:T(8,128)(2,1)}, bf16[2,128,1152]{2,1,0:T(8,128)(2,1)S(1)}, u32[]{:S(2)}, u32[]{:S(2)}) collective-permute-start(bf16[2,128,1152]{2,1,0:T(8,128)(2,1)} %get-tuple-element.55), channel_id=1, source_target_pairs={{0,1},{1,2},{2,3},{3,0},{4,5},{5,6},{6,7},{7,4},{8,9},{9,10},{10,1... | collective-permute-start | bytes 1769480 | tf_op jit(solution)/shard_map/ppermute | solution.py:56
  161.1 30.5 %collective-permute-start.10 = (bf16[2,128,1152]{2,1,0:T(8,128)(2,1)}, bf16[2,128,1152]{2,1,0:T(8,128)(2,1)S(1)}, u32[]{:S(2)}, u32[]{:S(2)}) collective-permute-start(bf16[2,128,1152]{2,1,0:T(8,128)(2,1)} %get-tuple-element.54), channel_id=1, source_target_pairs={{0,3},{1,0},{2,1},{3,2},{4,7},{5,4},{6,5},{7,6},{8,11},{9,8},{10,9... | collective-permute-start | bytes 1769480 | tf_op jit(solution)/shard_map/ppermute | solution.py:56
  162.5 29.0 %collective-permute-start.11 = (bf16[2,128,1152]{2,1,0:T(8,128)(2,1)S(1)}, bf16[2,128,1152]{2,1,0:T(8,128)(2,1)S(1)}, u32[]{:S(2)}, u32[]{:S(2)}) collective-permute-start(bf16[2,128,1152]{2,1,0:T(8,128)(2,1)S(1)} %get-tuple-element.53), channel_id=1, source_target_pairs={{0,2},{1,3},{2,0},{3,1},{4,6},{5,7},{6,4},{7,5},{8,10},{9,11},{10,... | collective-permute-start | bytes 1769480 | tf_op jit(solution)/shard_map/ppermute | solution.py:56
  175.6 13.7 %all-to-all-start.1 = ((f32[32,8,128]{2,1,0:T(8,128)}), f32[32,8,128]{2,1,0:T(8,128)S(1)}, u32[]{:S(2)}, u32[]{:S(2)}) async-start(f32[32,8,128]{2,1,0:T(8,128)} %bitcast.22), calls=%async_computation.1 | async-start | bytes 262144 | tf_op jit(solution)/shard_map/all_to_all | solution.py:551
  189.3 0.7 copy-start.13
  191.5 7.6 %copy-start.10 = (bf16[2,128,1152]{2,1,0:T(8,128)(2,1)}, bf16[2,128,1152]{2,1,0:T(8,128)(2,1)S(1)}, u32[]{:S(2)}) copy-start(bf16[2,128,1152]{2,1,0:T(8,128)(2,1)S(1)} %collective-permute-done.9.sent_1) | copy-start | bytes 1769476
  191.6 7.6 %copy-start.11 = (bf16[2,128,1152]{2,1,0:T(8,128)(2,1)}, bf16[2,128,1152]{2,1,0:T(8,128)(2,1)S(1)}, u32[]{:S(2)}) copy-start(bf16[2,128,1152]{2,1,0:T(8,128)(2,1)S(1)} %collective-permute-done.10.sent_2) | copy-start | bytes 1769476
  191.6 7.5 %copy-start.12 = (bf16[2,128,1152]{2,1,0:T(8,128)(2,1)}, bf16[2,128,1152]{2,1,0:T(8,128)(2,1)S(1)}, u32[]{:S(2)}) copy-start(bf16[2,128,1152]{2,1,0:T(8,128)(2,1)S(1)} %collective-permute-done.11.sent_3) | copy-start | bytes 1769476
  191.6 16.4 %all-to-all-start.2 = ((f32[32,8,128]{2,1,0:T(8,128)}), f32[32,8,128]{2,1,0:T(8,128)S(1)}, u32[]{:S(2)}, u32[]{:S(2)}) async-start(f32[32,8,128]{2,1,0:T(8,128)} %total.1), calls=%async_computation.2 | async-start | bytes 262144 | tf_op jit(solution)/shard_map/all_to_all | solution.py:554
  210.4 3.9 %collective-permute-start.12 = (f32[64,256]{1,0:T(8,128)S(1)}, f32[64,256]{1,0:T(8,128)S(1)}, u32[]{:S(2)}, u32[]{:S(2)}) collective-permute-start(f32[64,256]{1,0:T(8,128)S(1)} %get-tuple-element.57), channel_id=1, source_target_pairs={{0,4},{4,0},{8,12},{12,8},{16,20},{20,16},{24,28},{28,24},{32,36},... | collective-permute-start | bytes 196616 | tf_op jit(solution)/shard_map/ppermute | solution.py:52
Sparse Core Ops, SparseCore 0:
  10.8 104.1 all-gather.1

commit v4 on v3

--- a/solution.py
+++ b/solution.py
@@ -313,21 +313,29 @@
     )(place, mine, other, gain, router, live)
 
 
-def pack_kernel(w_query, w_key, w_value, w_out, out):
+def pack_kernel(w_query, w_key, w_value, w_out, out, sems):
+    moves = []
     for core in range(NC):
         cols = pl.ds(core * 2 * HD, 2 * HD)
-        for i, w in enumerate((w_query, w_key, w_value)):
-            out[:, pl.ds((3 * core + i) * 2 * HD, 2 * HD)] = w[:, cols]
-        out[:, pl.ds((6 + core) * 2 * HD, 2 * HD)] = w_out[:, cols]
+        for i, w in enumerate((w_query, w_key, w_value, w_out)):
+            block = 3 * core + i if i < 3 else 6 + core
+            target = out.at[:, pl.ds(block * 2 * HD, 2 * HD)]
+            moves.append(pltpu.make_async_copy(w.at[:, cols], target, sems.at[4 * core + i]))
+    for move in moves:
+        move.start()
+    for move in moves:
+        move.wait()
 
 
 def pack(*weights):
-    whole = pl.BlockSpec(memory_space=pltpu.VMEM)
+    outside = pl.BlockSpec(memory_space=pl.ANY)
     return pl.pallas_call(
         pack_kernel,
-        in_specs=[whole] * 4,
-        out_specs=whole,
+        in_specs=[outside] * 4,
+        out_specs=outside,
         out_shape=pltpu.HBM((64, 16 * HD), BF),
+        scratch_shapes=[pltpu.SemaphoreType.DMA((8,))],
+        compiler_params=pltpu.CompilerParams(vmem_limit_bytes=VMEM_LIMIT),
         name="pack",
     )(*weights)
 

time: 222 us -> 228 us (1.027)
  Pallas kernels: 42.1 us -> 49.4 us
    pallas_call x1, Pallas kernels: 1.8 us -> 9.11 us  [pack(): pl.pallas_call(pack_kernel, in_specs=[outside] * 4, out_specs=outside, ou...]
  transfers between devices with their start and end apart: 17 -> 17, of which waited for: 10 -> 10; matrix products, arithmetic and copies ran while one was open for 4% -> 3% of each run, Pallas kernels for 13% -> 13%
where the time goes in v4:
time: 228 us; the launch traced here: 227 us
  waiting for transfers between devices  117 us (51%)
  Pallas kernels  49.4 us (22%)
  starting transfers between devices  31.5 us (14%)
  between operations  15 us (7%)
  local copies, waits for them, and re-layouts  6.56 us (3%)
  other arithmetic  5.73 us (3%)
  matrix products  2.59 us (1%)
    all_gather x1, waiting for transfers between devices, per_device(): weight = lax.all_gather(packed, 'dp', axis=0, tiled=True)  55.2 us
    ppermute x6, waiting for transfers between devices, move_x(): return lax.ppermute(v, 'mp', [(i, (i + k) % NX) for i in range(NX)])  25.5 us
    pallas_call x1, Pallas kernels, backward(): pl.pallas_call(backward_kernel, grid_spec=pltpu.PrefetchScalarGridSpec(nu...  11.9 us
    ppermute x3, waiting for transfers between devices, move_y(): return lax.ppermute(v, 'dp', dp_perm(0, k, 0))  11.4 us
    all_to_all x2, starting transfers between devices, per_device(): lax.all_to_all(pieces, 'dp', 0, 0, tiled=True, axis_index_groups=GROUPS_ZY)  11.3 us
    all_to_all x2, waiting for transfers between devices, per_device(): lax.all_to_all(pieces, 'dp', 0, 0, tiled=True, axis_index_groups=GROUPS_ZY)  10.6 us
    all_to_all x1, waiting for transfers between devices, per_device(): lax.all_to_all(column, 'dp', 0, 0, tiled=True, axis_index_groups=GROUPS_Z)  10.5 us
    pallas_call x1, Pallas kernels, forward(): pl.pallas_call(forward_kernel, in_specs=[pl.BlockSpec(memory_space=pltpu....  9.36 us
  transfers between devices with their start and end apart: 17, of which 10 were waited for; matrix products, arithmetic and copies ran while one was open for 3% of the time, Pallas kernels for 13%

profile of v4, /device:TPU:1, one launch (start us, length us, event | category | flops | bytes accessed | tf_op | source)
XLA Modules:
  0.0 227.5 jit_solution(680751055484953453)
XLA Ops:
  7.2 9.1 %pack.1 = bf16[64,2048]{1,0:T(8,128)(2,1)} custom-call(bf16[64,512]{1,0:T(8,128)(2,1)} %w_query.1, bf16[64,512]{1,0:T(8,128)(2,1)} %w_key.1, bf16[64,512]{1,0:T(8,128)(2,1)} %w_value.1, bf16[64,512]{1,0:T(8,128)(2,1)} %bitcast.70), custom_call_target="tpu_custom_call" | custom-call | tf_op jit(solution)/shard_map/pack/pallas_call | solution.py:332
  16.4 2.1 fusion.1
  18.5 0.5 fusion
  19.1 3.4 %collective-permute-start = (bf16[2,128,1024]{2,1,0:T(8,128)(2,1)S(1)}, bf16[2,128,1024]{2,1,0:T(8,128)(2,1)S(1)}, u32[]{:S(2)}, u32[]{:S(2)}) collective-permute-start(bf16[2,128,1024]{2,1,0:T(8,128)(2,1)S(1)} %pad_maximum_fusion.refs_0_.part), channel_id=1, source_target_pairs={{0,3},{1,0},{2,1},{3,2},{4,7},{5,4},{6,5},{7,6},{8,11},{9,8},{10,9... | collective-permute-start | bytes 1572872 | tf_op jit(solution)/shard_map/ppermute | solution.py:56
  22.5 0.5 collective-permute-start.1
  23.0 0.6 collective-permute-start.2
  23.6 12.5 %collective-permute-done.refs_1_ = bf16[2,128,1024]{2,1,0:T(8,128)(2,1)S(1)} collective-permute-done((bf16[2,128,1024]{2,1,0:T(8,128)(2,1)S(1)}, bf16[2,128,1024]{2,1,0:T(8,128)(2,1)S(1)}, u32[]{:S(2)}, u32[]{:S(2)}) %collective-permute-start) | collective-permute-done | bytes 524320 | tf_op jit(solution)/shard_map/ppermute | solution.py:56
  36.1 0.4 collective-permute-done.1.refs_2_
  36.5 12.6 %collective-permute-done.2.refs_3_ = bf16[2,128,1024]{2,1,0:T(8,128)(2,1)S(1)} collective-permute-done((bf16[2,128,1024]{2,1,0:T(8,128)(2,1)S(1)}, bf16[2,128,1024]{2,1,0:T(8,128)(2,1)S(1)}, u32[]{:S(2)}, u32[]{:S(2)}) %collective-permute-start.2) | collective-permute-done | bytes 524320 | tf_op jit(solution)/shard_map/ppermute | solution.py:56
  49.1 0.8 copy-done.16
  49.9 3.0 %stack.54.mine = bf16[4,2,128,1024]{3,2,1,0:T(8,128)(2,1)} custom-call(bf16[2,128,1024]{2,1,0:T(8,128)(2,1)} %copy-done.9, bf16[2,128,1024]{2,1,0:T(8,128)(2,1)} %copy-done.14, bf16[2,128,1024]{2,1,0:T(8,128)(2,1)} %copy-done.15, bf16[2,128,1024]{2,1,0:T(8,128)(2,1)} %copy-done.16), custom_call_target="tpu_custom_call" | custom-call | tf_op jit(solution)/shard_map/stack/pallas_call | solution.py:269
  52.9 0.5 collective-permute-start.3
  54.1 0.2 select_reduce_fusion
  54.3 0.1 collective-permute-start.4
  54.5 2.7 %collective-permute-done.4 = s32[3,128]{1,0:T(4,128)S(1)} collective-permute-done((s32[3,128]{1,0:T(4,128)S(1)}, s32[3,128]{1,0:T(4,128)S(1)}, u32[]{:S(2)}, u32[]{:S(2)}) %collective-permute-start.4) | collective-permute-done | bytes 1568 | tf_op jit(solution)/shard_map/ppermute | solution.py:52
  57.2 0.1 copy.15.live
  57.4 0.8 fusion.11.mask
  58.2 1.6 copy-done
  59.8 2.4 %prep.1 = (bf16[4,256,1024]{2,1,0:T(8,128)(2,1)S(1)}, bf16[4,256,1024]{2,1,0:T(8,128)(2,1)S(1)}, f32[256,128]{1,0:T(8,128)S(1)}) custom-call(s32[3]{0:T(128)S(1)} %pad_add_fusion.3.place, bf16[4,2,128,1024]{3,2,1,0:T(8,128)(2,1)S(1)} %copy-done, bf16[4,2,128,1024]{3,2,1,0:T(8,128)(2,1)S(1)} %collective-permute-done.3.other, f32[4,1,1024]{2,1,0:T(1,128)S(1)} %bitcast.67, ...), custom_call_target="tpu_custom_call" | custom-call | tf_op jit(solution)/shard_map/prep/pallas_call | solution.py:302
  62.2 1.3 copy-done.1
  63.5 1.3 copy-done.2
  64.8 0.6 copy-done.4
  65.4 55.2 %all-gather.2.cloned.1.call-done.weight.out_all.out_weight = bf16[4096,2048]{1,0:T(8,128)(2,1)} async-done(((bf16[64,2048]{1,0:T(8,128)(2,1)}), bf16[4096,2048]{1,0:T(8,128)(2,1)}) %all-gather.2.cloned.1.call-update) | async-done | bytes 16777232 | tf_op jit(solution)/shard_map/all_gather | solution.py:513
  120.7 9.4 %forward.1 = (bf16[256,768]{1,0:T(8,128)(2,1)}, bf16[256,256]{1,0:T(8,128)(2,1)}, f32[2,2,128,128]{3,2,1,0:T(8,128)}, bf16[8,256,128]{2,1,0:T(8,128)(2,1)}, bf16...) custom-call(s32[3]{0:T(128)} %copy-done.7, bf16[4,256,1024]{2,1,0:T(8,128)(2,1)} %copy-done.2, ...), custom_call_target="tpu_custom_call" | custom-call | flops 2147483648 | bytes 13631488 | tf_op jit(solution)/shard_map/forward/pallas_call | solution.py:147
  130.1 2.7 %collective-permute-start.6 = (bf16[8,256,128]{2,1,0:T(8,128)(2,1)}, bf16[8,256,128]{2,1,0:T(8,128)(2,1)S(1)}, u32[]{:S(2)}, u32[]{:S(2)}) collective-permute-start(bf16[8,256,128]{2,1,0:T(8,128)(2,1)} %get-tuple-element.31), channel_id=1, source_target_pairs={{0,24},{4,28},{8,0},{12,4},{16,8},{20,12},{24,16},{28,20},{32,56},... | collective-permute-start | bytes 1572872 | tf_op jit(solution)/shard_map/ppermute | solution.py:48
  132.8 11.9 %backward.1 = (bf16[4,2,128,1152]{3,2,1,0:T(8,128)(2,1)}, bf16[4,2,128,1152]{3,2,1,0:T(8,128)(2,1)}) custom-call(s32[3]{0:T(128)} %copy-done.7, bf16[256,768]{1,0:T(8,128)(2,1)} %get-tuple-element.34.qkv, bf16[4,256,1024]{2,1,0:T(8,128)(2,1)} %copy-done.1, bf16[4096,2048]{1,0:T(8,128)(2,1)} %all-gather.2.cloned.1.call-done.weight.out_all.out_weight, ...), custom_call_target="tpu_custom_call" | custom-call | flops 2147483648 | bytes 14680064 | tf_op jit(solution)/shard_map/backward/pallas_call | solution.py:231
  144.7 11.4 %collective-permute-done.5.refs_1_ = bf16[8,256,128]{2,1,0:T(8,128)(2,1)S(1)} collective-permute-done((bf16[8,256,128]{2,1,0:T(8,128)(2,1)}, bf16[8,256,128]{2,1,0:T(8,128)(2,1)S(1)}, u32[]{:S(2)}, u32[]{:S(2)}) %collective-permute-start.5) | collective-permute-done | bytes 524320 | tf_op jit(solution)/shard_map/ppermute | solution.py:48
  156.1 1.1 collective-permute-start.8
  157.1 1.0 add.54
  158.2 4.0 %all-to-all-start = ((bf16[8,256,128]{2,1,0:T(8,128)(2,1)}), bf16[8,256,128]{2,1,0:T(8,128)(2,1)S(1)}, u32[]{:S(2)}, u32[]{:S(2)}) async-start(bf16[8,256,128]{2,1,0:T(8,128)(2,1)} %add.54), calls=%async_computation | async-start | bytes 1048576 | tf_op jit(solution)/shard_map/all_to_all | solution.py:556
  162.2 3.4 %fusion.4 = (bf16[2,128,1152]{2,1,0:T(8,128)(2,1)S(1)}, bf16[2,128,1152]{2,1,0:T(8,128)(2,1)}, bf16[2,128,1152]{2,1,0:T(8,128)(2,1)}) fusion(bf16[4,2,128,1152]{3,2,1,0:T(8,128)(2,1)} %collective-permute-done.8.got, bf16[4,2,128,1152]{3,2,1,0:T(8,128)(2,1)} %get-tuple-element.37.own), kind=kLoop, calls=%fused_computation.9 | loop fusion | flops 3538944 | bytes 5308416 | tf_op jit(solution)/shard_map/convert_element_type | solution.py:552
  165.6 1.2 collective-permute-start.9
  166.8 1.5 collective-permute-start.10
  168.3 1.5 collective-permute-start.11
  169.7 10.5 %all-to-all-done.parts = bf16[8,256,128]{2,1,0:T(8,128)(2,1)S(1)} async-done(((bf16[8,256,128]{2,1,0:T(8,128)(2,1)}), bf16[8,256,128]{2,1,0:T(8,128)(2,1)S(1)}, u32[]{:S(2)}, u32[]{:S(2)}) %all-to-all-start) | async-done | bytes 524320 | tf_op jit(solution)/shard_map/all_to_all | solution.py:556
  180.2 1.1 gram.1
  181.3 4.3 %all-to-all-start.1 = ((f32[32,8,128]{2,1,0:T(8,128)}), f32[32,8,128]{2,1,0:T(8,128)S(1)}, u32[]{:S(2)}, u32[]{:S(2)}) async-start(f32[32,8,128]{2,1,0:T(8,128)} %bitcast.22), calls=%async_computation.1 | async-start | bytes 262144 | tf_op jit(solution)/shard_map/all_to_all | solution.py:559
  185.7 9.3 %all-to-all-done.1.pieces = f32[32,8,128]{2,1,0:T(8,128)S(1)} async-done(((f32[32,8,128]{2,1,0:T(8,128)}), f32[32,8,128]{2,1,0:T(8,128)S(1)}, u32[]{:S(2)}, u32[]{:S(2)}) %all-to-all-start.1) | async-done | bytes 131104 | tf_op jit(solution)/shard_map/all_to_all | solution.py:559
  195.0 0.7 copy-done.13
  195.7 1.6 total.1
  197.3 7.0 %all-to-all-start.2 = ((f32[32,8,128]{2,1,0:T(8,128)}), f32[32,8,128]{2,1,0:T(8,128)S(1)}, u32[]{:S(2)}, u32[]{:S(2)}) async-start(f32[32,8,128]{2,1,0:T(8,128)} %total.1), calls=%async_computation.2 | async-start | bytes 262144 | tf_op jit(solution)/shard_map/all_to_all | solution.py:562
  204.3 0.5 fusion.12.slots
  204.8 7.6 %finish.1 = (bf16[1024,1024]{1,0:T(8,128)(2,1)}, bf16[1024,1024]{1,0:T(8,128)(2,1)}) custom-call(s32[3]{0:T(128)} %copy-done.7, bf16[4,2,128,1152]{3,2,1,0:T(8,128)(2,1)} %get-tuple-element.37.own, bf16[4,2,128,1152]{3,2,1,0:T(8,128)(2,1)} %collective-permute-done.8.got, bf16[2,128,1152]{2,1,0:T(8,128)(2,1)} %copy-done.10, bf16[2,128,1152]{2,1,0:T(8,128)(2,1)} %copy-done.11, ...), custom_call_target="tpu_custom_call" | custom-call | flops 536870912 | bytes 11534336 | tf_op jit(solution)/shard_map/finish/pallas_call | solution.py:384
  212.4 1.2 all-to-all-done.2
  213.7 2.4 %muon.1 = f32[128,256]{1,0:T(8,128)S(1)} custom-call(f32[2,128,128]{2,1,0:T(8,128)S(1)} %bitcast.64, f32[256,128]{1,0:T(8,128)S(1)} %get-tuple-element.50.total), custom_call_target="tpu_custom_call" | custom-call | tf_op jit(solution)/shard_map/muon/pallas_call | solution.py:495
  216.1 3.0 %collective-permute-start.12 = (f32[64,256]{1,0:T(8,128)S(1)}, f32[64,256]{1,0:T(8,128)S(1)}, u32[]{:S(2)}, u32[]{:S(2)}) collective-permute-start(f32[64,256]{1,0:T(8,128)S(1)} %get-tuple-element.57), channel_id=1, source_target_pairs={{0,4},{4,0},{8,12},{12,8},{16,20},{20,16},{24,28},{28,24},{32,36},... | collective-permute-start | bytes 196616 | tf_op jit(solution)/shard_map/ppermute | solution.py:52
  219.1 0.9 collective-permute-done.12
  220.0 0.7 fusion.7
  (52 shorter events, 0.4 us)
Async XLA Ops:
  7.2 11.3 %copy-start.17 = (s32[128]{0:T(128)S(1)}, s32[128]{0:T(128)}, u32[]{:S(2)}) copy-start(s32[128]{0:T(128)} %param.19) | copy-start | bytes 1540
  7.2 11.3 %copy-start.8 = (bf16[1024,1024]{1,0:T(8,128)(2,1)S(1)}, bf16[1024,1024]{1,0:T(8,128)(2,1)}, u32[]{:S(2)}) copy-start(bf16[1024,1024]{1,0:T(8,128)(2,1)} %tokens.1) | copy-start | bytes 6291460
  7.2 113.5 %all-gather.2.cloned.1.call-start = ((), (), s32[]{:S(2)}) async-start(), calls=%async_computation.3 | async-start | bytes 17039360 | tf_op jit(solution)/shard_map/all_gather | solution.py:513
  19.1 30.0 %copy-start.9 = (bf16[2,128,1024]{2,1,0:T(8,128)(2,1)}, bf16[2,128,1024]{2,1,0:T(8,128)(2,1)S(1)}, u32[]{:S(2)}) copy-start(bf16[2,128,1024]{2,1,0:T(8,128)(2,1)S(1)} %pad_maximum_fusion.refs_0_.part) | copy-start | bytes 1572868
  19.1 35.0 %copy-start.18 = (s32[1024]{0:T(1024)S(1)}, s32[1024]{0:T(1024)}, u32[]{:S(2)}) copy-start(s32[1024]{0:T(1024)} %param.21) | copy-start | bytes 12292
  19.1 39.1 %copy-start.5 = (f32[4096]{0:T(1024)S(1)}, f32[4096]{0:T(1024)}, u32[]{:S(2)}) copy-start(f32[4096]{0:T(1024)} %param.17) | copy-start | bytes 49156
  19.1 39.1 %copy-start.6 = (f32[4096]{0:T(1024)S(1)}, f32[4096]{0:T(1024)}, u32[]{:S(2)}) copy-start(f32[4096]{0:T(1024)} %param.18) | copy-start | bytes 49156
  19.1 17.0 %collective-permute-start = (bf16[2,128,1024]{2,1,0:T(8,128)(2,1)S(1)}, bf16[2,128,1024]{2,1,0:T(8,128)(2,1)S(1)}, u32[]{:S(2)}, u32[]{:S(2)}) collective-permute-start(bf16[2,128,1024]{2,1,0:T(8,128)(2,1)S(1)} %pad_maximum_fusion.refs_0_.part), channel_id=1, source_target_pairs={{0,3},{1,0},{2,1},{3,2},{4,7},{5,4},{6,5},{7,6},{8,11},{9,8},{10,9... | collective-permute-start | bytes 1572872 | tf_op jit(solution)/shard_map/ppermute | solution.py:56
  22.5 14.0 %collective-permute-start.1 = (bf16[2,128,1024]{2,1,0:T(8,128)(2,1)S(1)}, bf16[2,128,1024]{2,1,0:T(8,128)(2,1)S(1)}, u32[]{:S(2)}, u32[]{:S(2)}) collective-permute-start(bf16[2,128,1024]{2,1,0:T(8,128)(2,1)S(1)} %pad_maximum_fusion.refs_0_.part), channel_id=1, source_target_pairs={{0,2},{1,3},{2,0},{3,1},{4,6},{5,7},{6,4},{7,5},{8,10},{9,11},{10,... | collective-permute-start | bytes 1572872 | tf_op jit(solution)/shard_map/ppermute | solution.py:56
  23.0 26.1 %collective-permute-start.2 = (bf16[2,128,1024]{2,1,0:T(8,128)(2,1)S(1)}, bf16[2,128,1024]{2,1,0:T(8,128)(2,1)S(1)}, u32[]{:S(2)}, u32[]{:S(2)}) collective-permute-start(bf16[2,128,1024]{2,1,0:T(8,128)(2,1)S(1)} %pad_maximum_fusion.refs_0_.part), channel_id=1, source_target_pairs={{0,1},{1,2},{2,3},{3,0},{4,5},{5,6},{6,7},{7,4},{8,9},{9,10},{10,1... | collective-permute-start | bytes 1572872 | tf_op jit(solution)/shard_map/ppermute | solution.py:56
  36.1 12.9 %copy-start.14 = (bf16[2,128,1024]{2,1,0:T(8,128)(2,1)}, bf16[2,128,1024]{2,1,0:T(8,128)(2,1)S(1)}, u32[]{:S(2)}) copy-start(bf16[2,128,1024]{2,1,0:T(8,128)(2,1)S(1)} %collective-permute-done.refs_1_) | copy-start | bytes 1572868
  36.5 12.6 %copy-start.15 = (bf16[2,128,1024]{2,1,0:T(8,128)(2,1)}, bf16[2,128,1024]{2,1,0:T(8,128)(2,1)S(1)}, u32[]{:S(2)}) copy-start(bf16[2,128,1024]{2,1,0:T(8,128)(2,1)S(1)} %collective-permute-done.1.refs_2_) | copy-start | bytes 1572868
  49.1 0.8 copy-start.16
  52.9 5.3 %collective-permute-start.3 = (bf16[4,2,128,1024]{3,2,1,0:T(8,128)(2,1)}, bf16[4,2,128,1024]{3,2,1,0:T(8,128)(2,1)S(1)}, u32[]{:S(2)}, u32[]{:S(2)}) collective-permute-start(bf16[4,2,128,1024]{3,2,1,0:T(8,128)(2,1)} %stack.54.mine), channel_id=1, source_target_pairs={{0,4},{4,0},{8,12},{12,8},{16,20},{20,16},{24,28},{28,24},{32,36},... | collective-permute-start | bytes 6291464 | tf_op jit(solution)/shard_map/ppermute | solution.py:52
  54.3 2.9 %collective-permute-start.4 = (s32[3,128]{1,0:T(4,128)S(1)}, s32[3,128]{1,0:T(4,128)S(1)}, u32[]{:S(2)}, u32[]{:S(2)}) collective-permute-start(s32[3,128]{1,0:T(4,128)S(1)} %get-tuple-element.61), channel_id=1, source_target_pairs={{0,4},{4,0},{8,12},{12,8},{16,20},{20,16},{24,28},{28,24},{32,36},... | collective-permute-start | bytes 4616 | tf_op jit(solution)/shard_map/ppermute | solution.py:52
  54.5 7.6 %copy-start.7 = (s32[3]{0:T(128)}, s32[3]{0:T(128)S(1)}, u32[]{:S(2)}) copy-start(s32[3]{0:T(128)S(1)} %pad_add_fusion.3.place) | copy-start | bytes 40
  58.2 1.6 copy-start
  62.2 1.3 copy-start.1
  63.5 1.3 copy-start.2
  64.8 0.6 copy-start.4
  130.1 26.0 %collective-permute-start.5 = (bf16[8,256,128]{2,1,0:T(8,128)(2,1)}, bf16[8,256,128]{2,1,0:T(8,128)(2,1)S(1)}, u32[]{:S(2)}, u32[]{:S(2)}) collective-permute-start(bf16[8,256,128]{2,1,0:T(8,128)(2,1)} %get-tuple-element.30), channel_id=1, source_target_pairs={{0,8},{4,12},{8,16},{12,20},{16,24},{20,28},{24,0},{28,4},{32,40},... | collective-permute-start | bytes 1572872 | tf_op jit(solution)/shard_map/ppermute | solution.py:48
  130.1 25.9 %collective-permute-start.6 = (bf16[8,256,128]{2,1,0:T(8,128)(2,1)}, bf16[8,256,128]{2,1,0:T(8,128)(2,1)S(1)}, u32[]{:S(2)}, u32[]{:S(2)}) collective-permute-start(bf16[8,256,128]{2,1,0:T(8,128)(2,1)} %get-tuple-element.31), channel_id=1, source_target_pairs={{0,24},{4,28},{8,0},{12,4},{16,8},{20,12},{24,16},{28,20},{32,56},... | collective-permute-start | bytes 1572872 | tf_op jit(solution)/shard_map/ppermute | solution.py:48
  132.8 23.3 %collective-permute-start.7 = (bf16[8,256,128]{2,1,0:T(8,128)(2,1)}, bf16[8,256,128]{2,1,0:T(8,128)(2,1)S(1)}, u32[]{:S(2)}, u32[]{:S(2)}) collective-permute-start(bf16[8,256,128]{2,1,0:T(8,128)(2,1)} %get-tuple-element.32), channel_id=1, source_target_pairs={{0,16},{4,20},{8,24},{12,28},{16,0},{20,4},{24,8},{28,12},{32,48},... | collective-permute-start | bytes 1572872 | tf_op jit(solution)/shard_map/ppermute | solution.py:48
  132.8 24.3 %copy-start.3 = (bf16[8,256,128]{2,1,0:T(8,128)(2,1)S(1)}, bf16[8,256,128]{2,1,0:T(8,128)(2,1)}, u32[]{:S(2)}) copy-start(bf16[8,256,128]{2,1,0:T(8,128)(2,1)} %get-tuple-element.29.refs_0_) | copy-start | bytes 1572868
  156.1 6.1 %collective-permute-start.8 = (bf16[4,2,128,1152]{3,2,1,0:T(8,128)(2,1)}, bf16[4,2,128,1152]{3,2,1,0:T(8,128)(2,1)}, u32[]{:S(2)}, u32[]{:S(2)}) collective-permute-start(bf16[4,2,128,1152]{3,2,1,0:T(8,128)(2,1)} %get-tuple-element.39), channel_id=1, source_target_pairs={{0,4},{4,0},{8,12},{12,8},{16,20},{20,16},{24,28},{28,24},{32,36},... | collective-permute-start | bytes 7077896 | tf_op jit(solution)/shard_map/ppermute | solution.py:52
  158.2 22.0 %all-to-all-start = ((bf16[8,256,128]{2,1,0:T(8,128)(2,1)}), bf16[8,256,128]{2,1,0:T(8,128)(2,1)S(1)}, u32[]{:S(2)}, u32[]{:S(2)}) async-start(bf16[8,256,128]{2,1,0:T(8,128)(2,1)} %add.54), calls=%async_computation | async-start | bytes 1048576 | tf_op jit(solution)/shard_map/all_to_all | solution.py:556
  165.6 31.7 %collective-permute-start.9 = (bf16[2,128,1152]{2,1,0:T(8,128)(2,1)}, bf16[2,128,1152]{2,1,0:T(8,128)(2,1)S(1)}, u32[]{:S(2)}, u32[]{:S(2)}) collective-permute-start(bf16[2,128,1152]{2,1,0:T(8,128)(2,1)} %get-tuple-element.55), channel_id=1, source_target_pairs={{0,1},{1,2},{2,3},{3,0},{4,5},{5,6},{6,7},{7,4},{8,9},{9,10},{10,1... | collective-permute-start | bytes 1769480 | tf_op jit(solution)/shard_map/ppermute | solution.py:56
  166.8 30.5 %collective-permute-start.10 = (bf16[2,128,1152]{2,1,0:T(8,128)(2,1)}, bf16[2,128,1152]{2,1,0:T(8,128)(2,1)S(1)}, u32[]{:S(2)}, u32[]{:S(2)}) collective-permute-start(bf16[2,128,1152]{2,1,0:T(8,128)(2,1)} %get-tuple-element.54), channel_id=1, source_target_pairs={{0,3},{1,0},{2,1},{3,2},{4,7},{5,4},{6,5},{7,6},{8,11},{9,8},{10,9... | collective-permute-start | bytes 1769480 | tf_op jit(solution)/shard_map/ppermute | solution.py:56
  168.3 29.0 %collective-permute-start.11 = (bf16[2,128,1152]{2,1,0:T(8,128)(2,1)S(1)}, bf16[2,128,1152]{2,1,0:T(8,128)(2,1)S(1)}, u32[]{:S(2)}, u32[]{:S(2)}) collective-permute-start(bf16[2,128,1152]{2,1,0:T(8,128)(2,1)S(1)} %get-tuple-element.53), channel_id=1, source_target_pairs={{0,2},{1,3},{2,0},{3,1},{4,6},{5,7},{6,4},{7,5},{8,10},{9,11},{10,... | collective-permute-start | bytes 1769480 | tf_op jit(solution)/shard_map/ppermute | solution.py:56
  181.3 13.7 %all-to-all-start.1 = ((f32[32,8,128]{2,1,0:T(8,128)}), f32[32,8,128]{2,1,0:T(8,128)S(1)}, u32[]{:S(2)}, u32[]{:S(2)}) async-start(f32[32,8,128]{2,1,0:T(8,128)} %bitcast.22), calls=%async_computation.1 | async-start | bytes 262144 | tf_op jit(solution)/shard_map/all_to_all | solution.py:559
  195.0 0.7 copy-start.13
  197.3 7.6 %copy-start.10 = (bf16[2,128,1152]{2,1,0:T(8,128)(2,1)}, bf16[2,128,1152]{2,1,0:T(8,128)(2,1)S(1)}, u32[]{:S(2)}) copy-start(bf16[2,128,1152]{2,1,0:T(8,128)(2,1)S(1)} %collective-permute-done.9.sent_1) | copy-start | bytes 1769476
  197.3 7.6 %copy-start.11 = (bf16[2,128,1152]{2,1,0:T(8,128)(2,1)}, bf16[2,128,1152]{2,1,0:T(8,128)(2,1)S(1)}, u32[]{:S(2)}) copy-start(bf16[2,128,1152]{2,1,0:T(8,128)(2,1)S(1)} %collective-permute-done.10.sent_2) | copy-start | bytes 1769476
  197.3 7.5 %copy-start.12 = (bf16[2,128,1152]{2,1,0:T(8,128)(2,1)}, bf16[2,128,1152]{2,1,0:T(8,128)(2,1)S(1)}, u32[]{:S(2)}) copy-start(bf16[2,128,1152]{2,1,0:T(8,128)(2,1)S(1)} %collective-permute-done.11.sent_3) | copy-start | bytes 1769476
  197.3 16.4 %all-to-all-start.2 = ((f32[32,8,128]{2,1,0:T(8,128)}), f32[32,8,128]{2,1,0:T(8,128)S(1)}, u32[]{:S(2)}, u32[]{:S(2)}) async-start(f32[32,8,128]{2,1,0:T(8,128)} %total.1), calls=%async_computation.2 | async-start | bytes 262144 | tf_op jit(solution)/shard_map/all_to_all | solution.py:562
  216.1 3.9 %collective-permute-start.12 = (f32[64,256]{1,0:T(8,128)S(1)}, f32[64,256]{1,0:T(8,128)S(1)}, u32[]{:S(2)}, u32[]{:S(2)}) collective-permute-start(f32[64,256]{1,0:T(8,128)S(1)} %get-tuple-element.57), channel_id=1, source_target_pairs={{0,4},{4,0},{8,12},{12,8},{16,20},{20,16},{24,28},{28,24},{32,36},... | collective-permute-start | bytes 196616 | tf_op jit(solution)/shard_map/ppermute | solution.py:52
Sparse Core Ops, SparseCore 0:
  16.5 104.1 all-gather.1
